TPU v7x, 32 devices: a whole 2x2x4 slice. The times are simulated.
32 devices in a mesh: section: 2 (over x), tp: 4 (over y, core), ctx: 4 (over z).
Axes of the slice: x: 2, y: 2, z: 4, core: 2. Of those that a mesh axis runs over, the one named last changes fastest.
Arguments:
- tokens_in: bfloat16 [2, 8, 16384], P(None, None, 'ctx'), may hold values from -6 to 6
- norm_gain: bfloat16 [2, 16384], P('section', 'ctx'), may hold values from 0.25 to 1.75
- w_qkv: bfloat16 [2, 16384, 18432], P('section', 'ctx', 'tp'), may hold values from -0.375 to 0.375
- w_out: bfloat16 [2, 16384, 16384], P('section', 'tp', 'ctx'), may hold values from -0.046875 to 0.046875
- prefix_keys: bfloat16 [2, 8, 16384, 128], P('section', 'tp', 'ctx'), may hold values from -400 to 400
- prefix_values: bfloat16 [2, 8, 16384, 128], P('section', 'tp', 'ctx'), may hold values from -6 to 6
- suffix_keys: bfloat16 [2, 8, 8, 512, 128], P('section', 'tp', 'ctx'), may hold values from -27 to 27
- suffix_values: bfloat16 [2, 8, 8, 512, 128], P('section', 'tp', 'ctx'), may hold values from -6 to 6
- lengths: int32 [8], replicated, may hold values from 1 to 512, 2048 in all
- order: int32 [8], replicated, may hold values from 0 to 7, each once
Outputs:
- layer_out: float32 [2, 2, 8, 16384], P('section', None, 'tp', 'ctx')
Inputs may be any that keep to these rules, and one draw needn't show every extreme that they name: `lengths`: some sample has 512. `order`: each sample appears in exactly one row.
All inputs are finite; a program needn't handle non-finite values.
Results may differ from a plain program's by a relative error of at most 0.014.
Values may be sent and summed in bfloat16 or wider, within the bound.
No kernel may reach another device: no remote copies, remote signals or barrier semaphores. Data moves between devices by JAX's collectives and lax.ppermute only.
A program may use at most 128 MiB of HBM per device.

v0:
```python
import jax
import jax.numpy as jnp
from jax import lax
from jax.sharding import PartitionSpec as P

D = 16384
HD = 128
G = 16


EPSILON = 1e-05
NEGATIVE = -1e30


def from_behind(value, axis, steps):
    count = lax.axis_size(axis)
    initial, last = (max(0, -steps), min(count, count - steps))
    return lax.ppermute(value, axis, [(source, source + steps) for source in range(initial, last)])


def combine(earlier, later):
    first_max, first_sum, first_out = earlier
    second_max, second_sum, second_out = later
    joint_max = jnp.maximum(first_max, second_max)
    first_scale = jnp.exp(first_max - joint_max)
    second_scale = jnp.exp(second_max - joint_max)
    return (
        joint_max,
        first_sum * first_scale + second_sum * second_scale,
        first_out * first_scale[..., None] + second_out * second_scale[..., None],
    )


def rounded(values):
    return lax.optimization_barrier(values.astype(jnp.bfloat16)).astype(jnp.float32)


def finish(joined, queries, keys_new, values_new, keys_old, values_old, old_on):
    row_max, row_sum, row_out = joined
    score_scale = HD ** (-0.5)
    own_scores = (
        jnp.einsum("rjgd,rjd->rjg", queries, keys_new, preferred_element_type=jnp.float32)
        * score_scale
    )
    terms = [(own_scores, values_new)]
    if keys_old is not None:
        old_scores = (
            jnp.einsum("rjgd,rjd->rjg", queries, keys_old, preferred_element_type=jnp.float32)
            * score_scale
        )
        terms.append((jnp.where(old_on, old_scores, NEGATIVE), values_old))
    joint_max = row_max
    for scores, values in terms:
        joint_max = jnp.maximum(joint_max, scores)
    factor = jnp.exp(row_max - joint_max)
    row_sum = row_sum * factor
    row_out = row_out * factor[..., None]
    for scores, values in terms:
        weights = jnp.exp(scores - joint_max)
        row_sum = row_sum + weights
        row_out = row_out + rounded(weights)[..., None] * values.astype(jnp.float32)[:, :, None, :]
    return (row_out / row_sum[..., None]).astype(jnp.bfloat16)


def layer_pass(
    hidden,
    gain,
    qkv_weight,
    out_weight,
    pre_keys,
    pre_values,
    suf_keys,
    suf_values,
    local_lengths,
    row_order,
    first_sample,
    keys_old,
    values_old,
    old_on,
):
    row_count = hidden.shape[0]
    squares = jnp.sum(hidden * hidden, axis=1)
    scaled = (hidden * gain.astype(jnp.float32)[None, :]).astype(jnp.bfloat16)
    partial_proj = jnp.dot(scaled, qkv_weight, preferred_element_type=jnp.float32)
    squares, partial_proj = lax.psum((squares, partial_proj), "ctx")
    projected = (partial_proj * lax.rsqrt(squares / D + EPSILON)[:, None]).astype(jnp.bfloat16)
    heads_local = projected.shape[1] // ((G + 2) * HD)
    projected = projected.reshape(row_count, heads_local, G + 2, HD)
    queries = projected[:, :, :G]
    keys_new = projected[:, :, G]
    values_new = projected[:, :, G + 1]
    score_scale = HD ** (-0.5)
    prefix_scores = (
        jnp.einsum("rjgd,jpd->rjgp", queries, pre_keys, preferred_element_type=jnp.float32)
        * score_scale
    )
    prefix_max = jnp.max(prefix_scores, axis=3)
    prefix_weights = jnp.exp(prefix_scores - prefix_max[..., None])
    prefix_sum = jnp.sum(prefix_weights, axis=3)
    prefix_out = jnp.einsum(
        "rjgp,jpd->rjgd",
        prefix_weights.astype(jnp.bfloat16),
        pre_values,
        preferred_element_type=jnp.float32,
    )
    sample_slots = suf_keys.shape[1]
    sample_ids = first_sample + jnp.arange(sample_slots, dtype=jnp.int32)
    owners = (row_order[None, :] == sample_ids[:, None]).astype(jnp.float32)
    owned = jnp.sum(owners, axis=0) > 0.5
    local_queries = jnp.einsum(
        "ir,rjgd->ijgd", owners, queries.astype(jnp.float32), precision=lax.Precision.HIGHEST
    ).astype(jnp.bfloat16)
    suffix_scores = (
        jnp.einsum("ijgd,jipd->ijgp", local_queries, suf_keys, preferred_element_type=jnp.float32)
        * score_scale
    )
    in_suffix = (jnp.arange(suf_keys.shape[2], dtype=jnp.int32)[None, :] < local_lengths[:, None])[
        :, None, None, :
    ]
    suffix_max = jnp.max(jnp.where(in_suffix, suffix_scores, NEGATIVE), axis=3)
    suffix_weights = jnp.where(in_suffix, jnp.exp(suffix_scores - suffix_max[..., None]), 0.0)
    suffix_sum = jnp.sum(suffix_weights, axis=3)
    suffix_out = jnp.einsum(
        "ijgp,jipd->ijgd",
        suffix_weights.astype(jnp.bfloat16),
        suf_values,
        preferred_element_type=jnp.float32,
    )
    mapped_max = jnp.where(
        owned[:, None, None],
        jnp.einsum("ir,ijg->rjg", owners, suffix_max, precision=lax.Precision.HIGHEST),
        NEGATIVE,
    )
    mapped_sum = jnp.einsum("ir,ijg->rjg", owners, suffix_sum, precision=lax.Precision.HIGHEST)
    mapped_out = jnp.einsum("ir,ijgd->rjgd", owners, suffix_out, precision=lax.Precision.HIGHEST)
    local = combine((prefix_max, prefix_sum, prefix_out), (mapped_max, mapped_sum, mapped_out))
    all_max, all_sum, all_out = (
        lax.all_to_all(local[0][None], "ctx", split_axis=1, concat_axis=0, tiled=True),
        lax.all_to_all(local[1][None], "ctx", split_axis=1, concat_axis=0, tiled=True),
        lax.all_to_all(local[2][None], "ctx", split_axis=1, concat_axis=0, tiled=True),
    )
    joint_max = jnp.max(all_max, axis=0)
    factors = jnp.exp(all_max - joint_max[None])
    joined = (
        joint_max,
        jnp.sum(all_sum * factors, axis=0),
        jnp.sum(all_out * factors[..., None], axis=0),
    )
    share = row_count // lax.axis_size("ctx")
    offset = lax.axis_index("ctx") * share

    def rows_here(values):
        if values is None:
            return None
        return lax.dynamic_slice_in_dim(values, offset, share, 0)

    attention_share = finish(
        joined,
        rows_here(queries),
        rows_here(keys_new),
        rows_here(values_new),
        rows_here(keys_old),
        rows_here(values_old),
        old_on,
    )
    attention = lax.all_gather(attention_share, "ctx", axis=0, tiled=True)
    head_terms = jnp.dot(
        attention.reshape(row_count, -1), out_weight, preferred_element_type=jnp.float32
    )
    tp_share = row_count // lax.axis_size("tp")
    tp_offset = lax.axis_index("tp") * tp_share
    summed = lax.psum(head_terms, "tp")
    passed = hidden + summed
    kept = lax.dynamic_slice_in_dim(passed, tp_offset, tp_share, 0)
    return (passed, kept, keys_new, values_new)


def on_device(
    tokens_in,
    norm_gain,
    w_qkv,
    w_out,
    prefix_keys,
    prefix_values,
    suffix_keys,
    suffix_values,
    lengths,
    order,
):
    on_first = lax.axis_index("section") == 0
    groups = 1
    plan = [(step_index, group) for step_index in range(2) for group in range(groups)]
    batch = tokens_in.shape[1]
    row_count = batch // groups
    sample_slots = suffix_keys.shape[2]
    first_sample = lax.axis_index("ctx") * sample_slots
    local_lengths = lax.dynamic_slice_in_dim(lengths, first_sample, sample_slots, 0)
    stored = []
    kept_first = {}
    kept_second = {}
    received = None
    for slot_index in range(len(plan) + 1):
        leading = plan[slot_index] if slot_index < len(plan) else None
        trailing = plan[slot_index - 1] if slot_index >= 1 else None
        if leading is None:
            fresh = jnp.zeros((row_count, tokens_in.shape[2]), jnp.float32)
        else:
            fresh = tokens_in[leading[0]].astype(jnp.float32)
        hidden = fresh if received is None else jnp.where(on_first, fresh, received)
        row_order = jnp.where(on_first, order, order)
        if slot_index >= groups:
            keys_old, values_old = stored[slot_index - groups]
            old_on = jnp.logical_or(on_first, slot_index - 1 >= groups)
        else:
            keys_old, values_old = (None, None)
            old_on = on_first
        passed, kept, keys_new, values_new = layer_pass(
            hidden,
            norm_gain[0],
            w_qkv[0],
            w_out[0],
            prefix_keys[0],
            prefix_values[0],
            suffix_keys[0],
            suffix_values[0],
            local_lengths,
            row_order,
            first_sample,
            keys_old,
            values_old,
            old_on,
        )
        stored.append((keys_new, values_new))
        if leading is not None:
            kept_first[leading] = kept
        if trailing is not None:
            kept_second[trailing] = kept
        if slot_index < len(plan):
            received = from_behind(passed, "section", 1)

    def assemble(kept_map):
        step_rows = []
        for step_index in range(2):
            shares = kept_map[step_index, 0]
            step_rows.append(shares)
        return jnp.stack(step_rows)

    result = jnp.where(on_first, assemble(kept_first), assemble(kept_second))
    return result[None]


def solution(mesh):
    in_specs = (
        P(None, None, "ctx"),
        P("section", "ctx"),
        P("section", "ctx", "tp"),
        P("section", "tp", "ctx"),
        P("section", "tp", "ctx", None),
        P("section", "tp", "ctx", None),
        P("section", "tp", "ctx", None, None),
        P("section", "tp", "ctx", None, None),
        P(),
        P(),
    )
    out_specs = P("section", None, "tp", "ctx")
    return jax.shard_map(
        on_device, mesh=mesh, in_specs=in_specs, out_specs=out_specs, check_vma=False
    )
```

profile of v0, /device:TPU:0, one launch (start us, length us, event | category | flops | bytes accessed | tf_op | source)
XLA Modules:
  0.0 482.0 jit_solution(9767877265907647229)
XLA Ops:
  7.5 17.3 %fusion.4 = f32[8,4608]{1,0:T(8,128)} fusion(bf16[1,4096,4608]{2,1,0:T(8,128)(2,1)} %param.12, f32[4096]{0:T(1024)S(1)} %bitcast.251, bf16[2,8,4096]{2,1,0:T(8,128)(2,1)} %param.10), kind=kOutput, calls=%fused_computation.4 | convolution fusion | flops 302088192 | bytes 37978112 | tf_op jit(solution)/shard_map/dot_general | solution.py:84
  25.2 13.4 %psum.64 = f32[8]{0:T(128)S(1)} all-reduce(f32[8]{0:T(128)S(1)} %fusion.113), channel_id=1, replica_groups=mesh['section'=2,'tp'=4,'ctx'=4] {'ctx'}, use_global_device_ids=true, to_apply=%region_2.3 | all-reduce | flops 8 | bytes 64 | tf_op jit(solution)/shard_map/psum | solution.py:85
  38.8 23.3 %all-reduce.7.cloned.1.call-done = f32[8,4608]{1,0:T(8,128)} async-done(((f32[8,4608]{1,0:T(8,128)}), f32[8,4608]{1,0:T(8,128)}) %all-reduce.7.cloned.1.call-update) | async-done | bytes 147472 | tf_op jit(solution)/shard_map/psum | solution.py:85
  63.8 1.3 fusion.106
  66.2 1.9 copy-done.3
  69.6 3.7 all-to-all-start.1
  73.5 3.7 fusion.91
  78.9 4.1 all-to-all-start.2
  83.7 4.9 %all-to-all-done.2 = f32[1,8,2,16]{3,2,0,1:T(2,128)S(1)} async-done(((f32[1,8,2,16]{3,2,0,1:T(2,128)}), f32[1,8,2,16]{3,2,0,1:T(2,128)S(1)}, u32[]{:S(2)}, u32[]{:S(2)}) %all-to-all-start.2) | async-done | bytes 1056 | tf_op jit(solution)/shard_map/all_to_all | solution.py:139
  88.6 3.3 all-to-all-start
  92.1 5.7 %all-to-all-done = f32[1,8,2,16,128]{4,3,2,0,1:T(8,128)S(1)} async-done(((f32[1,8,2,16,128]{4,3,2,0,1:T(8,128)}), f32[1,8,2,16,128]{4,3,2,0,1:T(8,128)S(1)}, u32[]{:S(2)}, u32[]{:S(2)}) %all-to-all-start) | async-done | bytes 131104 | tf_op jit(solution)/shard_map/all_to_all | solution.py:140
  98.1 13.1 %all_gather.9 = bf16[8,2,16,128]{3,2,1,0:T(8,128)(2,1)S(1)} all-gather(bf16[2,2,16,128]{3,2,1,0:T(8,128)(2,1)S(1)} %copy.90), channel_id=1, replica_groups=mesh['section'=2,'tp'=4,'ctx'=4] {'ctx'}, dimensions={0}, use_global_device_ids=true | all-gather | bytes 81920 | tf_op jit(solution)/shard_map/all_gather | solution.py:166
  111.2 13.5 %fusion.10 = f32[8,4096]{1,0:T(8,128)} fusion(bf16[1,4096,4096]{2,1,0:T(8,128)(2,1)} %param.13, bf16[1,8,32,128]{3,2,1,0:T(8,128)(2,1)S(1)} %bitcast.254), kind=kOutput, calls=%fused_computation.10 | convolution fusion | flops 268435456 | bytes 33751040 | tf_op jit(solution)/shard_map/dot_general | solution.py:167
  124.8 30.6 %all-reduce.9.cloned.1.call-done = f32[8,4096]{1,0:T(8,128)} async-done(((f32[8,4096]{1,0:T(8,128)}), f32[8,4096]{1,0:T(8,128)}) %all-reduce.9.cloned.1.call-update) | async-done | bytes 131088 | tf_op jit(solution)/shard_map/psum | solution.py:172
  156.2 3.4 collective-permute-start
  159.6 2.5 collective-permute-done
  162.3 11.9 %psum.67 = f32[8]{0:T(128)S(1)} all-reduce(f32[8]{0:T(128)S(1)} %multiply_reduce_fusion.1), channel_id=1, replica_groups=mesh['section'=2,'tp'=4,'ctx'=4] {'ctx'}, use_global_device_ids=true, to_apply=%region_14.15 | all-reduce | flops 8 | bytes 64 | tf_op jit(solution)/shard_map/psum | solution.py:85
  174.1 14.9 %fusion.2 = f32[8,4608]{1,0:T(8,128)} fusion(bf16[1,4096,4608]{2,1,0:T(8,128)(2,1)} %param.12, f32[4096]{0:T(1024)S(1)} %bitcast.252, f32[8,4096]{1,0:T(8,128)S(1)} %collective-permute-done, bf16[2,8,4096]{2,1,0:T(8,128)(2,1)S(1)} %copy-done.5, pred[]{:T(512)S(6)} %eq.8), kind=kOutput, calls=%fused_computation.2 | convolution fusion | flops 302120960 | bytes 38109184 | tf_op jit(solution)/shard_map/dot_general | solution.py:84
  189.1 32.7 %all-reduce.11.cloned.1.call-done = f32[8,4608]{1,0:T(8,128)} async-done(((f32[8,4608]{1,0:T(8,128)}), f32[8,4608]{1,0:T(8,128)}) %all-reduce.11.cloned.1.call-update) | async-done | bytes 147472 | tf_op jit(solution)/shard_map/psum | solution.py:85
  223.5 1.3 fusion.104
  226.3 1.2 copy-done.2
  228.8 3.7 all-to-all-start.4
  232.5 3.7 fusion.76
  237.0 1.1 all-to-all-done.4
  238.1 4.0 all-to-all-start.5
  242.8 4.9 %all-to-all-done.5 = f32[1,8,2,16]{3,2,0,1:T(2,128)S(1)} async-done(((f32[1,8,2,16]{3,2,0,1:T(2,128)}), f32[1,8,2,16]{3,2,0,1:T(2,128)S(1)}, u32[]{:S(2)}, u32[]{:S(2)}) %all-to-all-start.5) | async-done | bytes 1056 | tf_op jit(solution)/shard_map/all_to_all | solution.py:139
  247.7 3.3 all-to-all-start.3
  251.2 5.7 %all-to-all-done.3 = f32[1,8,2,16,128]{4,3,2,0,1:T(8,128)S(1)} async-done(((f32[1,8,2,16,128]{4,3,2,0,1:T(8,128)}), f32[1,8,2,16,128]{4,3,2,0,1:T(8,128)S(1)}, u32[]{:S(2)}, u32[]{:S(2)}) %all-to-all-start.3) | async-done | bytes 131104 | tf_op jit(solution)/shard_map/all_to_all | solution.py:140
  257.2 13.1 %all_gather.10 = bf16[8,2,16,128]{3,2,1,0:T(8,128)(2,1)S(1)} all-gather(bf16[2,2,16,128]{3,2,1,0:T(8,128)(2,1)S(1)} %copy.109), channel_id=1, replica_groups=mesh['section'=2,'tp'=4,'ctx'=4] {'ctx'}, dimensions={0}, use_global_device_ids=true | all-gather | bytes 81920 | tf_op jit(solution)/shard_map/all_gather | solution.py:166
  270.3 13.5 %fusion.8 = f32[8,4096]{1,0:T(8,128)} fusion(bf16[1,4096,4096]{2,1,0:T(8,128)(2,1)} %param.13, bf16[1,8,32,128]{3,2,1,0:T(8,128)(2,1)S(1)} %bitcast.255), kind=kOutput, calls=%fused_computation.8 | convolution fusion | flops 268435456 | bytes 33751040 | tf_op jit(solution)/shard_map/dot_general | solution.py:167
  283.8 30.6 %all-reduce.13.cloned.1.call-done = f32[8,4096]{1,0:T(8,128)} async-done(((f32[8,4096]{1,0:T(8,128)}), f32[8,4096]{1,0:T(8,128)}) %all-reduce.13.cloned.1.call-update) | async-done | bytes 131088 | tf_op jit(solution)/shard_map/psum | solution.py:172
  315.3 3.4 collective-permute-start.1
  318.7 2.5 collective-permute-done.1
  321.4 11.7 %psum.70 = f32[8]{0:T(128)S(1)} all-reduce(f32[8]{0:T(128)S(1)} %get-tuple-element.7), channel_id=1, replica_groups=mesh['section'=2,'tp'=4,'ctx'=4] {'ctx'}, use_global_device_ids=true, to_apply=%region_25.26 | all-reduce | flops 8 | bytes 64 | tf_op jit(solution)/shard_map/psum | solution.py:85
  333.0 14.9 %fusion = f32[8,4608]{1,0:T(8,128)} fusion(bf16[1,4096,4608]{2,1,0:T(8,128)(2,1)} %param.12, f32[8,4096]{1,0:T(8,128)S(1)} %get-tuple-element.8, f32[4096]{0:T(1024)S(1)} %bitcast.253), kind=kOutput, calls=%fused_computation | convolution fusion | flops 302055424 | bytes 38043648 | tf_op jit(solution)/shard_map/dot_general | solution.py:84
  348.0 32.7 %all-reduce.15.cloned.1.call-done = f32[8,4608]{1,0:T(8,128)} async-done(((f32[8,4608]{1,0:T(8,128)}), f32[8,4608]{1,0:T(8,128)}) %all-reduce.15.cloned.1.call-update) | async-done | bytes 147472 | tf_op jit(solution)/shard_map/psum | solution.py:85
  382.4 1.3 fusion.102
  385.2 1.2 copy-done.1
  387.7 3.7 all-to-all-start.7
  391.4 3.7 fusion.61
  395.9 1.1 all-to-all-done.7
  397.0 4.2 all-to-all-start.8
  401.9 4.9 %all-to-all-done.8 = f32[1,8,2,16]{3,2,0,1:T(2,128)S(1)} async-done(((f32[1,8,2,16]{3,2,0,1:T(2,128)}), f32[1,8,2,16]{3,2,0,1:T(2,128)S(1)}, u32[]{:S(2)}, u32[]{:S(2)}) %all-to-all-start.8) | async-done | bytes 1056 | tf_op jit(solution)/shard_map/all_to_all | solution.py:139
  406.8 3.3 all-to-all-start.6
  410.3 5.7 %all-to-all-done.6 = f32[1,8,2,16,128]{4,3,2,0,1:T(8,128)S(1)} async-done(((f32[1,8,2,16,128]{4,3,2,0,1:T(8,128)}), f32[1,8,2,16,128]{4,3,2,0,1:T(8,128)S(1)}, u32[]{:S(2)}, u32[]{:S(2)}) %all-to-all-start.6) | async-done | bytes 131104 | tf_op jit(solution)/shard_map/all_to_all | solution.py:140
  416.3 13.1 %all_gather.11 = bf16[8,2,16,128]{3,2,1,0:T(8,128)(2,1)S(1)} all-gather(bf16[2,2,16,128]{3,2,1,0:T(8,128)(2,1)S(1)} %copy.128), channel_id=1, replica_groups=mesh['section'=2,'tp'=4,'ctx'=4] {'ctx'}, dimensions={0}, use_global_device_ids=true | all-gather | bytes 81920 | tf_op jit(solution)/shard_map/all_gather | solution.py:166
  429.4 13.5 %fusion.6 = f32[8,4096]{1,0:T(8,128)} fusion(bf16[1,4096,4096]{2,1,0:T(8,128)(2,1)} %param.13, bf16[1,8,32,128]{3,2,1,0:T(8,128)(2,1)S(1)} %bitcast.256), kind=kOutput, calls=%fused_computation.6 | convolution fusion | flops 268435456 | bytes 33751040 | tf_op jit(solution)/shard_map/dot_general | solution.py:167
  442.9 30.6 %all-reduce.17.cloned.1.call-done = f32[8,4096]{1,0:T(8,128)} async-done(((f32[8,4096]{1,0:T(8,128)}), f32[8,4096]{1,0:T(8,128)}) %all-reduce.17.cloned.1.call-update) | async-done | bytes 131088 | tf_op jit(solution)/shard_map/psum | solution.py:172
  (136 shorter events, 24.9 us)
Async XLA Ops:
  6.5 58.9 %copy-start = (bf16[1,2,4096,128]{3,2,1,0:T(8,128)(2,1)S(1)}, bf16[1,2,4096,128]{3,2,1,0:T(8,128)(2,1)}, u32[]{:S(2)}) copy-start(bf16[1,2,4096,128]{3,2,1,0:T(8,128)(2,1)} %param.14) | copy-start | bytes 6291460
  6.5 55.6 %all-reduce.7.cloned.1.call-start = ((), (), s32[]{:S(2)}) async-start(), calls=%async_computation.9 | async-start | bytes 294912 | tf_op jit(solution)/shard_map/psum | solution.py:85
  7.4 17.4 %copy-start.5 = (bf16[2,8,4096]{2,1,0:T(8,128)(2,1)S(1)}, bf16[2,8,4096]{2,1,0:T(8,128)(2,1)}, u32[]{:S(2)}) copy-start(bf16[2,8,4096]{2,1,0:T(8,128)(2,1)} %param.10) | copy-start | bytes 393220
  7.4 17.6 %copy-start.6 = (s32[8]{0:T(128)S(1)}, s32[8]{0:T(128)}, u32[]{:S(2)}) copy-start(s32[8]{0:T(128)} %param.19) | copy-start | bytes 100
  7.5 31.2 %copy-start.7 = (s32[8]{0:T(128)S(1)}, s32[8]{0:T(128)}, u32[]{:S(2)}) copy-start(s32[8]{0:T(128)} %param.18) | copy-start | bytes 100
  7.5 55.8 %copy-start.4 = (bf16[1,2,2,512,128]{4,3,2,1,0:T(8,128)(2,1)S(1)}, bf16[1,2,2,512,128]{4,3,2,1,0:T(8,128)(2,1)}, u32[]{:S(2)}) copy-start(bf16[1,2,2,512,128]{4,3,2,1,0:T(8,128)(2,1)} %param.16) | copy-start | bytes 1572868
  66.2 1.9 copy-start.3
  69.6 9.3 %all-to-all-start.1 = ((f32[1,8,2,16]{3,2,0,1:T(2,128)}), f32[1,8,2,16]{3,2,0,1:T(2,128)S(1)}, u32[]{:S(2)}, u32[]{:S(2)}) async-start(f32[1,8,2,16]{3,2,0,1:T(2,128)} %copy.82), calls=%async_computation.1 | async-start | bytes 16384 | tf_op jit(solution)/shard_map/all_to_all | solution.py:138
  78.9 9.7 %all-to-all-start.2 = ((f32[1,8,2,16]{3,2,0,1:T(2,128)}), f32[1,8,2,16]{3,2,0,1:T(2,128)S(1)}, u32[]{:S(2)}, u32[]{:S(2)}) async-start(f32[1,8,2,16]{3,2,0,1:T(2,128)} %copy.88), calls=%async_computation.2 | async-start | bytes 16384 | tf_op jit(solution)/shard_map/all_to_all | solution.py:139
  88.6 9.2 %all-to-all-start = ((f32[1,8,2,16,128]{4,3,2,0,1:T(8,128)}), f32[1,8,2,16,128]{4,3,2,0,1:T(8,128)S(1)}, u32[]{:S(2)}, u32[]{:S(2)}) async-start(f32[1,8,2,16,128]{4,3,2,0,1:T(8,128)} %copy.81), calls=%async_computation | async-start | bytes 262144 | tf_op jit(solution)/shard_map/all_to_all | solution.py:140
  92.0 63.3 %all-reduce.9.cloned.1.call-start = ((), (), s32[]{:S(2)}) async-start(), calls=%async_computation.10 | async-start | bytes 262144 | tf_op jit(solution)/shard_map/psum | solution.py:172
  124.7 97.1 %all-reduce.11.cloned.1.call-start = ((), (), s32[]{:S(2)}) async-start(), calls=%async_computation.11 | async-start | bytes 294912 | tf_op jit(solution)/shard_map/psum | solution.py:85
  156.2 5.9 %collective-permute-start = (f32[8,4096]{1,0:T(8,128)S(1)}, f32[8,4096]{1,0:T(8,128)S(1)}, u32[]{:S(2)}, u32[]{:S(2)}) collective-permute-start(f32[8,4096]{1,0:T(8,128)S(1)} %fusion.111), channel_id=1, source_target_pairs={{0,16},{1,17},{2,18},{3,19},{4,20},{5,21},{6,22},{7,23},{8,24},{9,... | collective-permute-start | bytes 393224 | tf_op jit(solution)/shard_map/ppermute | solution.py:18
  225.6 1.9 copy-start.2
  228.8 9.3 %all-to-all-start.4 = ((f32[1,8,2,16]{3,2,0,1:T(2,128)}), f32[1,8,2,16]{3,2,0,1:T(2,128)S(1)}, u32[]{:S(2)}, u32[]{:S(2)}) async-start(f32[1,8,2,16]{3,2,0,1:T(2,128)} %copy.100), calls=%async_computation.4 | async-start | bytes 16384 | tf_op jit(solution)/shard_map/all_to_all | solution.py:138
  238.1 9.6 %all-to-all-start.5 = ((f32[1,8,2,16]{3,2,0,1:T(2,128)}), f32[1,8,2,16]{3,2,0,1:T(2,128)S(1)}, u32[]{:S(2)}, u32[]{:S(2)}) async-start(f32[1,8,2,16]{3,2,0,1:T(2,128)} %copy.107), calls=%async_computation.5 | async-start | bytes 16384 | tf_op jit(solution)/shard_map/all_to_all | solution.py:139
  247.7 9.2 %all-to-all-start.3 = ((f32[1,8,2,16,128]{4,3,2,0,1:T(8,128)}), f32[1,8,2,16,128]{4,3,2,0,1:T(8,128)S(1)}, u32[]{:S(2)}, u32[]{:S(2)}) async-start(f32[1,8,2,16,128]{4,3,2,0,1:T(8,128)} %copy.99), calls=%async_computation.3 | async-start | bytes 262144 | tf_op jit(solution)/shard_map/all_to_all | solution.py:140
  251.0 63.4 %all-reduce.13.cloned.1.call-start = ((), (), s32[]{:S(2)}) async-start(), calls=%async_computation.12 | async-start | bytes 262144 | tf_op jit(solution)/shard_map/psum | solution.py:172
  283.8 96.9 %all-reduce.15.cloned.1.call-start = ((), (), s32[]{:S(2)}) async-start(), calls=%async_computation.13 | async-start | bytes 294912 | tf_op jit(solution)/shard_map/psum | solution.py:85
  315.3 5.9 %collective-permute-start.1 = (f32[8,4096]{1,0:T(8,128)S(1)}, f32[8,4096]{1,0:T(8,128)S(1)}, u32[]{:S(2)}, u32[]{:S(2)}) collective-permute-start(f32[8,4096]{1,0:T(8,128)S(1)} %fusion.148), channel_id=1, source_target_pairs={{0,16},{1,17},{2,18},{3,19},{4,20},{5,21},{6,22},{7,23},{8,24},{9,... | collective-permute-start | bytes 393224 | tf_op jit(solution)/shard_map/ppermute | solution.py:18
  384.5 1.9 copy-start.1
  387.7 9.3 %all-to-all-start.7 = ((f32[1,8,2,16]{3,2,0,1:T(2,128)}), f32[1,8,2,16]{3,2,0,1:T(2,128)S(1)}, u32[]{:S(2)}, u32[]{:S(2)}) async-start(f32[1,8,2,16]{3,2,0,1:T(2,128)} %copy.119), calls=%async_computation.7 | async-start | bytes 16384 | tf_op jit(solution)/shard_map/all_to_all | solution.py:138
  397.0 9.8 %all-to-all-start.8 = ((f32[1,8,2,16]{3,2,0,1:T(2,128)}), f32[1,8,2,16]{3,2,0,1:T(2,128)S(1)}, u32[]{:S(2)}, u32[]{:S(2)}) async-start(f32[1,8,2,16]{3,2,0,1:T(2,128)} %copy.126), calls=%async_computation.8 | async-start | bytes 16384 | tf_op jit(solution)/shard_map/all_to_all | solution.py:139
  406.8 9.2 %all-to-all-start.6 = ((f32[1,8,2,16,128]{4,3,2,0,1:T(8,128)}), f32[1,8,2,16,128]{4,3,2,0,1:T(8,128)S(1)}, u32[]{:S(2)}, u32[]{:S(2)}) async-start(f32[1,8,2,16,128]{4,3,2,0,1:T(8,128)} %copy.118), calls=%async_computation.6 | async-start | bytes 262144 | tf_op jit(solution)/shard_map/all_to_all | solution.py:140
  410.2 63.4 %all-reduce.17.cloned.1.call-start = ((), (), s32[]{:S(2)}) async-start(), calls=%async_computation.14 | async-start | bytes 262144 | tf_op jit(solution)/shard_map/psum | solution.py:172
Sparse Core Ops, SparseCore 0:
  25.0 37.0 all-reduce.6
  124.8 30.4 all-reduce.8
  189.2 32.5 all-reduce.10
  283.9 30.4 all-reduce.12
  348.1 32.5 all-reduce.14
  443.0 30.4 all-reduce.16
where the time goes:
time: 483 us; the launch traced here: 482 us
  waiting for transfers between devices  221 us (46%)
  matrix products  109 us (23%)
  blocking collectives  76.4 us (16%)
  starting transfers between devices  40.4 us (8%)
  between operations  14.1 us (3%)
  other arithmetic  11.4 us (2%)
  local copies, waits for them, and re-layouts  10.2 us (2%)
    psum x3, waiting for transfers between devices, layer_pass(): summed = lax.psum(head_terms, 'tp')  91.7 us
    psum x3, waiting for transfers between devices, layer_pass(): squares, partial_proj = lax.psum((squares, partial_proj), 'ctx')  88.7 us
    dot_general x3, matrix products, layer_pass(): jnp.dot(scaled, qkv_weight, preferred_element_type=jnp.float32)  47.2 us
    dot_general x3, matrix products, layer_pass(): jnp.dot(attention.reshape(row_count, -1), out_weight, preferred_element_t...  40.5 us
    all_gather x3, blocking collectives, layer_pass(): attention = lax.all_gather(attention_share, 'ctx', axis=0, tiled=True)  39.4 us
    psum x3, blocking collectives, layer_pass(): squares, partial_proj = lax.psum((squares, partial_proj), 'ctx')  37 us
    all_to_all x3, waiting for transfers between devices, layer_pass(): lax.all_to_all(local[2][None], 'ctx', split_axis=1, concat_axis=0, tiled=...  17.2 us
    all_to_all x3, waiting for transfers between devices, layer_pass(): lax.all_to_all(local[1][None], 'ctx', split_axis=1, concat_axis=0, tiled=...  14.8 us
  transfers between devices with their start and end apart: 17, of which 17 were waited for; matrix products, arithmetic and copies ran while one was open for 3% of the time, Pallas kernels for 0%

commit v1 on v0

v1 whole, which is shorter than its diff:
```python
import functools
import math

import jax
import jax.numpy as jnp
from jax import lax
from jax.experimental import pallas as pl
from jax.experimental.pallas import tpu as pltpu
from jax.sharding import PartitionSpec as P

EPSILON = 1e-05
NEGATIVE = -1e30
LANES = 128
F32 = jnp.float32
BF16 = jnp.bfloat16


def params(megabytes):
    return pltpu.CompilerParams(vmem_limit_bytes=megabytes << 20)


def whole(shape):
    return pl.BlockSpec(shape, lambda *_: (0,) * len(shape))


def split3(value):
    high = value.astype(BF16).astype(F32)
    rest = value - high
    middle = rest.astype(BF16).astype(F32)
    return high, middle, rest - middle


def divisor(size, largest):
    best = LANES
    while best * 2 <= largest and size % (best * 2) == 0:
        best *= 2
    return best


def project_kernel(chunks, depth, fresh, me_ref, x_ref, aux_ref, w_ref, *rest):
    outs, (xg_ref, sq_ref, acc_ref) = rest[:chunks], rest[chunks:]
    k, step = pl.program_id(0), pl.program_id(1)
    wide = xg_ref.shape[0] * depth

    @pl.when(jnp.logical_and(k == 0, step == 0))
    def _():
        if fresh:
            x = x_ref[...].astype(F32)
            xg = (x * aux_ref[...].astype(F32)).astype(BF16)
            squares = jnp.sum(x * x, axis=1, keepdims=True)
        else:
            turn = aux_ref[...]
            xg = jnp.dot(turn, x_ref[:, :wide], preferred_element_type=F32).astype(BF16)
            terms = jnp.dot(turn, x_ref[:, wide:], preferred_element_type=F32)
            squares = terms[:, 0:1] + terms[:, 1:2] + terms[:, 2:3]
        for i in range(xg_ref.shape[0]):
            xg_ref[i] = xg[:, i * depth : (i + 1) * depth]
        sq_ref[...] = jnp.broadcast_to(squares, sq_ref.shape)

    part = jnp.dot(xg_ref[step], w_ref[...], preferred_element_type=F32)

    @pl.when(step == 0)
    def _():
        acc_ref[...] = part

    @pl.when(step > 0)
    def _():
        acc_ref[...] += part

    width = acc_ref.shape[1]
    for i in range(chunks):

        @pl.when(jnp.logical_and(k == i, step == pl.num_programs(1) - 1))
        def _():
            outs[i][:, :width] = acc_ref[...]
            outs[i][:, width:] = sq_ref[...]


def project(x, aux, w, me, chunks, fresh):
    rows = x.shape[0]
    model, columns = w.shape[1:]
    width = columns // chunks
    depth = divisor(model, 1024)
    shape = jax.ShapeDtypeStruct((rows, width + LANES), F32)
    return pl.pallas_call(
        functools.partial(project_kernel, chunks, depth, fresh),
        out_shape=[shape] * chunks,
        grid_spec=pltpu.PrefetchScalarGridSpec(
            num_scalar_prefetch=1,
            grid=(chunks, model // depth),
            in_specs=[
                whole(x.shape),
                whole(aux.shape),
                pl.BlockSpec(
                    (None, depth, width),
                    lambda k, i, me: (0, i, lax.rem(me[0] - k + chunks, chunks)),
                ),
            ],
            out_specs=[whole(shape.shape)] * chunks,
            scratch_shapes=[
                pltpu.VMEM((model // depth, rows, depth), BF16),
                pltpu.VMEM((rows, LANES), F32),
                pltpu.VMEM((rows, width), F32),
            ],
        ),
        compiler_params=params(24),
        cost_estimate=pl.CostEstimate(
            flops=2 * rows * model * columns, bytes_accessed=2 * model * columns, transcendentals=0
        ),
    )(me, x, aux, w)


def normalize_kernel(model, *refs):
    total = refs[0][...]
    for ref in refs[1:-1]:
        total = total + ref[...]
    out_ref = refs[-1]
    width = out_ref.shape[1]
    scale = lax.rsqrt(total[:, width : width + 1] / model + EPSILON)
    out_ref[...] = (total[:, :width] * scale).astype(BF16)


def normalize(parts, model):
    rows, width = parts[0].shape
    return pl.pallas_call(
        functools.partial(normalize_kernel, model),
        out_shape=jax.ShapeDtypeStruct((rows, width - LANES), BF16),
        compiler_params=params(8),
        cost_estimate=pl.CostEstimate(
            flops=rows * width * 4, bytes_accessed=rows * width * 16, transcendentals=0
        ),
    )(*parts)


def attend_kernel(
    blocks, chunks, batch, group, me_ref, order_ref, lengths_ref, *rest
):
    parts = rest[:blocks]
    pre_k, pre_v, suf_k, suf_v = rest[blocks : blocks + 4]
    outs = rest[blocks + 4 : blocks + 4 + chunks]
    q_ref, s_ref, o_ref = rest[blocks + 4 + chunks :]
    head = pl.program_id(0)
    me = me_ref[0]
    rows, hd = q_ref.shape[1], pre_k.shape[1]
    slots = group + 2
    own = parts[0].shape[1] // hd
    scale = hd**-0.5 * math.log2(math.e)

    @pl.when(head == 0)
    def _():
        for k in range(blocks):
            at = lax.rem(me - k + blocks, blocks)
            for i in range(own):
                q_ref[at * own + i] = parts[k][:, i * hd : (i + 1) * hd]

    first = head * slots
    q = jnp.concatenate([q_ref[first + g] for g in range(group)], axis=0)
    count = group * rows
    positions = pre_k.shape[0]
    samples, depth = suf_k.shape[0], suf_k.shape[1]
    step = divisor(positions, 1024)
    sstep = divisor(depth, 1024)
    pad = -rows % LANES
    zeros = jnp.zeros((pad, hd), BF16)
    keys_new = jnp.concatenate([q_ref[first + group], zeros], axis=0)
    values_new = jnp.concatenate([q_ref[first + group + 1], zeros], axis=0)
    tail = rows + pad

    def dot_t(a, b):
        return lax.dot_general(a, b, (((1,), (1,)), ((), ())), preferred_element_type=F32)

    top = jnp.full((count, LANES), NEGATIVE, F32)

    def keep(top, scores, start):
        s_ref[:, start : start + scores.shape[1]] = scores
        for i in range(0, scores.shape[1], LANES):
            top = jnp.maximum(top, scores[:, i : i + LANES])
        return top

    def masked(scores, mask):
        bias = jnp.where(mask, 0.0, NEGATIVE)
        shaped = scores.reshape(group, rows, scores.shape[1]) + bias[None]
        return shaped.reshape(scores.shape)

    pieces = []
    start = 0
    for i in range(0, positions, step):
        top = keep(top, dot_t(q, pre_k[i : i + step]), start)
        pieces.append((start, step, pre_v, None, i))
        start += step
    for s in range(samples):
        sample = me * samples + s
        row = jnp.int32(0)
        for b in range(batch):
            row = row + jnp.where(order_ref[b] == sample, b, 0)
        length = lengths_ref[sample]
        for i in range(0, depth, sstep):
            r = lax.broadcasted_iota(jnp.int32, (rows, sstep), 0)
            p = lax.broadcasted_iota(jnp.int32, (rows, sstep), 1) + i
            mine = r == row
            for t in range(1, rows // batch):
                mine = jnp.logical_or(mine, r == row + t * batch)
            mask = jnp.logical_and(mine, p < length)
            top = keep(top, masked(dot_t(q, suf_k[s, i : i + sstep]), mask), start)
            pieces.append((start, sstep, suf_v, s, i))
            start += sstep
    r = lax.broadcasted_iota(jnp.int32, (rows, tail), 0)
    p = lax.broadcasted_iota(jnp.int32, (rows, tail), 1)
    gap = jnp.where(me == 0, r - p, -1)
    mask = gap == 0
    for t in range(1, rows // batch):
        mask = jnp.logical_or(mask, gap == t * batch)
    top = keep(top, masked(dot_t(q, keys_new), mask), start)
    pieces.append((start, tail, None, None, 0))

    row_max = jnp.max(top, axis=1, keepdims=True) * scale
    total = jnp.zeros((count, LANES), F32)
    mixed = jnp.zeros((count, hd), F32)
    for start, size, values, s, i in pieces:
        weights = jnp.exp2(s_ref[:, start : start + size] * scale - row_max)
        for lane in range(0, size, LANES):
            total = total + weights[:, lane : lane + LANES]
        if values is None:
            v = values_new
        elif s is None:
            v = values[i : i + size]
        else:
            v = values[s, i : i + size]
        mixed = mixed + jnp.dot(weights.astype(BF16), v, preferred_element_type=F32)
    total = jnp.sum(total, axis=1, keepdims=True)
    mixed = mixed * (1.0 / total)
    level = row_max + jnp.log2(total)
    terms = split3(level)

    per = o_ref.shape[2] // hd - 1
    lane = lax.broadcasted_iota(jnp.int32, (rows, LANES), 1)
    for first_head in range(0, group, per):
        at = head * (group // per) + first_head // per
        stats = jnp.zeros((rows, LANES), F32)
        for i in range(per):
            g = first_head + i
            o_ref[at, :, i * hd : (i + 1) * hd] = mixed[g * rows : (g + 1) * rows].astype(BF16)
            for n in range(3):
                stats = jnp.where(lane == n * per + i, terms[n][g * rows : (g + 1) * rows], stats)
        o_ref[at, :, per * hd :] = stats.astype(BF16)

    @pl.when(head == pl.num_programs(0) - 1)
    def _():
        for k in range(chunks):
            outs[k][...] = o_ref[lax.rem(me - k + chunks, chunks)]


def attend(parts, keys, values, suffix_keys, suffix_values, me, order, lengths, chunks, group):
    rows = parts[0].shape[0]
    heads, positions, hd = keys.shape[1:]
    samples, depth = suffix_keys.shape[2:4]
    width = heads * group * hd // chunks + LANES
    total = positions + samples * depth + rows + (-rows % LANES)
    shape = jax.ShapeDtypeStruct((rows, width), BF16)
    cache = pl.BlockSpec((None, None, positions, hd), lambda h, *_: (0, h, 0, 0))
    suffix = pl.BlockSpec((None, None, samples, depth, hd), lambda h, *_: (0, h, 0, 0, 0))
    return pl.pallas_call(
        functools.partial(attend_kernel, len(parts), chunks, order.shape[0], group),
        out_shape=[shape] * chunks,
        grid_spec=pltpu.PrefetchScalarGridSpec(
            num_scalar_prefetch=3,
            grid=(heads,),
            in_specs=[whole(part.shape) for part in parts] + [cache, cache, suffix, suffix],
            out_specs=[whole(shape.shape)] * chunks,
            scratch_shapes=[
                pltpu.VMEM((heads * (group + 2), rows, hd), BF16),
                pltpu.VMEM((group * rows, total), F32),
                pltpu.VMEM((chunks, rows, width), BF16),
            ],
        ),
        compiler_params=params(56),
        cost_estimate=pl.CostEstimate(
            flops=4 * heads * group * rows * total * hd,
            bytes_accessed=4 * heads * total * hd,
            transcendentals=heads * group * rows * total,
        ),
    )(me, order, lengths, *parts, keys, values, suffix_keys, suffix_values)


def merge_kernel(hd, *refs):
    parts, out_ref = refs[:-1], refs[-1]
    per = out_ref.shape[1] // hd
    stats = [ref[:, per * hd :].astype(F32) for ref in parts]
    for i in range(per):
        levels = [
            s[:, i : i + 1] + s[:, per + i : per + i + 1] + s[:, 2 * per + i : 2 * per + i + 1]
            for s in stats
        ]
        top = functools.reduce(jnp.maximum, levels)
        shares = [jnp.exp2(level - top) for level in levels]
        inverse = 1.0 / functools.reduce(jnp.add, shares)
        mixed = 0.0
        for ref, share in zip(parts, shares):
            mixed = mixed + ref[:, i * hd : (i + 1) * hd].astype(F32) * (share * inverse)
        out_ref[:, i * hd : (i + 1) * hd] = mixed.astype(BF16)


def merge(parts, hd):
    rows, width = parts[0].shape
    return pl.pallas_call(
        functools.partial(merge_kernel, hd),
        out_shape=jax.ShapeDtypeStruct((rows, width - LANES), BF16),
        compiler_params=params(8),
        cost_estimate=pl.CostEstimate(
            flops=rows * width * 8, bytes_accessed=rows * width * 10, transcendentals=rows * LANES
        ),
    )(*parts)


def output_kernel(blocks, per, groups, me_ref, turn_ref, *rest):
    parts = rest[:blocks]
    w_ref = rest[blocks]
    outs = rest[blocks + 1 : blocks + 1 + groups]
    a_ref, acc_ref = rest[blocks + 1 + groups :]
    step = pl.program_id(0)
    depth = a_ref.shape[2]

    @pl.when(step == 0)
    def _():
        for k in range(blocks):
            turned = jnp.dot(turn_ref[...], parts[k][...], preferred_element_type=F32).astype(BF16)
            for i in range(per):
                a_ref[k * per + i] = turned[:, i * depth : (i + 1) * depth]

    part = jnp.dot(a_ref[step], w_ref[...], preferred_element_type=F32)

    @pl.when(step == 0)
    def _():
        acc_ref[...] = part

    @pl.when(step > 0)
    def _():
        acc_ref[...] += part

    @pl.when(step == pl.num_programs(0) - 1)
    def _():
        size = outs[0].shape[0]
        stride = acc_ref.shape[0] // groups
        for k in range(groups):
            outs[k][...] = acc_ref[k * stride : k * stride + size, :]


def output(parts, turn, w, me, groups, size):
    blocks = len(parts)
    rows, width = parts[0].shape
    columns = w.shape[2]
    depth = divisor(width, 512)
    per = width // depth
    padded = turn.shape[0]
    shape = jax.ShapeDtypeStruct((size, columns), F32)
    return pl.pallas_call(
        functools.partial(output_kernel, blocks, per, groups),
        out_shape=[shape] * groups,
        grid_spec=pltpu.PrefetchScalarGridSpec(
            num_scalar_prefetch=1,
            grid=(blocks * per,),
            in_specs=[whole(turn.shape)]
            + [whole(part.shape) for part in parts]
            + [
                pl.BlockSpec(
                    (None, depth, columns),
                    lambda i, me: (0, lax.rem(me[0] - i // per + blocks, blocks) * per + i % per, 0),
                )
            ],
            out_specs=[whole(shape.shape)] * groups,
            scratch_shapes=[
                pltpu.VMEM((blocks * per, padded, depth), BF16),
                pltpu.VMEM((padded, columns), F32),
            ],
        ),
        compiler_params=params(24),
        cost_estimate=pl.CostEstimate(
            flops=2 * rows * blocks * width * columns,
            bytes_accessed=2 * blocks * width * columns,
            transcendentals=0,
        ),
    )(me, turn, *parts, w)


def add_kernel(*refs):
    parts, gain_ref, y_ref, out_ref = refs[:-3], refs[-3], refs[-2], refs[-1]
    total = parts[0][...]
    for ref in parts[1:]:
        total = total + ref[...]
    y_ref[...] = total
    wide = total.shape[1]
    out_ref[:, :wide] = (total * gain_ref[...].astype(F32)).astype(BF16)
    squares = jnp.sum(total * total, axis=1, keepdims=True)
    lane = lax.broadcasted_iota(jnp.int32, (total.shape[0], LANES), 1)
    terms = jnp.zeros((total.shape[0], LANES), F32)
    for n, term in enumerate(split3(squares)):
        terms = jnp.where(lane == n, term, terms)
    out_ref[:, wide:] = terms.astype(BF16)


def add_up(parts, gain):
    rows, width = parts[0].shape
    return pl.pallas_call(
        add_kernel,
        out_shape=[
            jax.ShapeDtypeStruct((rows, width), F32),
            jax.ShapeDtypeStruct((rows, width + LANES), BF16),
        ],
        compiler_params=params(8),
        cost_estimate=pl.CostEstimate(
            flops=rows * width * 8, bytes_accessed=rows * width * 24, transcendentals=0
        ),
    )(*parts, gain)


def back(parts, axis):
    count = lax.axis_size(axis)
    return [parts[0]] + [
        lax.ppermute(parts[k], axis, [(i, (i - k) % count) for i in range(count)])
        for k in range(1, count)
    ]


def around(part, axis):
    count = lax.axis_size(axis)
    return [part] + [
        lax.ppermute(part, axis, [(i, (i + k) % count) for i in range(count)])
        for k in range(1, count)
    ]


def on_device(
    tokens_in,
    norm_gain,
    w_qkv,
    w_out,
    prefix_keys,
    prefix_values,
    suffix_keys,
    suffix_values,
    lengths,
    order,
):
    sections = lax.axis_size("section")
    ctx, tp = lax.axis_size("ctx"), lax.axis_size("tp")
    steps, batch, columns = tokens_in.shape
    rows = steps * batch
    heads, hd = prefix_keys.shape[1], prefix_keys.shape[4 - 1]
    slots = w_qkv.shape[2] // (heads * hd)
    group = slots - 2
    model = w_qkv.shape[1] * ctx
    share = batch // tp
    size = steps * share
    section, tp_me = lax.axis_index("section"), lax.axis_index("tp")
    me = lax.axis_index("ctx").astype(jnp.int32).reshape(1)
    even = (heads * slots) % ctx == 0
    zero = jnp.zeros((1,), jnp.int32)

    stride = size + (-size % 8)
    i = jnp.arange(tp * stride)
    k, j = i // stride, i % stride
    owner = lax.rem(tp_me - k + tp, tp)
    natural = jnp.where(j < size, (j // share) * batch + owner * share + j % share, -1)
    turn = (natural[:, None] == jnp.arange(rows)[None, :]).astype(BF16)
    i = jnp.arange(tp * size)
    k, j = i // size, i % size
    owner = lax.rem(tp_me - k + tp, tp)
    natural = (j // share) * batch + owner * share + j % share
    unturn = (jnp.arange(rows)[:, None] == natural[None, :]).astype(BF16)

    mine = lax.dynamic_slice_in_dim(tokens_in, tp_me * share, share, 1)
    residual = mine.astype(F32).reshape(size, columns)
    gain = norm_gain
    next_gain = lax.ppermute(
        norm_gain, "section", [(s, (s - 1) % sections) for s in range(sections)]
    )

    x, aux = tokens_in.reshape(rows, columns), gain
    result = None
    for layer in range(sections):
        fresh = layer == 0
        if even:
            parts = back(project(x, aux, w_qkv, me, ctx, fresh), "ctx")
            parts = around(normalize(parts, model), "ctx")
        else:
            part = project(x, aux, w_qkv, zero, 1, fresh)[0]
            parts = [normalize([lax.psum(part, "ctx")], model)]
        parts = attend(
            parts, prefix_keys, prefix_values, suffix_keys, suffix_values,
            me, order, lengths, ctx, group,
        )
        parts = around(merge(back(parts, "ctx"), hd), "ctx")
        parts = back(output(parts, turn, w_out, me, tp, size), "tp")
        y, message = add_up(parts + [residual], next_gain)
        result = y if result is None else jnp.where(section == layer, y, result)
        if layer + 1 < sections:
            here, there = layer * tp, (layer + 1) * tp
            received = [
                lax.ppermute(
                    message, ("section", "tp"), [(here + n, there + (n + k) % tp) for n in range(tp)]
                )
                for k in range(tp)
            ]
            x, aux = jnp.concatenate(received, axis=0), unturn
            residual = lax.ppermute(y, "section", [(layer, layer + 1)])
    return result.reshape(1, steps, share, columns)


def solution(mesh):
    in_specs = (
        P(None, None, "ctx"),
        P("section", "ctx"),
        P("section", "ctx", "tp"),
        P("section", "tp", "ctx"),
        P("section", "tp", "ctx", None),
        P("section", "tp", "ctx", None),
        P("section", "tp", "ctx", None, None),
        P("section", "tp", "ctx", None, None),
        P(),
        P(),
    )
    out_specs = P("section", None, "tp", "ctx")
    return jax.shard_map(
        on_device, mesh=mesh, in_specs=in_specs, out_specs=out_specs, check_vma=False
    )
```

time: 483 us -> 184 us (0.38)
  waiting for transfers between devices: 221 us -> 39.4 us
  matrix products: 109 us -> 0 us
  Pallas kernels: 0 us -> 86 us
  blocking collectives: 76.4 us -> 0 us
  between operations: 14.1 us -> 0.26 us
  starting transfers between devices: 40.4 us -> 51.3 us
  other arithmetic: 11.4 us -> 1.14 us
  local copies, waits for them, and re-layouts: 10.2 us -> 4.51 us
    psum x6 -> x0, waiting for transfers between devices: 180 us -> none  [the longest x3 91.7 us: layer_pass(): summed = lax.psum(head_terms, 'tp')]
    dot_general x35 -> x0, matrix products: 109 us -> none  [the longest x3 47.2 us: layer_pass(): jnp.dot(scaled, qkv_weight, preferred_element_type=jnp.float32)]
    pallas_call x0 -> x12, Pallas kernels: none -> 86 us  [the longest x2 38.3 us: project(): pl.pallas_call(functools.partial(project_kernel, chunks, depth, fresh), o...]
    ppermute x2 -> x36, starting transfers between devices: 6.76 us -> 51.3 us  [the longest x18 20.5 us: back(): lax.ppermute(parts[k], axis, [(i, (i - k) % count) for i in range(count)])]
    all_gather x3 -> x0, blocking collectives: 39.4 us -> none  [layer_pass(): attention = lax.all_gather(attention_share, 'ctx', axis=0, tiled=True)]
    psum x3 -> x0, blocking collectives: 37 us -> none  [layer_pass(): squares, partial_proj = lax.psum((squares, partial_proj), 'ctx')]
    all_to_all x9 -> x0, waiting for transfers between devices: 35.1 us -> none  [the longest x3 17.2 us: layer_pass(): lax.all_to_all(local[2][None], 'ctx', split_axis=1, concat_axis=0, tiled=...]
    ppermute x2 -> x36, waiting for transfers between devices: 4.96 us -> 39.4 us  [the longest x18 31 us: back(): lax.ppermute(parts[k], axis, [(i, (i - k) % count) for i in range(count)])]
  transfers between devices with their start and end apart: 17 -> 36, of which waited for: 17 -> 24; matrix products, arithmetic and copies ran while one was open for 3% -> 1% of each run, Pallas kernels for 0% -> 21%
where the time goes in v1:
time: 184 us; the launch traced here: 183 us
  Pallas kernels  86 us (47%)
  starting transfers between devices  51.3 us (28%)
  waiting for transfers between devices  39.4 us (21%)
  local copies, waits for them, and re-layouts  4.51 us (2%)
    pallas_call x2, Pallas kernels, project(): pl.pallas_call(functools.partial(project_kernel, chunks, depth, fresh), o...  38.3 us
    ppermute x18, waiting for transfers between devices, back(): lax.ppermute(parts[k], axis, [(i, (i - k) % count) for i in range(count)])  31 us
    pallas_call x2, Pallas kernels, output(): pl.pallas_call(functools.partial(output_kernel, blocks, per, groups), out...  28.9 us
    ppermute x18, starting transfers between devices, back(): lax.ppermute(parts[k], axis, [(i, (i - k) % count) for i in range(count)])  20.5 us
    pallas_call x2, Pallas kernels, attend(): pl.pallas_call(functools.partial(attend_kernel, len(parts), chunks, order...  17.3 us
    ppermute x12, starting transfers between devices, around(): lax.ppermute(part, axis, [(i, (i + k) % count) for i in range(count)])  16.9 us
    ppermute x4, starting transfers between devices, on_device(): lax.ppermute(message, ('section', 'tp'), [(here + n, there + (n + k) % tp...  7.57 us
    ppermute x12, waiting for transfers between devices, around(): lax.ppermute(part, axis, [(i, (i + k) % count) for i in range(count)])  6.81 us
  transfers between devices with their start and end apart: 36, of which 24 were waited for; matrix products, arithmetic and copies ran while one was open for 1% of the time, Pallas kernels for 21%

profile of v1, /device:TPU:0, one launch (start us, length us, event | category | flops | bytes accessed | tf_op | source)
XLA Modules:
  0.0 182.6 jit_solution(11796051283217762903)
XLA Ops:
  0.0 0.9 copy-done
  0.9 19.1 %shard_map.100 = (f32[16,1280]{1,0:T(8,128)S(1)}, f32[16,1280]{1,0:T(8,128)S(1)}, f32[16,1280]{1,0:T(8,128)S(1)}, f32[16,1280]{1,0:T(8,128)S(1)}) custom-call(s32[1]{0:T(128)} %bitcast.me_ref, bf16[16,4096]{1,0:T(8,128)(2,1)S(1)} %bitcast.2, bf16[1,4096]{1,0:T(2,128)(2,1)} %aux_ref.1, bf16[1,4096,4608]{2,1,0:T(8,128)(2,1)} %w_ref.3), custom_call_target="tpu_custom_call" | custom-call | flops 603979776 | bytes 37748736 | tf_op jit(solution)/shard_map/pallas_call | solution.py:85
  20.0 5.1 %collective-permute-start = (f32[16,1280]{1,0:T(8,128)S(1)}, f32[16,1280]{1,0:T(8,128)S(1)}, u32[]{:S(2)}, u32[]{:S(2)}) collective-permute-start(f32[16,1280]{1,0:T(8,128)S(1)} %get-tuple-element.33), channel_id=1, source_target_pairs={{0,3},{1,0},{2,1},{3,2},{4,7},{5,4},{6,5},{7,6},{8,11},{9,8},{10,9... | collective-permute-start | bytes 245768 | tf_op jit(solution)/shard_map/ppermute | solution.py:419
  25.1 1.0 collective-permute-start.2
  26.1 1.5 collective-permute-start.15
  27.9 4.7 %collective-permute-done.1.refs_2_ = f32[16,1280]{1,0:T(8,128)S(1)} collective-permute-done((f32[16,1280]{1,0:T(8,128)S(1)}, f32[16,1280]{1,0:T(8,128)S(1)}, u32[]{:S(2)}, u32[]{:S(2)}) %collective-permute-start.1) | collective-permute-done | bytes 81952 | tf_op jit(solution)/shard_map/ppermute | solution.py:419
  33.0 2.5 %collective-permute-start.4 = (bf16[16,1152]{1,0:T(8,128)(2,1)S(1)}, bf16[16,1152]{1,0:T(8,128)(2,1)S(1)}, u32[]{:S(2)}, u32[]{:S(2)}) collective-permute-start(bf16[16,1152]{1,0:T(8,128)(2,1)S(1)} %shard_map.101.rest_0_), channel_id=1, source_target_pairs={{0,2},{1,3},{2,0},{3,1},{4,6},{5,7},{6,4},{7,5},{8,10},{9,11},{10,... | collective-permute-start | bytes 110600 | tf_op jit(solution)/shard_map/ppermute | solution.py:427
  35.4 2.3 %collective-permute-start.5 = (bf16[16,1152]{1,0:T(8,128)(2,1)S(1)}, bf16[16,1152]{1,0:T(8,128)(2,1)S(1)}, u32[]{:S(2)}, u32[]{:S(2)}) collective-permute-start(bf16[16,1152]{1,0:T(8,128)(2,1)S(1)} %shard_map.101.rest_0_), channel_id=1, source_target_pairs={{0,3},{1,0},{2,1},{3,2},{4,7},{5,4},{6,5},{7,6},{8,11},{9,8},{10,9... | collective-permute-start | bytes 110600 | tf_op jit(solution)/shard_map/ppermute | solution.py:427
  37.8 0.9 dynamic-slice_convert_fusion
  40.0 8.6 %shard_map.102 = (bf16[16,1152]{1,0:T(8,128)(2,1)}, bf16[16,1152]{1,0:T(8,128)(2,1)}, bf16[16,1152]{1,0:T(8,128)(2,1)}, bf16[16,1152]{1,0:T(8,128)(2,1)}) custom-call(s32[1]{0:T(128)} %bitcast.me_ref, s32[8]{0:T(128)} %order_ref.3, s32[8]{0:T(128)} %lengths_ref.3, bf16[16,1152]{1,0:T(8,128)(2,1)} %copy-done.1, bf16[16,1152]{1,0:T(8,128)(2,1)} %copy-done.5, ...), custom_call_target="tpu_custom_call" | custom-call | flops 1375731712 | bytes 5373952 | tf_op jit(solution)/shard_map/pallas_call | solution.py:262
  48.7 4.2 %collective-permute-start.6 = (bf16[16,1152]{1,0:T(8,128)(2,1)}, bf16[16,1152]{1,0:T(8,128)(2,1)S(1)}, u32[]{:S(2)}, u32[]{:S(2)}) collective-permute-start(bf16[16,1152]{1,0:T(8,128)(2,1)} %get-tuple-element.37), channel_id=1, source_target_pairs={{0,3},{1,0},{2,1},{3,2},{4,7},{5,4},{6,5},{7,6},{8,11},{9,8},{10,9... | collective-permute-start | bytes 110600 | tf_op jit(solution)/shard_map/ppermute | solution.py:419
  53.5 1.3 collective-permute-done.6.refs_1_
  54.8 3.1 %collective-permute-done.7.refs_2_ = bf16[16,1152]{1,0:T(8,128)(2,1)S(1)} collective-permute-done((bf16[16,1152]{1,0:T(8,128)(2,1)}, bf16[16,1152]{1,0:T(8,128)(2,1)S(1)}, u32[]{:S(2)}, u32[]{:S(2)}) %collective-permute-start.7) | collective-permute-done | bytes 36896 | tf_op jit(solution)/shard_map/ppermute | solution.py:419
  57.9 1.2 collective-permute-done.8.refs_3_
  59.1 0.8 copy-done.3
  60.1 0.9 collective-permute-start.10
  61.7 1.3 collective-permute-start.9
  63.1 2.0 %collective-permute-done.10.rest_2_ = bf16[16,1024]{1,0:T(8,128)(2,1)S(1)} collective-permute-done((bf16[16,1024]{1,0:T(8,128)(2,1)S(1)}, bf16[16,1024]{1,0:T(8,128)(2,1)S(1)}, u32[]{:S(2)}, u32[]{:S(2)}) %collective-permute-start.10) | collective-permute-done | bytes 32800 | tf_op jit(solution)/shard_map/ppermute | solution.py:427
  65.3 2.2 %collective-permute-done.9.rest_1_ = bf16[16,1024]{1,0:T(8,128)(2,1)S(1)} collective-permute-done((bf16[16,1024]{1,0:T(8,128)(2,1)S(1)}, bf16[16,1024]{1,0:T(8,128)(2,1)S(1)}, u32[]{:S(2)}, u32[]{:S(2)}) %collective-permute-start.9) | collective-permute-done | bytes 32800 | tf_op jit(solution)/shard_map/ppermute | solution.py:427
  67.4 14.4 %shard_map.104 = (f32[4,4096]{1,0:T(4,128)S(1)}, f32[4,4096]{1,0:T(4,128)S(1)}, f32[4,4096]{1,0:T(4,128)S(1)}, f32[4,4096]{1,0:T(4,128)S(1)}) custom-call(s32[1]{0:T(128)} %bitcast.me_ref, bf16[32,16]{1,0:T(8,128)(2,1)S(1)} %fusion.turn_ref, bf16[16,1024]{1,0:T(8,128)(2,1)S(1)} %shard_map.103.rest_0_, bf16[16,1024]{1,0:T(8,128)(2,1)S(1)} %collective-permute-done.9.rest_1_, ...), custom_call_target="tpu_custom_call" | custom-call | flops 536870912 | bytes 33554432 | tf_op jit(solution)/shard_map/pallas_call | solution.py:356
  81.9 1.6 collective-permute-start.13
  83.8 3.8 %collective-permute-done.13.refs_2_ = f32[4,4096]{1,0:T(4,128)S(1)} collective-permute-done((f32[4,4096]{1,0:T(4,128)S(1)}, f32[4,4096]{1,0:T(4,128)S(1)}, u32[]{:S(2)}, u32[]{:S(2)}) %collective-permute-start.13) | collective-permute-done | bytes 65568 | tf_op jit(solution)/shard_map/ppermute | solution.py:419
  87.9 3.4 %collective-permute-start.16 = (bf16[4,4224]{1,0:T(4,128)(2,1)S(1)}, bf16[4,4224]{1,0:T(4,128)(2,1)S(1)}, u32[]{:S(2)}, u32[]{:S(2)}) collective-permute-start(bf16[4,4224]{1,0:T(4,128)(2,1)S(1)} %get-tuple-element.44), channel_id=1, source_target_pairs={{0,16},{4,20},{8,24},{12,28},{1,17},{5,21},{9,25},{13,29},{2,18},{... | collective-permute-start | bytes 101384 | tf_op jit(solution)/shard_map/ppermute | solution.py:499
  91.3 1.3 collective-permute-start.17
  92.6 1.6 collective-permute-start.18
  94.2 1.3 collective-permute-start.19
  95.8 1.3 collective-permute-done.19
  97.2 19.2 %shard_map.106 = (f32[16,1280]{1,0:T(8,128)S(1)}, f32[16,1280]{1,0:T(8,128)S(1)}, f32[16,1280]{1,0:T(8,128)S(1)}, f32[16,1280]{1,0:T(8,128)S(1)}) custom-call(s32[1]{0:T(128)} %bitcast.me_ref, bf16[16,4224]{1,0:T(8,128)(2,1)S(1)} %pad_maximum_fusion.x_ref, bf16[16,16]{1,0:T(8,128)(2,1)S(1)} %fusion.1.aux_ref, bf16[1,4096,4608]{2,1,0:T(8,128)(2,1)} %w_ref.3), custom_call_target="tpu_custom_call" | custom-call | flops 603979776 | bytes 37748736 | tf_op jit(solution)/shard_map/pallas_call | solution.py:85
  116.4 1.1 collective-permute-start.20
  117.5 1.0 collective-permute-start.22
  118.5 3.0 %collective-permute-done.20.refs_1_ = f32[16,1280]{1,0:T(8,128)S(1)} collective-permute-done((f32[16,1280]{1,0:T(8,128)S(1)}, f32[16,1280]{1,0:T(8,128)S(1)}, u32[]{:S(2)}, u32[]{:S(2)}) %collective-permute-start.20) | collective-permute-done | bytes 81952 | tf_op jit(solution)/shard_map/ppermute | solution.py:419
  121.5 4.1 %collective-permute-done.21.refs_2_ = f32[16,1280]{1,0:T(8,128)S(1)} collective-permute-done((f32[16,1280]{1,0:T(8,128)S(1)}, f32[16,1280]{1,0:T(8,128)S(1)}, u32[]{:S(2)}, u32[]{:S(2)}) %collective-permute-start.21) | collective-permute-done | bytes 81952 | tf_op jit(solution)/shard_map/ppermute | solution.py:419
  125.7 1.9 %collective-permute-start.24 = (bf16[16,1152]{1,0:T(8,128)(2,1)S(1)}, bf16[16,1152]{1,0:T(8,128)(2,1)S(1)}, u32[]{:S(2)}, u32[]{:S(2)}) collective-permute-start(bf16[16,1152]{1,0:T(8,128)(2,1)S(1)} %shard_map.107.rest_0_), channel_id=1, source_target_pairs={{0,2},{1,3},{2,0},{3,1},{4,6},{5,7},{6,4},{7,5},{8,10},{9,11},{10,... | collective-permute-start | bytes 110600 | tf_op jit(solution)/shard_map/ppermute | solution.py:427
  127.5 2.6 %collective-permute-start.25 = (bf16[16,1152]{1,0:T(8,128)(2,1)S(1)}, bf16[16,1152]{1,0:T(8,128)(2,1)S(1)}, u32[]{:S(2)}, u32[]{:S(2)}) collective-permute-start(bf16[16,1152]{1,0:T(8,128)(2,1)S(1)} %shard_map.107.rest_0_), channel_id=1, source_target_pairs={{0,3},{1,0},{2,1},{3,2},{4,7},{5,4},{6,5},{7,6},{8,11},{9,8},{10,9... | collective-permute-start | bytes 110600 | tf_op jit(solution)/shard_map/ppermute | solution.py:427
  130.2 1.3 collective-permute-done.23.rest_1_
  132.7 8.6 %shard_map.108 = (bf16[16,1152]{1,0:T(8,128)(2,1)}, bf16[16,1152]{1,0:T(8,128)(2,1)}, bf16[16,1152]{1,0:T(8,128)(2,1)}, bf16[16,1152]{1,0:T(8,128)(2,1)}) custom-call(s32[1]{0:T(128)} %bitcast.me_ref, s32[8]{0:T(128)} %order_ref.3, s32[8]{0:T(128)} %lengths_ref.3, bf16[16,1152]{1,0:T(8,128)(2,1)} %copy-done.2, bf16[16,1152]{1,0:T(8,128)(2,1)} %copy-done.6, ...), custom_call_target="tpu_custom_call" | custom-call | flops 1375731712 | bytes 5373952 | tf_op jit(solution)/shard_map/pallas_call | solution.py:262
  141.3 3.9 %collective-permute-start.26 = (bf16[16,1152]{1,0:T(8,128)(2,1)}, bf16[16,1152]{1,0:T(8,128)(2,1)S(1)}, u32[]{:S(2)}, u32[]{:S(2)}) collective-permute-start(bf16[16,1152]{1,0:T(8,128)(2,1)} %get-tuple-element.50), channel_id=1, source_target_pairs={{0,3},{1,0},{2,1},{3,2},{4,7},{5,4},{6,5},{7,6},{8,11},{9,8},{10,9... | collective-permute-start | bytes 110600 | tf_op jit(solution)/shard_map/ppermute | solution.py:419
  145.9 1.3 collective-permute-done.26.refs_1_
  147.2 3.1 %collective-permute-done.27.refs_2_ = bf16[16,1152]{1,0:T(8,128)(2,1)S(1)} collective-permute-done((bf16[16,1152]{1,0:T(8,128)(2,1)}, bf16[16,1152]{1,0:T(8,128)(2,1)S(1)}, u32[]{:S(2)}, u32[]{:S(2)}) %collective-permute-start.27) | collective-permute-done | bytes 36896 | tf_op jit(solution)/shard_map/ppermute | solution.py:419
  150.3 0.9 collective-permute-done.28.refs_3_
  152.3 1.4 collective-permute-start.30
  153.7 2.8 %collective-permute-start.31 = (bf16[16,1024]{1,0:T(8,128)(2,1)S(1)}, bf16[16,1024]{1,0:T(8,128)(2,1)S(1)}, u32[]{:S(2)}, u32[]{:S(2)}) collective-permute-start(bf16[16,1024]{1,0:T(8,128)(2,1)S(1)} %shard_map.109.rest_0_), channel_id=1, source_target_pairs={{0,3},{1,0},{2,1},{3,2},{4,7},{5,4},{6,5},{7,6},{8,11},{9,8},{10,9... | collective-permute-start | bytes 98312 | tf_op jit(solution)/shard_map/ppermute | solution.py:427
  156.6 4.8 %collective-permute-start.35 = (f32[4,4096]{1,0:T(4,128)S(1)}, f32[4,4096]{1,0:T(4,128)S(1)}, u32[]{:S(2)}, u32[]{:S(2)}) collective-permute-start(f32[4,4096]{1,0:T(4,128)S(1)} %get-tuple-element.57), channel_id=1, source_target_pairs={{0,16},{1,17},{2,18},{3,19},{4,20},{5,21},{6,22},{7,23},{8,24},{9,... | collective-permute-start | bytes 196616 | tf_op jit(solution)/shard_map/ppermute | solution.py:505
  161.4 14.4 %shard_map.110 = (f32[4,4096]{1,0:T(4,128)S(1)}, f32[4,4096]{1,0:T(4,128)S(1)}, f32[4,4096]{1,0:T(4,128)S(1)}, f32[4,4096]{1,0:T(4,128)S(1)}) custom-call(s32[1]{0:T(128)} %bitcast.me_ref, bf16[32,16]{1,0:T(8,128)(2,1)S(1)} %fusion.turn_ref, bf16[16,1024]{1,0:T(8,128)(2,1)S(1)} %shard_map.109.rest_0_, bf16[16,1024]{1,0:T(8,128)(2,1)S(1)} %collective-permute-done.29.rest_1_, ...), custom_call_target="tpu_custom_call" | custom-call | flops 536870912 | bytes 33554432 | tf_op jit(solution)/shard_map/pallas_call | solution.py:356
  175.9 1.0 collective-permute-start.33
  177.1 1.0 collective-permute-done.32.refs_1_
  178.0 2.9 %collective-permute-done.33.refs_2_ = f32[4,4096]{1,0:T(4,128)S(1)} collective-permute-done((f32[4,4096]{1,0:T(4,128)S(1)}, f32[4,4096]{1,0:T(4,128)S(1)}, u32[]{:S(2)}, u32[]{:S(2)}) %collective-permute-start.33) | collective-permute-done | bytes 65568 | tf_op jit(solution)/shard_map/ppermute | solution.py:419
  181.2 0.8 shard_map.111
  (67 shorter events, 9.2 us)
Async XLA Ops:
  0.0 0.9 copy-start
  20.0 8.0 %collective-permute-start = (f32[16,1280]{1,0:T(8,128)S(1)}, f32[16,1280]{1,0:T(8,128)S(1)}, u32[]{:S(2)}, u32[]{:S(2)}) collective-permute-start(f32[16,1280]{1,0:T(8,128)S(1)} %get-tuple-element.33), channel_id=1, source_target_pairs={{0,3},{1,0},{2,1},{3,2},{4,7},{5,4},{6,5},{7,6},{8,11},{9,8},{10,9... | collective-permute-start | bytes 245768 | tf_op jit(solution)/shard_map/ppermute | solution.py:419
  25.1 7.5 %collective-permute-start.1 = (f32[16,1280]{1,0:T(8,128)S(1)}, f32[16,1280]{1,0:T(8,128)S(1)}, u32[]{:S(2)}, u32[]{:S(2)}) collective-permute-start(f32[16,1280]{1,0:T(8,128)S(1)} %get-tuple-element.34), channel_id=1, source_target_pairs={{0,2},{1,3},{2,0},{3,1},{4,6},{5,7},{6,4},{7,5},{8,10},{9,11},{10,... | collective-permute-start | bytes 245768 | tf_op jit(solution)/shard_map/ppermute | solution.py:419
  25.1 7.5 %collective-permute-start.2 = (f32[16,1280]{1,0:T(8,128)S(1)}, f32[16,1280]{1,0:T(8,128)S(1)}, u32[]{:S(2)}, u32[]{:S(2)}) collective-permute-start(f32[16,1280]{1,0:T(8,128)S(1)} %get-tuple-element.35), channel_id=1, source_target_pairs={{0,1},{1,2},{2,3},{3,0},{4,5},{5,6},{6,7},{7,4},{8,9},{9,10},{10,1... | collective-permute-start | bytes 245768 | tf_op jit(solution)/shard_map/ppermute | solution.py:419
  26.1 57.6 %collective-permute-start.15 = (bf16[1,4096]{1,0:T(2,128)(2,1)}, bf16[1,4096]{1,0:T(2,128)(2,1)S(1)}, u32[]{:S(2)}, u32[]{:S(2)}) collective-permute-start(bf16[1,4096]{1,0:T(2,128)(2,1)} %aux_ref.1), channel_id=1, source_target_pairs={{0,16},{16,0},{1,17},{17,1},{2,18},{18,2},{3,19},{19,3},{4,20},{20... | collective-permute-start | bytes 24584 | tf_op jit(solution)/shard_map/ppermute | solution.py:474
  32.7 6.7 %copy-start.1 = (bf16[16,1152]{1,0:T(8,128)(2,1)}, bf16[16,1152]{1,0:T(8,128)(2,1)S(1)}, u32[]{:S(2)}) copy-start(bf16[16,1152]{1,0:T(8,128)(2,1)S(1)} %shard_map.101.rest_0_) | copy-start | bytes 110596
  32.7 6.0 %collective-permute-start.3 = (bf16[16,1152]{1,0:T(8,128)(2,1)S(1)}, bf16[16,1152]{1,0:T(8,128)(2,1)S(1)}, u32[]{:S(2)}, u32[]{:S(2)}) collective-permute-start(bf16[16,1152]{1,0:T(8,128)(2,1)S(1)} %shard_map.101.rest_0_), channel_id=1, source_target_pairs={{0,1},{1,2},{2,3},{3,0},{4,5},{5,6},{6,7},{7,4},{8,9},{9,10},{10,1... | collective-permute-start | bytes 110600 | tf_op jit(solution)/shard_map/ppermute | solution.py:427
  33.0 5.8 %collective-permute-start.4 = (bf16[16,1152]{1,0:T(8,128)(2,1)S(1)}, bf16[16,1152]{1,0:T(8,128)(2,1)S(1)}, u32[]{:S(2)}, u32[]{:S(2)}) collective-permute-start(bf16[16,1152]{1,0:T(8,128)(2,1)S(1)} %shard_map.101.rest_0_), channel_id=1, source_target_pairs={{0,2},{1,3},{2,0},{3,1},{4,6},{5,7},{6,4},{7,5},{8,10},{9,11},{10,... | collective-permute-start | bytes 110600 | tf_op jit(solution)/shard_map/ppermute | solution.py:427
  35.4 4.0 %collective-permute-start.5 = (bf16[16,1152]{1,0:T(8,128)(2,1)S(1)}, bf16[16,1152]{1,0:T(8,128)(2,1)S(1)}, u32[]{:S(2)}, u32[]{:S(2)}) collective-permute-start(bf16[16,1152]{1,0:T(8,128)(2,1)S(1)} %shard_map.101.rest_0_), channel_id=1, source_target_pairs={{0,3},{1,0},{2,1},{3,2},{4,7},{5,4},{6,5},{7,6},{8,11},{9,8},{10,9... | collective-permute-start | bytes 110600 | tf_op jit(solution)/shard_map/ppermute | solution.py:427
  38.7 0.7 copy-start.5
  38.7 0.7 copy-start.7
  39.4 0.6 copy-start.9
  48.7 6.1 %collective-permute-start.6 = (bf16[16,1152]{1,0:T(8,128)(2,1)}, bf16[16,1152]{1,0:T(8,128)(2,1)S(1)}, u32[]{:S(2)}, u32[]{:S(2)}) collective-permute-start(bf16[16,1152]{1,0:T(8,128)(2,1)} %get-tuple-element.37), channel_id=1, source_target_pairs={{0,3},{1,0},{2,1},{3,2},{4,7},{5,4},{6,5},{7,6},{8,11},{9,8},{10,9... | collective-permute-start | bytes 110600 | tf_op jit(solution)/shard_map/ppermute | solution.py:419
  52.8 5.1 %collective-permute-start.7 = (bf16[16,1152]{1,0:T(8,128)(2,1)}, bf16[16,1152]{1,0:T(8,128)(2,1)S(1)}, u32[]{:S(2)}, u32[]{:S(2)}) collective-permute-start(bf16[16,1152]{1,0:T(8,128)(2,1)} %get-tuple-element.38), channel_id=1, source_target_pairs={{0,2},{1,3},{2,0},{3,1},{4,6},{5,7},{6,4},{7,5},{8,10},{9,11},{10,... | collective-permute-start | bytes 110600 | tf_op jit(solution)/shard_map/ppermute | solution.py:419
  52.8 6.2 %collective-permute-start.8 = (bf16[16,1152]{1,0:T(8,128)(2,1)}, bf16[16,1152]{1,0:T(8,128)(2,1)S(1)}, u32[]{:S(2)}, u32[]{:S(2)}) collective-permute-start(bf16[16,1152]{1,0:T(8,128)(2,1)} %get-tuple-element.39), channel_id=1, source_target_pairs={{0,1},{1,2},{2,3},{3,0},{4,5},{5,6},{6,7},{7,4},{8,9},{9,10},{10,1... | collective-permute-start | bytes 110600 | tf_op jit(solution)/shard_map/ppermute | solution.py:419
  59.1 0.8 copy-start.3
  60.1 5.0 %collective-permute-start.10 = (bf16[16,1024]{1,0:T(8,128)(2,1)S(1)}, bf16[16,1024]{1,0:T(8,128)(2,1)S(1)}, u32[]{:S(2)}, u32[]{:S(2)}) collective-permute-start(bf16[16,1024]{1,0:T(8,128)(2,1)S(1)} %shard_map.103.rest_0_), channel_id=1, source_target_pairs={{0,2},{1,3},{2,0},{3,1},{4,6},{5,7},{6,4},{7,5},{8,10},{9,11},{10,... | collective-permute-start | bytes 98312 | tf_op jit(solution)/shard_map/ppermute | solution.py:427
  61.0 4.3 %collective-permute-start.11 = (bf16[16,1024]{1,0:T(8,128)(2,1)S(1)}, bf16[16,1024]{1,0:T(8,128)(2,1)S(1)}, u32[]{:S(2)}, u32[]{:S(2)}) collective-permute-start(bf16[16,1024]{1,0:T(8,128)(2,1)S(1)} %shard_map.103.rest_0_), channel_id=1, source_target_pairs={{0,3},{1,0},{2,1},{3,2},{4,7},{5,4},{6,5},{7,6},{8,11},{9,8},{10,9... | collective-permute-start | bytes 98312 | tf_op jit(solution)/shard_map/ppermute | solution.py:427
  61.7 5.7 %collective-permute-start.9 = (bf16[16,1024]{1,0:T(8,128)(2,1)S(1)}, bf16[16,1024]{1,0:T(8,128)(2,1)S(1)}, u32[]{:S(2)}, u32[]{:S(2)}) collective-permute-start(bf16[16,1024]{1,0:T(8,128)(2,1)S(1)} %shard_map.103.rest_0_), channel_id=1, source_target_pairs={{0,1},{1,2},{2,3},{3,0},{4,5},{5,6},{6,7},{7,4},{8,9},{9,10},{10,1... | collective-permute-start | bytes 98312 | tf_op jit(solution)/shard_map/ppermute | solution.py:427
  81.9 2.0 %collective-permute-start.12 = (f32[4,4096]{1,0:T(4,128)S(1)}, f32[4,4096]{1,0:T(4,128)S(1)}, u32[]{:S(2)}, u32[]{:S(2)}) collective-permute-start(f32[4,4096]{1,0:T(4,128)S(1)} %get-tuple-element.41), channel_id=1, source_target_pairs={{0,12},{4,0},{8,4},{12,8},{1,13},{5,1},{9,5},{13,9},{2,14},{6,2},{... | collective-permute-start | bytes 196616 | tf_op jit(solution)/shard_map/ppermute | solution.py:419
  81.9 5.7 %collective-permute-start.13 = (f32[4,4096]{1,0:T(4,128)S(1)}, f32[4,4096]{1,0:T(4,128)S(1)}, u32[]{:S(2)}, u32[]{:S(2)}) collective-permute-start(f32[4,4096]{1,0:T(4,128)S(1)} %get-tuple-element.42), channel_id=1, source_target_pairs={{0,8},{4,12},{8,0},{12,4},{1,9},{5,13},{9,1},{13,5},{2,10},{6,14},... | collective-permute-start | bytes 196616 | tf_op jit(solution)/shard_map/ppermute | solution.py:419
  83.5 4.3 %collective-permute-start.14 = (f32[4,4096]{1,0:T(4,128)S(1)}, f32[4,4096]{1,0:T(4,128)S(1)}, u32[]{:S(2)}, u32[]{:S(2)}) collective-permute-start(f32[4,4096]{1,0:T(4,128)S(1)} %get-tuple-element.43), channel_id=1, source_target_pairs={{0,4},{4,8},{8,12},{12,0},{1,5},{5,9},{9,13},{13,1},{2,6},{6,10},{... | collective-permute-start | bytes 196616 | tf_op jit(solution)/shard_map/ppermute | solution.py:419
  87.9 7.6 %collective-permute-start.16 = (bf16[4,4224]{1,0:T(4,128)(2,1)S(1)}, bf16[4,4224]{1,0:T(4,128)(2,1)S(1)}, u32[]{:S(2)}, u32[]{:S(2)}) collective-permute-start(bf16[4,4224]{1,0:T(4,128)(2,1)S(1)} %get-tuple-element.44), channel_id=1, source_target_pairs={{0,16},{4,20},{8,24},{12,28},{1,17},{5,21},{9,25},{13,29},{2,18},{... | collective-permute-start | bytes 101384 | tf_op jit(solution)/shard_map/ppermute | solution.py:499
  91.3 4.2 %collective-permute-start.17 = (bf16[4,4224]{1,0:T(4,128)(2,1)S(1)}, bf16[4,4224]{1,0:T(4,128)(2,1)S(1)}, u32[]{:S(2)}, u32[]{:S(2)}) collective-permute-start(bf16[4,4224]{1,0:T(4,128)(2,1)S(1)} %get-tuple-element.44), channel_id=1, source_target_pairs={{0,20},{4,24},{8,28},{12,16},{1,21},{5,25},{9,29},{13,17},{2,22},{... | collective-permute-start | bytes 101384 | tf_op jit(solution)/shard_map/ppermute | solution.py:499
  92.6 3.2 %collective-permute-start.18 = (bf16[4,4224]{1,0:T(4,128)(2,1)S(1)}, bf16[4,4224]{1,0:T(4,128)(2,1)S(1)}, u32[]{:S(2)}, u32[]{:S(2)}) collective-permute-start(bf16[4,4224]{1,0:T(4,128)(2,1)S(1)} %get-tuple-element.44), channel_id=1, source_target_pairs={{0,24},{4,28},{8,16},{12,20},{1,25},{5,29},{9,17},{13,21},{2,26},{... | collective-permute-start | bytes 101384 | tf_op jit(solution)/shard_map/ppermute | solution.py:499
  94.2 2.9 %collective-permute-start.19 = (bf16[4,4224]{1,0:T(4,128)(2,1)S(1)}, bf16[4,4224]{1,0:T(4,128)(2,1)S(1)}, u32[]{:S(2)}, u32[]{:S(2)}) collective-permute-start(bf16[4,4224]{1,0:T(4,128)(2,1)S(1)} %get-tuple-element.44), channel_id=1, source_target_pairs={{0,28},{4,16},{8,20},{12,24},{1,29},{5,17},{9,21},{13,25},{2,30},{... | collective-permute-start | bytes 101384 | tf_op jit(solution)/shard_map/ppermute | solution.py:499
  116.4 5.0 %collective-permute-start.20 = (f32[16,1280]{1,0:T(8,128)S(1)}, f32[16,1280]{1,0:T(8,128)S(1)}, u32[]{:S(2)}, u32[]{:S(2)}) collective-permute-start(f32[16,1280]{1,0:T(8,128)S(1)} %get-tuple-element.46), channel_id=1, source_target_pairs={{0,3},{1,0},{2,1},{3,2},{4,7},{5,4},{6,5},{7,6},{8,11},{9,8},{10,9... | collective-permute-start | bytes 245768 | tf_op jit(solution)/shard_map/ppermute | solution.py:419
  117.5 8.0 %collective-permute-start.21 = (f32[16,1280]{1,0:T(8,128)S(1)}, f32[16,1280]{1,0:T(8,128)S(1)}, u32[]{:S(2)}, u32[]{:S(2)}) collective-permute-start(f32[16,1280]{1,0:T(8,128)S(1)} %get-tuple-element.47), channel_id=1, source_target_pairs={{0,2},{1,3},{2,0},{3,1},{4,6},{5,7},{6,4},{7,5},{8,10},{9,11},{10,... | collective-permute-start | bytes 245768 | tf_op jit(solution)/shard_map/ppermute | solution.py:419
  117.5 8.0 %collective-permute-start.22 = (f32[16,1280]{1,0:T(8,128)S(1)}, f32[16,1280]{1,0:T(8,128)S(1)}, u32[]{:S(2)}, u32[]{:S(2)}) collective-permute-start(f32[16,1280]{1,0:T(8,128)S(1)} %get-tuple-element.48), channel_id=1, source_target_pairs={{0,1},{1,2},{2,3},{3,0},{4,5},{5,6},{6,7},{7,4},{8,9},{9,10},{10,1... | collective-permute-start | bytes 245768 | tf_op jit(solution)/shard_map/ppermute | solution.py:419
  125.6 6.4 %copy-start.2 = (bf16[16,1152]{1,0:T(8,128)(2,1)}, bf16[16,1152]{1,0:T(8,128)(2,1)S(1)}, u32[]{:S(2)}) copy-start(bf16[16,1152]{1,0:T(8,128)(2,1)S(1)} %shard_map.107.rest_0_) | copy-start | bytes 110596
  125.6 5.8 %collective-permute-start.23 = (bf16[16,1152]{1,0:T(8,128)(2,1)S(1)}, bf16[16,1152]{1,0:T(8,128)(2,1)S(1)}, u32[]{:S(2)}, u32[]{:S(2)}) collective-permute-start(bf16[16,1152]{1,0:T(8,128)(2,1)S(1)} %shard_map.107.rest_0_), channel_id=1, source_target_pairs={{0,1},{1,2},{2,3},{3,0},{4,5},{5,6},{6,7},{7,4},{8,9},{9,10},{10,1... | collective-permute-start | bytes 110600 | tf_op jit(solution)/shard_map/ppermute | solution.py:427
  125.7 5.8 %collective-permute-start.24 = (bf16[16,1152]{1,0:T(8,128)(2,1)S(1)}, bf16[16,1152]{1,0:T(8,128)(2,1)S(1)}, u32[]{:S(2)}, u32[]{:S(2)}) collective-permute-start(bf16[16,1152]{1,0:T(8,128)(2,1)S(1)} %shard_map.107.rest_0_), channel_id=1, source_target_pairs={{0,2},{1,3},{2,0},{3,1},{4,6},{5,7},{6,4},{7,5},{8,10},{9,11},{10,... | collective-permute-start | bytes 110600 | tf_op jit(solution)/shard_map/ppermute | solution.py:427
  127.5 4.4 %collective-permute-start.25 = (bf16[16,1152]{1,0:T(8,128)(2,1)S(1)}, bf16[16,1152]{1,0:T(8,128)(2,1)S(1)}, u32[]{:S(2)}, u32[]{:S(2)}) collective-permute-start(bf16[16,1152]{1,0:T(8,128)(2,1)S(1)} %shard_map.107.rest_0_), channel_id=1, source_target_pairs={{0,3},{1,0},{2,1},{3,2},{4,7},{5,4},{6,5},{7,6},{8,11},{9,8},{10,9... | collective-permute-start | bytes 110600 | tf_op jit(solution)/shard_map/ppermute | solution.py:427
  131.4 0.6 copy-start.6
  131.5 0.6 copy-start.8
  132.1 0.6 copy-start.10
  141.3 5.9 %collective-permute-start.26 = (bf16[16,1152]{1,0:T(8,128)(2,1)}, bf16[16,1152]{1,0:T(8,128)(2,1)S(1)}, u32[]{:S(2)}, u32[]{:S(2)}) collective-permute-start(bf16[16,1152]{1,0:T(8,128)(2,1)} %get-tuple-element.50), channel_id=1, source_target_pairs={{0,3},{1,0},{2,1},{3,2},{4,7},{5,4},{6,5},{7,6},{8,11},{9,8},{10,9... | collective-permute-start | bytes 110600 | tf_op jit(solution)/shard_map/ppermute | solution.py:419
  145.2 5.1 %collective-permute-start.27 = (bf16[16,1152]{1,0:T(8,128)(2,1)}, bf16[16,1152]{1,0:T(8,128)(2,1)S(1)}, u32[]{:S(2)}, u32[]{:S(2)}) collective-permute-start(bf16[16,1152]{1,0:T(8,128)(2,1)} %get-tuple-element.51), channel_id=1, source_target_pairs={{0,2},{1,3},{2,0},{3,1},{4,6},{5,7},{6,4},{7,5},{8,10},{9,11},{10,... | collective-permute-start | bytes 110600 | tf_op jit(solution)/shard_map/ppermute | solution.py:419
  145.2 6.0 %collective-permute-start.28 = (bf16[16,1152]{1,0:T(8,128)(2,1)}, bf16[16,1152]{1,0:T(8,128)(2,1)S(1)}, u32[]{:S(2)}, u32[]{:S(2)}) collective-permute-start(bf16[16,1152]{1,0:T(8,128)(2,1)} %get-tuple-element.52), channel_id=1, source_target_pairs={{0,1},{1,2},{2,3},{3,0},{4,5},{5,6},{6,7},{7,4},{8,9},{9,10},{10,1... | collective-permute-start | bytes 110600 | tf_op jit(solution)/shard_map/ppermute | solution.py:419
  151.2 0.8 copy-start.4
  152.2 9.2 %collective-permute-start.29 = (bf16[16,1024]{1,0:T(8,128)(2,1)S(1)}, bf16[16,1024]{1,0:T(8,128)(2,1)S(1)}, u32[]{:S(2)}, u32[]{:S(2)}) collective-permute-start(bf16[16,1024]{1,0:T(8,128)(2,1)S(1)} %shard_map.109.rest_0_), channel_id=1, source_target_pairs={{0,1},{1,2},{2,3},{3,0},{4,5},{5,6},{6,7},{7,4},{8,9},{9,10},{10,1... | collective-permute-start | bytes 98312 | tf_op jit(solution)/shard_map/ppermute | solution.py:427
  152.3 9.1 %collective-permute-start.30 = (bf16[16,1024]{1,0:T(8,128)(2,1)S(1)}, bf16[16,1024]{1,0:T(8,128)(2,1)S(1)}, u32[]{:S(2)}, u32[]{:S(2)}) collective-permute-start(bf16[16,1024]{1,0:T(8,128)(2,1)S(1)} %shard_map.109.rest_0_), channel_id=1, source_target_pairs={{0,2},{1,3},{2,0},{3,1},{4,6},{5,7},{6,4},{7,5},{8,10},{9,11},{10,... | collective-permute-start | bytes 98312 | tf_op jit(solution)/shard_map/ppermute | solution.py:427
  153.7 7.7 %collective-permute-start.31 = (bf16[16,1024]{1,0:T(8,128)(2,1)S(1)}, bf16[16,1024]{1,0:T(8,128)(2,1)S(1)}, u32[]{:S(2)}, u32[]{:S(2)}) collective-permute-start(bf16[16,1024]{1,0:T(8,128)(2,1)S(1)} %shard_map.109.rest_0_), channel_id=1, source_target_pairs={{0,3},{1,0},{2,1},{3,2},{4,7},{5,4},{6,5},{7,6},{8,11},{9,8},{10,9... | collective-permute-start | bytes 98312 | tf_op jit(solution)/shard_map/ppermute | solution.py:427
  156.6 20.5 %collective-permute-start.35 = (f32[4,4096]{1,0:T(4,128)S(1)}, f32[4,4096]{1,0:T(4,128)S(1)}, u32[]{:S(2)}, u32[]{:S(2)}) collective-permute-start(f32[4,4096]{1,0:T(4,128)S(1)} %get-tuple-element.57), channel_id=1, source_target_pairs={{0,16},{1,17},{2,18},{3,19},{4,20},{5,21},{6,22},{7,23},{8,24},{9,... | collective-permute-start | bytes 196616 | tf_op jit(solution)/shard_map/ppermute | solution.py:505
  175.9 2.2 %collective-permute-start.32 = (f32[4,4096]{1,0:T(4,128)S(1)}, f32[4,4096]{1,0:T(4,128)S(1)}, u32[]{:S(2)}, u32[]{:S(2)}) collective-permute-start(f32[4,4096]{1,0:T(4,128)S(1)} %get-tuple-element.54), channel_id=1, source_target_pairs={{0,12},{4,0},{8,4},{12,8},{1,13},{5,1},{9,5},{13,9},{2,14},{6,2},{... | collective-permute-start | bytes 196616 | tf_op jit(solution)/shard_map/ppermute | solution.py:419
  175.9 5.0 %collective-permute-start.33 = (f32[4,4096]{1,0:T(4,128)S(1)}, f32[4,4096]{1,0:T(4,128)S(1)}, u32[]{:S(2)}, u32[]{:S(2)}) collective-permute-start(f32[4,4096]{1,0:T(4,128)S(1)} %get-tuple-element.55), channel_id=1, source_target_pairs={{0,8},{4,12},{8,0},{12,4},{1,9},{5,13},{9,1},{13,5},{2,10},{6,14},... | collective-permute-start | bytes 196616 | tf_op jit(solution)/shard_map/ppermute | solution.py:419
  176.9 4.3 %collective-permute-start.34 = (f32[4,4096]{1,0:T(4,128)S(1)}, f32[4,4096]{1,0:T(4,128)S(1)}, u32[]{:S(2)}, u32[]{:S(2)}) collective-permute-start(f32[4,4096]{1,0:T(4,128)S(1)} %get-tuple-element.56), channel_id=1, source_target_pairs={{0,4},{4,8},{8,12},{12,0},{1,5},{5,9},{9,13},{13,1},{2,6},{6,10},{... | collective-permute-start | bytes 196616 | tf_op jit(solution)/shard_map/ppermute | solution.py:419

commit v2 on v1

--- a/solution.py
+++ b/solution.py
@@ -30,6 +30,10 @@
     return high, middle, rest - middle
 
 
+def block_depth(model):
+    return divisor(model, 256)
+
+
 def divisor(size, largest):
     best = LANES
     while best * 2 <= largest and size % (best * 2) == 0:
@@ -37,77 +41,128 @@
     return best
 
 
-def project_kernel(chunks, depth, fresh, me_ref, x_ref, aux_ref, w_ref, *rest):
-    outs, (xg_ref, sq_ref, acc_ref) = rest[:chunks], rest[chunks:]
-    k, step = pl.program_id(0), pl.program_id(1)
-    wide = xg_ref.shape[0] * depth
-
-    @pl.when(jnp.logical_and(k == 0, step == 0))
-    def _():
-        if fresh:
-            x = x_ref[...].astype(F32)
-            xg = (x * aux_ref[...].astype(F32)).astype(BF16)
-            squares = jnp.sum(x * x, axis=1, keepdims=True)
-        else:
-            turn = aux_ref[...]
-            xg = jnp.dot(turn, x_ref[:, :wide], preferred_element_type=F32).astype(BF16)
-            terms = jnp.dot(turn, x_ref[:, wide:], preferred_element_type=F32)
-            squares = terms[:, 0:1] + terms[:, 1:2] + terms[:, 2:3]
-        for i in range(xg_ref.shape[0]):
-            xg_ref[i] = xg[:, i * depth : (i + 1) * depth]
-        sq_ref[...] = jnp.broadcast_to(squares, sq_ref.shape)
-
-    part = jnp.dot(xg_ref[step], w_ref[...], preferred_element_type=F32)
-
-    @pl.when(step == 0)
-    def _():
-        acc_ref[...] = part
-
-    @pl.when(step > 0)
-    def _():
-        acc_ref[...] += part
-
-    width = acc_ref.shape[1]
-    for i in range(chunks):
-
-        @pl.when(jnp.logical_and(k == i, step == pl.num_programs(1) - 1))
-        def _():
-            outs[i][:, :width] = acc_ref[...]
-            outs[i][:, width:] = sq_ref[...]
-
-
-def project(x, aux, w, me, chunks, fresh):
+def hbm():
+    return pl.BlockSpec(memory_space=pltpu.HBM)
+
+
+def vmem():
+    return pl.BlockSpec(memory_space=pltpu.VMEM)
+
+
+def smem():
+    return pl.BlockSpec(memory_space=pltpu.SMEM)
+
+
+def row_copy(w_ref, first, index, depth, to_ref, sem_ref):
+    rows = pl.ds(pl.multiple_of((first + index) * depth, depth), depth)
+    return pltpu.make_async_copy(w_ref.at[0, rows], to_ref.at[index], sem_ref.at[index])
+
+
+def load_kernel(first, w_ref, after_ref, out_ref, sem_ref):
+    count, depth = out_ref.shape[:2]
+    for i in range(count):
+        row_copy(w_ref, first, i, depth, out_ref, sem_ref).start()
+    for i in range(count):
+        row_copy(w_ref, first, i, depth, out_ref, sem_ref).wait()
+
+
+def load(w, first, count, depth, after):
+    columns = w.shape[2]
+    return pl.pallas_call(
+        functools.partial(load_kernel, first),
+        out_shape=jax.ShapeDtypeStruct((count, depth, columns), BF16),
+        in_specs=[hbm(), pl.BlockSpec(memory_space=pl.ANY)],
+        out_specs=vmem(),
+        scratch_shapes=[pltpu.SemaphoreType.DMA((count,))],
+        compiler_params=params(26),
+        cost_estimate=pl.CostEstimate(
+            flops=0, bytes_accessed=2 * count * depth * columns, transcendentals=0
+        ),
+    )(w, after)
+
+
+def each_block(apply, held, w_ref, buffer_ref, sem_ref):
+    at = 0
+    for part_ref in held:
+
+        @pl.loop(0, part_ref.shape[0])
+        def _(i, part_ref=part_ref, at=at):
+            apply(at + i, part_ref[i])
+
+        at += part_ref.shape[0]
+    depth = buffer_ref.shape[1]
+
+    @pl.loop(0, buffer_ref.shape[0])
+    def _(i):
+        row_copy(w_ref, at, i, depth, buffer_ref, sem_ref).wait()
+        apply(at + i, buffer_ref[i])
+
+
+def start_blocks(held, w_ref, buffer_ref, sem_ref):
+    at = sum(part_ref.shape[0] for part_ref in held)
+    for i in range(buffer_ref.shape[0]):
+        row_copy(w_ref, at, i, buffer_ref.shape[1], buffer_ref, sem_ref).start()
+
+
+def project_kernel(chunks, parts, fresh, me_ref, x_ref, aux_ref, w_ref, *rest):
+    held, outs = rest[:parts], rest[parts : parts + chunks]
+    xg_ref, sq_ref, acc_ref, buffer_ref, sem_ref = rest[parts + chunks :]
+    start_blocks(held, w_ref, buffer_ref, sem_ref)
+    blocks, rows, depth = xg_ref.shape
+    wide = blocks * depth
+    width = acc_ref.shape[2]
+    if fresh:
+        x = x_ref[...].astype(F32)
+        xg = (x * aux_ref[...].astype(F32)).astype(BF16)
+        squares = jnp.sum(x * x, axis=1, keepdims=True)
+    else:
+        turn = aux_ref[...]
+        xg = jnp.dot(turn, x_ref[:, :wide], preferred_element_type=F32).astype(BF16)
+        terms = jnp.dot(turn, x_ref[:, wide:], preferred_element_type=F32)
+        squares = terms[:, 0:1] + terms[:, 1:2] + terms[:, 2:3]
+    for i in range(blocks):
+        xg_ref[i] = xg[:, i * depth : (i + 1) * depth]
+    sq_ref[...] = jnp.broadcast_to(squares, sq_ref.shape)
+    acc_ref[...] = jnp.zeros_like(acc_ref)
+
+    def apply(i, w):
+        part = jnp.dot(xg_ref[i], w, preferred_element_type=F32)
+        for k in range(chunks):
+            acc_ref[k] += part[:, k * width : (k + 1) * width]
+
+    each_block(apply, held, w_ref, buffer_ref, sem_ref)
+    me = me_ref[0]
+    for k in range(chunks):
+        outs[k][:, :width] = acc_ref[lax.rem(me - k + chunks, chunks)]
+        outs[k][:, width:] = sq_ref[...]
+
+
+def project(x, aux, w, held, me, chunks, fresh):
     rows = x.shape[0]
     model, columns = w.shape[1:]
     width = columns // chunks
-    depth = divisor(model, 1024)
+    depth = block_depth(model)
+    left = model // depth - sum(part.shape[0] for part in held)
     shape = jax.ShapeDtypeStruct((rows, width + LANES), F32)
     return pl.pallas_call(
-        functools.partial(project_kernel, chunks, depth, fresh),
+        functools.partial(project_kernel, chunks, len(held), fresh),
         out_shape=[shape] * chunks,
-        grid_spec=pltpu.PrefetchScalarGridSpec(
-            num_scalar_prefetch=1,
-            grid=(chunks, model // depth),
-            in_specs=[
-                whole(x.shape),
-                whole(aux.shape),
-                pl.BlockSpec(
-                    (None, depth, width),
-                    lambda k, i, me: (0, i, lax.rem(me[0] - k + chunks, chunks)),
-                ),
-            ],
-            out_specs=[whole(shape.shape)] * chunks,
-            scratch_shapes=[
-                pltpu.VMEM((model // depth, rows, depth), BF16),
-                pltpu.VMEM((rows, LANES), F32),
-                pltpu.VMEM((rows, width), F32),
-            ],
-        ),
-        compiler_params=params(24),
-        cost_estimate=pl.CostEstimate(
-            flops=2 * rows * model * columns, bytes_accessed=2 * model * columns, transcendentals=0
-        ),
-    )(me, x, aux, w)
+        in_specs=[smem(), vmem(), vmem(), hbm()] + [vmem()] * len(held),
+        out_specs=[vmem()] * chunks,
+        scratch_shapes=[
+            pltpu.VMEM((model // depth, rows, depth), BF16),
+            pltpu.VMEM((rows, LANES), F32),
+            pltpu.VMEM((chunks, rows, width), F32),
+            pltpu.VMEM((left, depth, columns), BF16),
+            pltpu.SemaphoreType.DMA((left,)),
+        ],
+        compiler_params=params(6 + (2 * left * depth * columns >> 20)),
+        cost_estimate=pl.CostEstimate(
+            flops=2 * rows * model * columns,
+            bytes_accessed=2 * left * depth * columns,
+            transcendentals=0,
+        ),
+    )(me, x, aux, w, *held)
 
 
 def normalize_kernel(model, *refs):
@@ -273,7 +328,7 @@
                 pltpu.VMEM((chunks, rows, width), BF16),
             ],
         ),
-        compiler_params=params(56),
+        compiler_params=params(20 if group * rows * total < 1 << 21 else 48),
         cost_estimate=pl.CostEstimate(
             flops=4 * heads * group * rows * total * hd,
             bytes_accessed=4 * heads * total * hd,
@@ -283,7 +338,7 @@
 
 
 def merge_kernel(hd, *refs):
-    parts, out_ref = refs[:-1], refs[-1]
+    parts, out_ref = refs[:-2], refs[-1]
     per = out_ref.shape[1] // hd
     stats = [ref[:, per * hd :].astype(F32) for ref in parts]
     for i in range(per):
@@ -300,90 +355,73 @@
         out_ref[:, i * hd : (i + 1) * hd] = mixed.astype(BF16)
 
 
-def merge(parts, hd):
+def merge(parts, hd, after):
     rows, width = parts[0].shape
     return pl.pallas_call(
         functools.partial(merge_kernel, hd),
         out_shape=jax.ShapeDtypeStruct((rows, width - LANES), BF16),
+        in_specs=[vmem()] * len(parts) + [pl.BlockSpec(memory_space=pl.ANY)],
         compiler_params=params(8),
         cost_estimate=pl.CostEstimate(
             flops=rows * width * 8, bytes_accessed=rows * width * 10, transcendentals=rows * LANES
         ),
-    )(*parts)
-
-
-def output_kernel(blocks, per, groups, me_ref, turn_ref, *rest):
-    parts = rest[:blocks]
-    w_ref = rest[blocks]
-    outs = rest[blocks + 1 : blocks + 1 + groups]
-    a_ref, acc_ref = rest[blocks + 1 + groups :]
-    step = pl.program_id(0)
+    )(*parts, after)
+
+
+def output_kernel(blocks, groups, parts, me_ref, turn_ref, w_ref, *rest):
+    mixed, held = rest[:blocks], rest[blocks : blocks + parts]
+    outs = rest[blocks + parts : blocks + parts + groups]
+    a_ref, acc_ref, buffer_ref, sem_ref = rest[blocks + parts + groups :]
+    start_blocks(held, w_ref, buffer_ref, sem_ref)
     depth = a_ref.shape[2]
-
-    @pl.when(step == 0)
-    def _():
-        for k in range(blocks):
-            turned = jnp.dot(turn_ref[...], parts[k][...], preferred_element_type=F32).astype(BF16)
-            for i in range(per):
-                a_ref[k * per + i] = turned[:, i * depth : (i + 1) * depth]
-
-    part = jnp.dot(a_ref[step], w_ref[...], preferred_element_type=F32)
-
-    @pl.when(step == 0)
-    def _():
-        acc_ref[...] = part
-
-    @pl.when(step > 0)
-    def _():
-        acc_ref[...] += part
-
-    @pl.when(step == pl.num_programs(0) - 1)
-    def _():
-        size = outs[0].shape[0]
-        stride = acc_ref.shape[0] // groups
-        for k in range(groups):
-            outs[k][...] = acc_ref[k * stride : k * stride + size, :]
-
-
-def output(parts, turn, w, me, groups, size):
-    blocks = len(parts)
-    rows, width = parts[0].shape
-    columns = w.shape[2]
-    depth = divisor(width, 512)
-    per = width // depth
+    per = mixed[0].shape[1] // depth
+    me = me_ref[0]
+    for k in range(blocks):
+        turned = jnp.dot(turn_ref[...], mixed[k][...], preferred_element_type=F32).astype(BF16)
+        at = lax.rem(me - k + blocks, blocks) * per
+        for i in range(per):
+            a_ref[at + i] = turned[:, i * depth : (i + 1) * depth]
+    acc_ref[...] = jnp.zeros_like(acc_ref)
+
+    def apply(i, w):
+        acc_ref[...] += jnp.dot(a_ref[i], w, preferred_element_type=F32)
+
+    each_block(apply, held, w_ref, buffer_ref, sem_ref)
+    size = outs[0].shape[0]
+    stride = acc_ref.shape[0] // groups
+    for k in range(groups):
+        outs[k][...] = acc_ref[k * stride : k * stride + size, :]
+
+
+def output(mixed, turn, w, held, me, groups, size, depth):
+    blocks = len(mixed)
+    rows = mixed[0].shape[0]
+    model, columns = w.shape[1:]
+    left = model // depth - sum(part.shape[0] for part in held)
     padded = turn.shape[0]
     shape = jax.ShapeDtypeStruct((size, columns), F32)
     return pl.pallas_call(
-        functools.partial(output_kernel, blocks, per, groups),
+        functools.partial(output_kernel, blocks, groups, len(held)),
         out_shape=[shape] * groups,
-        grid_spec=pltpu.PrefetchScalarGridSpec(
-            num_scalar_prefetch=1,
-            grid=(blocks * per,),
-            in_specs=[whole(turn.shape)]
-            + [whole(part.shape) for part in parts]
-            + [
-                pl.BlockSpec(
-                    (None, depth, columns),
-                    lambda i, me: (0, lax.rem(me[0] - i // per + blocks, blocks) * per + i % per, 0),
-                )
-            ],
-            out_specs=[whole(shape.shape)] * groups,
-            scratch_shapes=[
-                pltpu.VMEM((blocks * per, padded, depth), BF16),
-                pltpu.VMEM((padded, columns), F32),
-            ],
-        ),
-        compiler_params=params(24),
-        cost_estimate=pl.CostEstimate(
-            flops=2 * rows * blocks * width * columns,
-            bytes_accessed=2 * blocks * width * columns,
+        in_specs=[smem(), vmem(), hbm()] + [vmem()] * (blocks + len(held)),
+        out_specs=[vmem()] * groups,
+        scratch_shapes=[
+            pltpu.VMEM((model // depth, padded, depth), BF16),
+            pltpu.VMEM((padded, columns), F32),
+            pltpu.VMEM((left, depth, columns), BF16),
+            pltpu.SemaphoreType.DMA((left,)),
+        ],
+        compiler_params=params(6 + (2 * left * depth * columns >> 20)),
+        cost_estimate=pl.CostEstimate(
+            flops=2 * rows * model * columns,
+            bytes_accessed=2 * left * depth * columns,
             transcendentals=0,
         ),
-    )(me, turn, *parts, w)
+    )(me, turn, w, *mixed, *held)
 
 
 def add_kernel(*refs):
-    parts, gain_ref, y_ref, out_ref = refs[:-3], refs[-3], refs[-2], refs[-1]
+    parts, (gain_ref, _, y_ref, out_ref) = refs[:-4], refs[-4:]
     total = parts[0][...]
     for ref in parts[1:]:
         total = total + ref[...]
@@ -398,7 +436,7 @@
     out_ref[:, wide:] = terms.astype(BF16)
 
 
-def add_up(parts, gain):
+def add_up(parts, gain, after):
     rows, width = parts[0].shape
     return pl.pallas_call(
         add_kernel,
@@ -406,11 +444,12 @@
             jax.ShapeDtypeStruct((rows, width), F32),
             jax.ShapeDtypeStruct((rows, width + LANES), BF16),
         ],
+        in_specs=[vmem()] * (len(parts) + 1) + [pl.BlockSpec(memory_space=pl.ANY)],
         compiler_params=params(8),
         cost_estimate=pl.CostEstimate(
             flops=rows * width * 8, bytes_accessed=rows * width * 24, transcendentals=0
         ),
-    )(*parts, gain)
+    )(*parts, gain, after)
 
 
 def back(parts, axis):
@@ -477,21 +516,31 @@
 
     x, aux = tokens_in.reshape(rows, columns), gain
     result = None
+    in_depth, out_depth = block_depth(columns), divisor(w_out.shape[1] // ctx, 256)
+    in_blocks, out_blocks = columns // in_depth, w_out.shape[1] // out_depth
+    ready = []
     for layer in range(sections):
         fresh = layer == 0
         if even:
-            parts = back(project(x, aux, w_qkv, me, ctx, fresh), "ctx")
+            sent = project(x, aux, w_qkv, ready, me, ctx, fresh)
+            parts = back(sent, "ctx")
             parts = around(normalize(parts, model), "ctx")
         else:
-            part = project(x, aux, w_qkv, zero, 1, fresh)[0]
+            part = project(x, aux, w_qkv, ready, zero, 1, fresh)[0]
             parts = [normalize([lax.psum(part, "ctx")], model)]
-        parts = attend(
+        sent = attend(
             parts, prefix_keys, prefix_values, suffix_keys, suffix_values,
             me, order, lengths, ctx, group,
         )
-        parts = around(merge(back(parts, "ctx"), hd), "ctx")
-        parts = back(output(parts, turn, w_out, me, tp, size), "tp")
-        y, message = add_up(parts + [residual], next_gain)
+        first = load(w_out, 0, out_blocks * 5 // 16, out_depth, sent[0])
+        mixed = merge(back(sent, "ctx"), hd, first)
+        second = load(w_out, first.shape[0], out_blocks * 5 // 16, out_depth, mixed)
+        parts = around(mixed, "ctx")
+        sent = output(parts, turn, w_out, [first, second], me, tp, size, out_depth)
+        first = sent[0]
+        if layer + 1 < sections:
+            first = load(w_qkv, 0, in_blocks * 5 // 16, in_depth, sent[0])
+        y, message = add_up(back(sent, "tp") + [residual], next_gain, first)
         result = y if result is None else jnp.where(section == layer, y, result)
         if layer + 1 < sections:
             here, there = layer * tp, (layer + 1) * tp
@@ -501,6 +550,8 @@
                 )
                 for k in range(tp)
             ]
+            second = load(w_qkv, first.shape[0], in_blocks * 5 // 16, in_depth, y)
+            ready = [first, second]
             x, aux = jnp.concatenate(received, axis=0), unturn
             residual = lax.ppermute(y, "section", [(layer, layer + 1)])
     return result.reshape(1, steps, share, columns)

time: 184 us -> 158 us (0.86)
  waiting for transfers between devices: 39.4 us -> 22.2 us
  Pallas kernels: 86 us -> 78 us
    ppermute x18, waiting for transfers between devices: 31 us -> 19 us  [back(): lax.ppermute(parts[k], axis, [(i, (i - k) % count) for i in range(count)])]
    pallas_call x2, Pallas kernels: 17.3 us -> 11.9 us  [attend(): pl.pallas_call(functools.partial(attend_kernel, len(parts), chunks, order...]
    pallas_call x4 -> x10, Pallas kernels: 67.1 us -> 63.1 us  [the longest x6 25.4 us: load(): pl.pallas_call(functools.partial(load_kernel, first), out_shape=jax.Shape...]
    ppermute x12, waiting for transfers between devices: 6.81 us -> 3.23 us  [around(): lax.ppermute(part, axis, [(i, (i + k) % count) for i in range(count)])]
    ppermute x1, starting transfers between devices: 4.8 us -> 1.28 us  [on_device(): residual = lax.ppermute(y, 'section', [(layer, layer + 1)])]
    unnamed x22 -> x18, local copies, waits for them, and re-layouts: 3.77 us -> 2.52 us
  transfers between devices with their start and end apart: 36 -> 36, of which waited for: 24 -> 15; matrix products, arithmetic and copies ran while one was open for 1% -> 2% of each run, Pallas kernels for 21% -> 31%
where the time goes in v2:
time: 158 us
  Pallas kernels  78 us (49%)
  starting transfers between devices  50.9 us (32%)
  waiting for transfers between devices  22.2 us (14%)
  local copies, waits for them, and re-layouts  4.1 us (3%)
  other arithmetic  2.25 us (1%)
    pallas_call x6, Pallas kernels, load(): pl.pallas_call(functools.partial(load_kernel, first), out_shape=jax.Shape...  25.4 us
    ppermute x18, starting transfers between devices, back(): lax.ppermute(parts[k], axis, [(i, (i - k) % count) for i in range(count)])  21.4 us
    pallas_call x2, Pallas kernels, project(): pl.pallas_call(functools.partial(project_kernel, chunks, len(held), fresh...  21.2 us
    ppermute x18, waiting for transfers between devices, back(): lax.ppermute(parts[k], axis, [(i, (i - k) % count) for i in range(count)])  19 us
    ppermute x12, starting transfers between devices, around(): lax.ppermute(part, axis, [(i, (i + k) % count) for i in range(count)])  18.5 us
    pallas_call x2, Pallas kernels, output(): pl.pallas_call(functools.partial(output_kernel, blocks, groups, len(held)...  16.5 us
    pallas_call x2, Pallas kernels, attend(): pl.pallas_call(functools.partial(attend_kernel, len(parts), chunks, order...  11.9 us
    ppermute x4, starting transfers between devices, on_device(): lax.ppermute(message, ('section', 'tp'), [(here + n, there + (n + k) % tp...  8.28 us
  transfers between devices with their start and end apart: 36, of which 15 were waited for; matrix products, arithmetic and copies ran while one was open for 2% of the time, Pallas kernels for 31%

profile of v2, /device:TPU:0, one launch (start us, length us, event | category | flops | bytes accessed | tf_op | source)
XLA Modules:
  0.0 157.9 jit_solution(1132838240140849752)
XLA Ops:
  0.0 0.9 copy-done.5
  0.9 14.0 %shard_map.100 = (f32[16,1280]{1,0:T(8,128)S(1)}, f32[16,1280]{1,0:T(8,128)}, f32[16,1280]{1,0:T(8,128)}, f32[16,1280]{1,0:T(8,128)}) custom-call(s32[1]{0:T(128)} %bitcast.me_ref, bf16[16,4096]{1,0:T(8,128)(2,1)S(1)} %bitcast.2, bf16[1,4096]{1,0:T(2,128)(2,1)} %aux_ref.1, bf16[1,4096,4608]{2,1,0:T(8,128)(2,1)} %w_ref.16), custom_call_target="tpu_custom_call" | custom-call | flops 603979776 | bytes 37748736 | tf_op jit(solution)/shard_map/pallas_call | solution.py:147
  15.0 5.1 %collective-permute-start = (f32[16,1280]{1,0:T(8,128)}, f32[16,1280]{1,0:T(8,128)S(1)}, u32[]{:S(2)}, u32[]{:S(2)}) collective-permute-start(f32[16,1280]{1,0:T(8,128)} %get-tuple-element.33), channel_id=1, source_target_pairs={{0,3},{1,0},{2,1},{3,2},{4,7},{5,4},{6,5},{7,6},{8,11},{9,8},{10,9... | collective-permute-start | bytes 245768 | tf_op jit(solution)/shard_map/ppermute | solution.py:458
  20.1 1.0 collective-permute-start.2
  21.1 1.5 collective-permute-start.15
  23.2 4.6 %collective-permute-done.1.refs_2_ = f32[16,1280]{1,0:T(8,128)S(1)} collective-permute-done((f32[16,1280]{1,0:T(8,128)}, f32[16,1280]{1,0:T(8,128)S(1)}, u32[]{:S(2)}, u32[]{:S(2)}) %collective-permute-start.1) | collective-permute-done | bytes 81952 | tf_op jit(solution)/shard_map/ppermute | solution.py:458
  28.2 2.4 %collective-permute-start.4 = (bf16[16,1152]{1,0:T(8,128)(2,1)S(1)}, bf16[16,1152]{1,0:T(8,128)(2,1)S(1)}, u32[]{:S(2)}, u32[]{:S(2)}) collective-permute-start(bf16[16,1152]{1,0:T(8,128)(2,1)S(1)} %shard_map.101.rest_0_), channel_id=1, source_target_pairs={{0,2},{1,3},{2,0},{3,1},{4,6},{5,7},{6,4},{7,5},{8,10},{9,11},{10,... | collective-permute-start | bytes 110600 | tf_op jit(solution)/shard_map/ppermute | solution.py:466
  30.6 2.3 %collective-permute-start.5 = (bf16[16,1152]{1,0:T(8,128)(2,1)S(1)}, bf16[16,1152]{1,0:T(8,128)(2,1)S(1)}, u32[]{:S(2)}, u32[]{:S(2)}) collective-permute-start(bf16[16,1152]{1,0:T(8,128)(2,1)S(1)} %shard_map.101.rest_0_), channel_id=1, source_target_pairs={{0,3},{1,0},{2,1},{3,2},{4,7},{5,4},{6,5},{7,6},{8,11},{9,8},{10,9... | collective-permute-start | bytes 110600 | tf_op jit(solution)/shard_map/ppermute | solution.py:466
  32.9 1.6 dynamic-slice_convert_fusion
  34.6 1.6 %copy-done.1 = bf16[1,2,4096,128]{3,2,1,0:T(8,128)(2,1)S(1)} copy-done((bf16[1,2,4096,128]{3,2,1,0:T(8,128)(2,1)S(1)}, bf16[1,2,4096,128]{3,2,1,0:T(8,128)(2,1)}, u32[]{:S(2)}) %copy-start.1) | copy-done | bytes 2097176
  36.2 6.0 %shard_map.102 = (bf16[16,1152]{1,0:T(8,128)(2,1)S(1)}, bf16[16,1152]{1,0:T(8,128)(2,1)S(1)}, bf16[16,1152]{1,0:T(8,128)(2,1)S(1)}, bf16[16,1152]{1,0:T(8,128)(2,1)S(1)}) custom-call(s32[1]{0:T(128)} %bitcast.me_ref, s32[8]{0:T(128)S(1)} %copy-done.6, s32[8]{0:T(128)S(1)} %copy-done.7, bf16[16,1152]{1,0:T(8,128)(2,1)S(1)} %shard_map.101.rest_0_, ...), custom_call_target="tpu_custom_call" | custom-call | flops 1375731712 | bytes 5373952 | tf_op jit(solution)/shard_map/pallas_call | solution.py:317
  42.2 4.2 %collective-permute-start.6 = (bf16[16,1152]{1,0:T(8,128)(2,1)S(1)}, bf16[16,1152]{1,0:T(8,128)(2,1)S(1)}, u32[]{:S(2)}, u32[]{:S(2)}) collective-permute-start(bf16[16,1152]{1,0:T(8,128)(2,1)S(1)} %get-tuple-element.37), channel_id=1, source_target_pairs={{0,3},{1,0},{2,1},{3,2},{4,7},{5,4},{6,5},{7,6},{8,11},{9,8},{10,9... | collective-permute-start | bytes 110600 | tf_op jit(solution)/shard_map/ppermute | solution.py:458
  47.0 4.1 %shard_map.103.refs_4_.rest_4_ = bf16[5,256,4096]{2,1,0:T(8,128)(2,1)S(1)} custom-call(bf16[1,4096,4096]{2,1,0:T(8,128)(2,1)} %w_ref.19, bf16[16,1152]{1,0:T(8,128)(2,1)S(1)} %get-tuple-element.36.after_ref.refs_0_), custom_call_target="tpu_custom_call" | custom-call | bytes 10485760 | tf_op jit(solution)/shard_map/pallas_call | solution.py:71
  51.2 0.9 collective-permute-done.8.refs_3_
  52.3 1.4 collective-permute-start.10
  53.7 2.9 %collective-permute-start.11 = (bf16[16,1024]{1,0:T(8,128)(2,1)S(1)}, bf16[16,1024]{1,0:T(8,128)(2,1)S(1)}, u32[]{:S(2)}, u32[]{:S(2)}) collective-permute-start(bf16[16,1024]{1,0:T(8,128)(2,1)S(1)} %shard_map.104.after_ref.rest_0_), channel_id=1, source_target_pairs={{0,3},{1,0},{2,1},{3,2},{4,7},{5,4},{6,5},{7,6},{8,11},{9,8},{10,9... | collective-permute-start | bytes 98312 | tf_op jit(solution)/shard_map/ppermute | solution.py:466
  56.7 4.1 %shard_map.105.rest_5_ = bf16[5,256,4096]{2,1,0:T(8,128)(2,1)S(1)} custom-call(bf16[1,4096,4096]{2,1,0:T(8,128)(2,1)} %w_ref.19, bf16[16,1024]{1,0:T(8,128)(2,1)S(1)} %shard_map.104.after_ref.rest_0_), custom_call_target="tpu_custom_call" | custom-call | bytes 10485760 | tf_op jit(solution)/shard_map/pallas_call | solution.py:71
  60.9 1.5 collective-permute-done.9.rest_1_
  62.4 8.6 %shard_map.106 = (f32[4,4096]{1,0:T(4,128)S(1)}, f32[4,4096]{1,0:T(4,128)}, f32[4,4096]{1,0:T(4,128)}, f32[4,4096]{1,0:T(4,128)S(1)}) custom-call(s32[1]{0:T(128)} %bitcast.me_ref, bf16[32,16]{1,0:T(8,128)(2,1)S(1)} %fusion.turn_ref, bf16[1,4096,4096]{2,1,0:T(8,128)(2,1)} %w_ref.19, bf16[16,1024]{1,0:T(8,128)(2,1)S(1)} %shard_map.104.after_ref.rest_0_, ...), custom_call_target="tpu_custom_call" | custom-call | flops 536870912 | bytes 12582912 | tf_op jit(solution)/shard_map/pallas_call | solution.py:403
  71.0 1.6 %collective-permute-start.13 = (f32[4,4096]{1,0:T(4,128)}, f32[4,4096]{1,0:T(4,128)S(1)}, u32[]{:S(2)}, u32[]{:S(2)}) collective-permute-start(f32[4,4096]{1,0:T(4,128)} %get-tuple-element.42), channel_id=1, source_target_pairs={{0,8},{4,12},{8,0},{12,4},{1,9},{5,13},{9,1},{13,5},{2,10},{6,14},... | collective-permute-start | bytes 196616 | tf_op jit(solution)/shard_map/ppermute | solution.py:458
  73.3 0.9 reshape.138.refs_4_
  74.2 4.5 %shard_map.107.refs_6_.rest_0_ = bf16[5,256,4608]{2,1,0:T(8,128)(2,1)S(1)} custom-call(bf16[1,4096,4608]{2,1,0:T(8,128)(2,1)} %w_ref.16, f32[4,4096]{1,0:T(4,128)S(1)} %get-tuple-element.40.after_ref.refs_0_), custom_call_target="tpu_custom_call" | custom-call | bytes 11796480 | tf_op jit(solution)/shard_map/pallas_call | solution.py:71
  78.7 0.9 shard_map.108
  79.6 3.4 %collective-permute-start.16 = (bf16[4,4224]{1,0:T(4,128)(2,1)S(1)}, bf16[4,4224]{1,0:T(4,128)(2,1)S(1)}, u32[]{:S(2)}, u32[]{:S(2)}) collective-permute-start(bf16[4,4224]{1,0:T(4,128)(2,1)S(1)} %get-tuple-element.44), channel_id=1, source_target_pairs={{0,16},{4,20},{8,24},{12,28},{1,17},{5,21},{9,25},{13,29},{2,18},{... | collective-permute-start | bytes 101384 | tf_op jit(solution)/shard_map/ppermute | solution.py:548
  83.0 1.4 collective-permute-start.17
  84.3 1.3 collective-permute-start.18
  85.6 2.2 %collective-permute-start.19 = (bf16[4,4224]{1,0:T(4,128)(2,1)S(1)}, bf16[4,4224]{1,0:T(4,128)(2,1)S(1)}, u32[]{:S(2)}, u32[]{:S(2)}) collective-permute-start(bf16[4,4224]{1,0:T(4,128)(2,1)S(1)} %get-tuple-element.44), channel_id=1, source_target_pairs={{0,28},{4,16},{8,20},{12,24},{1,29},{5,17},{9,21},{13,25},{2,30},{... | collective-permute-start | bytes 101384 | tf_op jit(solution)/shard_map/ppermute | solution.py:548
  87.9 4.5 %shard_map.109.rest_1_ = bf16[5,256,4608]{2,1,0:T(8,128)(2,1)S(1)} custom-call(bf16[1,4096,4608]{2,1,0:T(8,128)(2,1)} %w_ref.16, f32[4,4096]{1,0:T(4,128)S(1)} %get-tuple-element.45.after_ref), custom_call_target="tpu_custom_call" | custom-call | bytes 11796480 | tf_op jit(solution)/shard_map/pallas_call | solution.py:71
  92.6 7.2 %shard_map.110 = (f32[16,1280]{1,0:T(8,128)S(1)}, f32[16,1280]{1,0:T(8,128)S(1)}, f32[16,1280]{1,0:T(8,128)S(1)}, f32[16,1280]{1,0:T(8,128)S(1)}) custom-call(s32[1]{0:T(128)} %bitcast.me_ref, bf16[16,4224]{1,0:T(8,128)(2,1)S(1)} %pad_maximum_fusion.x_ref, bf16[16,16]{1,0:T(8,128)(2,1)S(1)} %fusion.1.aux_ref, bf16[1,4096,4608]{2,1,0:T(8,128)(2,1)} %w_ref.16, ...), custom_call_target="tpu_custom_call" | custom-call | flops 603979776 | bytes 14155776 | tf_op jit(solution)/shard_map/pallas_call | solution.py:147
  99.7 2.4 %collective-permute-start.20 = (f32[16,1280]{1,0:T(8,128)S(1)}, f32[16,1280]{1,0:T(8,128)S(1)}, u32[]{:S(2)}, u32[]{:S(2)}) collective-permute-start(f32[16,1280]{1,0:T(8,128)S(1)} %get-tuple-element.47), channel_id=1, source_target_pairs={{0,3},{1,0},{2,1},{3,2},{4,7},{5,4},{6,5},{7,6},{8,11},{9,8},{10,9... | collective-permute-start | bytes 245768 | tf_op jit(solution)/shard_map/ppermute | solution.py:458
  102.8 2.2 %collective-permute-done.20.refs_1_ = f32[16,1280]{1,0:T(8,128)S(1)} collective-permute-done((f32[16,1280]{1,0:T(8,128)S(1)}, f32[16,1280]{1,0:T(8,128)S(1)}, u32[]{:S(2)}, u32[]{:S(2)}) %collective-permute-start.20) | collective-permute-done | bytes 81952 | tf_op jit(solution)/shard_map/ppermute | solution.py:458
  105.0 5.1 %collective-permute-done.21.refs_2_ = f32[16,1280]{1,0:T(8,128)S(1)} collective-permute-done((f32[16,1280]{1,0:T(8,128)S(1)}, f32[16,1280]{1,0:T(8,128)S(1)}, u32[]{:S(2)}, u32[]{:S(2)}) %collective-permute-start.21) | collective-permute-done | bytes 81952 | tf_op jit(solution)/shard_map/ppermute | solution.py:458
  110.2 2.3 %collective-permute-start.24 = (bf16[16,1152]{1,0:T(8,128)(2,1)S(1)}, bf16[16,1152]{1,0:T(8,128)(2,1)S(1)}, u32[]{:S(2)}, u32[]{:S(2)}) collective-permute-start(bf16[16,1152]{1,0:T(8,128)(2,1)S(1)} %shard_map.111.rest_0_), channel_id=1, source_target_pairs={{0,2},{1,3},{2,0},{3,1},{4,6},{5,7},{6,4},{7,5},{8,10},{9,11},{10,... | collective-permute-start | bytes 110600 | tf_op jit(solution)/shard_map/ppermute | solution.py:466
  112.5 2.4 %collective-permute-start.25 = (bf16[16,1152]{1,0:T(8,128)(2,1)S(1)}, bf16[16,1152]{1,0:T(8,128)(2,1)S(1)}, u32[]{:S(2)}, u32[]{:S(2)}) collective-permute-start(bf16[16,1152]{1,0:T(8,128)(2,1)S(1)} %shard_map.111.rest_0_), channel_id=1, source_target_pairs={{0,3},{1,0},{2,1},{3,2},{4,7},{5,4},{6,5},{7,6},{8,11},{9,8},{10,9... | collective-permute-start | bytes 110600 | tf_op jit(solution)/shard_map/ppermute | solution.py:466
  114.9 1.3 collective-permute-done.23.rest_1_
  116.6 6.0 %shard_map.112 = (bf16[16,1152]{1,0:T(8,128)(2,1)S(1)}, bf16[16,1152]{1,0:T(8,128)(2,1)S(1)}, bf16[16,1152]{1,0:T(8,128)(2,1)S(1)}, bf16[16,1152]{1,0:T(8,128)(2,1)S(1)}) custom-call(s32[1]{0:T(128)} %bitcast.me_ref, s32[8]{0:T(128)S(1)} %copy-done.6, s32[8]{0:T(128)S(1)} %copy-done.7, bf16[16,1152]{1,0:T(8,128)(2,1)S(1)} %shard_map.111.rest_0_, ...), custom_call_target="tpu_custom_call" | custom-call | flops 1375731712 | bytes 5373952 | tf_op jit(solution)/shard_map/pallas_call | solution.py:317
  122.6 4.2 %collective-permute-start.26 = (bf16[16,1152]{1,0:T(8,128)(2,1)S(1)}, bf16[16,1152]{1,0:T(8,128)(2,1)S(1)}, u32[]{:S(2)}, u32[]{:S(2)}) collective-permute-start(bf16[16,1152]{1,0:T(8,128)(2,1)S(1)} %get-tuple-element.51), channel_id=1, source_target_pairs={{0,3},{1,0},{2,1},{3,2},{4,7},{5,4},{6,5},{7,6},{8,11},{9,8},{10,9... | collective-permute-start | bytes 110600 | tf_op jit(solution)/shard_map/ppermute | solution.py:458
  127.4 4.1 %shard_map.113.refs_4_.rest_4_ = bf16[5,256,4096]{2,1,0:T(8,128)(2,1)S(1)} custom-call(bf16[1,4096,4096]{2,1,0:T(8,128)(2,1)} %w_ref.19, bf16[16,1152]{1,0:T(8,128)(2,1)S(1)} %get-tuple-element.50.after_ref.refs_0_), custom_call_target="tpu_custom_call" | custom-call | bytes 10485760 | tf_op jit(solution)/shard_map/pallas_call | solution.py:71
  131.6 0.9 collective-permute-done.28.refs_3_
  132.7 1.9 %collective-permute-start.29 = (bf16[16,1024]{1,0:T(8,128)(2,1)S(1)}, bf16[16,1024]{1,0:T(8,128)(2,1)S(1)}, u32[]{:S(2)}, u32[]{:S(2)}) collective-permute-start(bf16[16,1024]{1,0:T(8,128)(2,1)S(1)} %shard_map.114.after_ref.rest_0_), channel_id=1, source_target_pairs={{0,1},{1,2},{2,3},{3,0},{4,5},{5,6},{6,7},{7,4},{8,9},{9,10},{10,1... | collective-permute-start | bytes 98312 | tf_op jit(solution)/shard_map/ppermute | solution.py:466
  134.7 0.9 collective-permute-start.30
  135.6 1.5 collective-permute-start.31
  137.1 1.3 collective-permute-start.35
  138.4 4.1 %shard_map.115.rest_5_ = bf16[5,256,4096]{2,1,0:T(8,128)(2,1)S(1)} custom-call(bf16[1,4096,4096]{2,1,0:T(8,128)(2,1)} %w_ref.19, bf16[16,1024]{1,0:T(8,128)(2,1)S(1)} %shard_map.114.after_ref.rest_0_), custom_call_target="tpu_custom_call" | custom-call | bytes 10485760 | tf_op jit(solution)/shard_map/pallas_call | solution.py:71
  142.5 7.9 %shard_map.116 = (f32[4,4096]{1,0:T(4,128)S(1)}, f32[4,4096]{1,0:T(4,128)S(1)}, f32[4,4096]{1,0:T(4,128)S(1)}, f32[4,4096]{1,0:T(4,128)S(1)}) custom-call(s32[1]{0:T(128)} %bitcast.me_ref, bf16[32,16]{1,0:T(8,128)(2,1)S(1)} %fusion.turn_ref, bf16[1,4096,4096]{2,1,0:T(8,128)(2,1)} %w_ref.19, bf16[16,1024]{1,0:T(8,128)(2,1)S(1)} %shard_map.114.after_ref.rest_0_, ...), custom_call_target="tpu_custom_call" | custom-call | flops 536870912 | bytes 12582912 | tf_op jit(solution)/shard_map/pallas_call | solution.py:403
  151.3 1.6 collective-permute-done.32.refs_1_
  152.9 2.6 %collective-permute-done.33.refs_2_ = f32[4,4096]{1,0:T(4,128)S(1)} collective-permute-done((f32[4,4096]{1,0:T(4,128)S(1)}, f32[4,4096]{1,0:T(4,128)S(1)}, u32[]{:S(2)}, u32[]{:S(2)}) %collective-permute-start.33) | collective-permute-done | bytes 65568 | tf_op jit(solution)/shard_map/ppermute | solution.py:458
  155.7 1.5 shard_map.117
  (69 shorter events, 7.0 us)
Async XLA Ops:
  0.0 0.9 copy-start.5
  0.9 33.7 %copy-start = (bf16[1,2,4096,128]{3,2,1,0:T(8,128)(2,1)S(1)}, bf16[1,2,4096,128]{3,2,1,0:T(8,128)(2,1)}, u32[]{:S(2)}) copy-start(bf16[1,2,4096,128]{3,2,1,0:T(8,128)(2,1)} %rest_4_.3) | copy-start | bytes 6291460
  0.9 33.7 %copy-start.3 = (bf16[1,2,2,512,128]{4,3,2,1,0:T(8,128)(2,1)S(1)}, bf16[1,2,2,512,128]{4,3,2,1,0:T(8,128)(2,1)}, u32[]{:S(2)}) copy-start(bf16[1,2,2,512,128]{4,3,2,1,0:T(8,128)(2,1)} %rest_6_.3) | copy-start | bytes 1572868
  0.9 33.7 %copy-start.4 = (bf16[1,2,2,512,128]{4,3,2,1,0:T(8,128)(2,1)S(1)}, bf16[1,2,2,512,128]{4,3,2,1,0:T(8,128)(2,1)}, u32[]{:S(2)}) copy-start(bf16[1,2,2,512,128]{4,3,2,1,0:T(8,128)(2,1)} %rest_7_.3) | copy-start | bytes 1572868
  0.9 33.7 %copy-start.6 = (s32[8]{0:T(128)S(1)}, s32[8]{0:T(128)}, u32[]{:S(2)}) copy-start(s32[8]{0:T(128)} %order_ref.3) | copy-start | bytes 100
  0.9 33.7 %copy-start.7 = (s32[8]{0:T(128)S(1)}, s32[8]{0:T(128)}, u32[]{:S(2)}) copy-start(s32[8]{0:T(128)} %lengths_ref.3) | copy-start | bytes 100
  15.0 8.3 %collective-permute-start = (f32[16,1280]{1,0:T(8,128)}, f32[16,1280]{1,0:T(8,128)S(1)}, u32[]{:S(2)}, u32[]{:S(2)}) collective-permute-start(f32[16,1280]{1,0:T(8,128)} %get-tuple-element.33), channel_id=1, source_target_pairs={{0,3},{1,0},{2,1},{3,2},{4,7},{5,4},{6,5},{7,6},{8,11},{9,8},{10,9... | collective-permute-start | bytes 245768 | tf_op jit(solution)/shard_map/ppermute | solution.py:458
  20.1 7.7 %collective-permute-start.1 = (f32[16,1280]{1,0:T(8,128)}, f32[16,1280]{1,0:T(8,128)S(1)}, u32[]{:S(2)}, u32[]{:S(2)}) collective-permute-start(f32[16,1280]{1,0:T(8,128)} %get-tuple-element.34), channel_id=1, source_target_pairs={{0,2},{1,3},{2,0},{3,1},{4,6},{5,7},{6,4},{7,5},{8,10},{9,11},{10,... | collective-permute-start | bytes 245768 | tf_op jit(solution)/shard_map/ppermute | solution.py:458
  20.1 7.7 %collective-permute-start.2 = (f32[16,1280]{1,0:T(8,128)}, f32[16,1280]{1,0:T(8,128)S(1)}, u32[]{:S(2)}, u32[]{:S(2)}) collective-permute-start(f32[16,1280]{1,0:T(8,128)} %get-tuple-element.35), channel_id=1, source_target_pairs={{0,1},{1,2},{2,3},{3,0},{4,5},{5,6},{6,7},{7,4},{8,9},{9,10},{10,1... | collective-permute-start | bytes 245768 | tf_op jit(solution)/shard_map/ppermute | solution.py:458
  21.1 57.6 %collective-permute-start.15 = (bf16[1,4096]{1,0:T(2,128)(2,1)}, bf16[1,4096]{1,0:T(2,128)(2,1)}, u32[]{:S(2)}, u32[]{:S(2)}) collective-permute-start(bf16[1,4096]{1,0:T(2,128)(2,1)} %aux_ref.1), channel_id=1, source_target_pairs={{0,16},{16,0},{1,17},{17,1},{2,18},{18,2},{3,19},{19,3},{4,20},{20... | collective-permute-start | bytes 24584 | tf_op jit(solution)/shard_map/ppermute | solution.py:513
  27.9 6.6 %collective-permute-start.3 = (bf16[16,1152]{1,0:T(8,128)(2,1)S(1)}, bf16[16,1152]{1,0:T(8,128)(2,1)S(1)}, u32[]{:S(2)}, u32[]{:S(2)}) collective-permute-start(bf16[16,1152]{1,0:T(8,128)(2,1)S(1)} %shard_map.101.rest_0_), channel_id=1, source_target_pairs={{0,1},{1,2},{2,3},{3,0},{4,5},{5,6},{6,7},{7,4},{8,9},{9,10},{10,1... | collective-permute-start | bytes 110600 | tf_op jit(solution)/shard_map/ppermute | solution.py:466
  28.2 6.3 %collective-permute-start.4 = (bf16[16,1152]{1,0:T(8,128)(2,1)S(1)}, bf16[16,1152]{1,0:T(8,128)(2,1)S(1)}, u32[]{:S(2)}, u32[]{:S(2)}) collective-permute-start(bf16[16,1152]{1,0:T(8,128)(2,1)S(1)} %shard_map.101.rest_0_), channel_id=1, source_target_pairs={{0,2},{1,3},{2,0},{3,1},{4,6},{5,7},{6,4},{7,5},{8,10},{9,11},{10,... | collective-permute-start | bytes 110600 | tf_op jit(solution)/shard_map/ppermute | solution.py:466
  30.6 4.0 %collective-permute-start.5 = (bf16[16,1152]{1,0:T(8,128)(2,1)S(1)}, bf16[16,1152]{1,0:T(8,128)(2,1)S(1)}, u32[]{:S(2)}, u32[]{:S(2)}) collective-permute-start(bf16[16,1152]{1,0:T(8,128)(2,1)S(1)} %shard_map.101.rest_0_), channel_id=1, source_target_pairs={{0,3},{1,0},{2,1},{3,2},{4,7},{5,4},{6,5},{7,6},{8,11},{9,8},{10,9... | collective-permute-start | bytes 110600 | tf_op jit(solution)/shard_map/ppermute | solution.py:466
  34.6 1.6 %copy-start.1 = (bf16[1,2,4096,128]{3,2,1,0:T(8,128)(2,1)S(1)}, bf16[1,2,4096,128]{3,2,1,0:T(8,128)(2,1)}, u32[]{:S(2)}) copy-start(bf16[1,2,4096,128]{3,2,1,0:T(8,128)(2,1)} %rest_5_.3) | copy-start | bytes 6291460
  42.2 9.0 %collective-permute-start.6 = (bf16[16,1152]{1,0:T(8,128)(2,1)S(1)}, bf16[16,1152]{1,0:T(8,128)(2,1)S(1)}, u32[]{:S(2)}, u32[]{:S(2)}) collective-permute-start(bf16[16,1152]{1,0:T(8,128)(2,1)S(1)} %get-tuple-element.37), channel_id=1, source_target_pairs={{0,3},{1,0},{2,1},{3,2},{4,7},{5,4},{6,5},{7,6},{8,11},{9,8},{10,9... | collective-permute-start | bytes 110600 | tf_op jit(solution)/shard_map/ppermute | solution.py:458
  46.3 4.9 %collective-permute-start.7 = (bf16[16,1152]{1,0:T(8,128)(2,1)S(1)}, bf16[16,1152]{1,0:T(8,128)(2,1)S(1)}, u32[]{:S(2)}, u32[]{:S(2)}) collective-permute-start(bf16[16,1152]{1,0:T(8,128)(2,1)S(1)} %get-tuple-element.38), channel_id=1, source_target_pairs={{0,2},{1,3},{2,0},{3,1},{4,6},{5,7},{6,4},{7,5},{8,10},{9,11},{10,... | collective-permute-start | bytes 110600 | tf_op jit(solution)/shard_map/ppermute | solution.py:458
  46.3 5.8 %collective-permute-start.8 = (bf16[16,1152]{1,0:T(8,128)(2,1)S(1)}, bf16[16,1152]{1,0:T(8,128)(2,1)S(1)}, u32[]{:S(2)}, u32[]{:S(2)}) collective-permute-start(bf16[16,1152]{1,0:T(8,128)(2,1)S(1)} %get-tuple-element.39), channel_id=1, source_target_pairs={{0,1},{1,2},{2,3},{3,0},{4,5},{5,6},{6,7},{7,4},{8,9},{9,10},{10,1... | collective-permute-start | bytes 110600 | tf_op jit(solution)/shard_map/ppermute | solution.py:458
  52.3 8.5 %collective-permute-start.10 = (bf16[16,1024]{1,0:T(8,128)(2,1)S(1)}, bf16[16,1024]{1,0:T(8,128)(2,1)S(1)}, u32[]{:S(2)}, u32[]{:S(2)}) collective-permute-start(bf16[16,1024]{1,0:T(8,128)(2,1)S(1)} %shard_map.104.after_ref.rest_0_), channel_id=1, source_target_pairs={{0,2},{1,3},{2,0},{3,1},{4,6},{5,7},{6,4},{7,5},{8,10},{9,11},{10,... | collective-permute-start | bytes 98312 | tf_op jit(solution)/shard_map/ppermute | solution.py:466
  53.7 7.1 %collective-permute-start.11 = (bf16[16,1024]{1,0:T(8,128)(2,1)S(1)}, bf16[16,1024]{1,0:T(8,128)(2,1)S(1)}, u32[]{:S(2)}, u32[]{:S(2)}) collective-permute-start(bf16[16,1024]{1,0:T(8,128)(2,1)S(1)} %shard_map.104.after_ref.rest_0_), channel_id=1, source_target_pairs={{0,3},{1,0},{2,1},{3,2},{4,7},{5,4},{6,5},{7,6},{8,11},{9,8},{10,9... | collective-permute-start | bytes 98312 | tf_op jit(solution)/shard_map/ppermute | solution.py:466
  56.7 5.7 %collective-permute-start.9 = (bf16[16,1024]{1,0:T(8,128)(2,1)S(1)}, bf16[16,1024]{1,0:T(8,128)(2,1)S(1)}, u32[]{:S(2)}, u32[]{:S(2)}) collective-permute-start(bf16[16,1024]{1,0:T(8,128)(2,1)S(1)} %shard_map.104.after_ref.rest_0_), channel_id=1, source_target_pairs={{0,1},{1,2},{2,3},{3,0},{4,5},{5,6},{6,7},{7,4},{8,9},{9,10},{10,1... | collective-permute-start | bytes 98312 | tf_op jit(solution)/shard_map/ppermute | solution.py:466
  71.0 7.7 %collective-permute-start.12 = (f32[4,4096]{1,0:T(4,128)}, f32[4,4096]{1,0:T(4,128)S(1)}, u32[]{:S(2)}, u32[]{:S(2)}) collective-permute-start(f32[4,4096]{1,0:T(4,128)} %get-tuple-element.41), channel_id=1, source_target_pairs={{0,12},{4,0},{8,4},{12,8},{1,13},{5,1},{9,5},{13,9},{2,14},{6,2},{... | collective-permute-start | bytes 196616 | tf_op jit(solution)/shard_map/ppermute | solution.py:458
  71.0 7.7 %collective-permute-start.13 = (f32[4,4096]{1,0:T(4,128)}, f32[4,4096]{1,0:T(4,128)S(1)}, u32[]{:S(2)}, u32[]{:S(2)}) collective-permute-start(f32[4,4096]{1,0:T(4,128)} %get-tuple-element.42), channel_id=1, source_target_pairs={{0,8},{4,12},{8,0},{12,4},{1,9},{5,13},{9,1},{13,5},{2,10},{6,14},... | collective-permute-start | bytes 196616 | tf_op jit(solution)/shard_map/ppermute | solution.py:458
  72.6 6.1 %collective-permute-start.14 = (f32[4,4096]{1,0:T(4,128)S(1)}, f32[4,4096]{1,0:T(4,128)S(1)}, u32[]{:S(2)}, u32[]{:S(2)}) collective-permute-start(f32[4,4096]{1,0:T(4,128)S(1)} %get-tuple-element.43), channel_id=1, source_target_pairs={{0,4},{4,8},{8,12},{12,0},{1,5},{5,9},{9,13},{13,1},{2,6},{6,10},{... | collective-permute-start | bytes 196616 | tf_op jit(solution)/shard_map/ppermute | solution.py:458
  78.7 9.2 %copy-start.8 = (s32[16]{0:T(128)S(1)}, s32[16]{0:T(128)}, u32[]{:S(2)}) copy-start(s32[16]{0:T(128)} %fusion.3) | copy-start | bytes 196
  79.6 12.8 %collective-permute-start.16 = (bf16[4,4224]{1,0:T(4,128)(2,1)S(1)}, bf16[4,4224]{1,0:T(4,128)(2,1)S(1)}, u32[]{:S(2)}, u32[]{:S(2)}) collective-permute-start(bf16[4,4224]{1,0:T(4,128)(2,1)S(1)} %get-tuple-element.44), channel_id=1, source_target_pairs={{0,16},{4,20},{8,24},{12,28},{1,17},{5,21},{9,25},{13,29},{2,18},{... | collective-permute-start | bytes 101384 | tf_op jit(solution)/shard_map/ppermute | solution.py:548
  83.0 9.4 %collective-permute-start.17 = (bf16[4,4224]{1,0:T(4,128)(2,1)S(1)}, bf16[4,4224]{1,0:T(4,128)(2,1)S(1)}, u32[]{:S(2)}, u32[]{:S(2)}) collective-permute-start(bf16[4,4224]{1,0:T(4,128)(2,1)S(1)} %get-tuple-element.44), channel_id=1, source_target_pairs={{0,20},{4,24},{8,28},{12,16},{1,21},{5,25},{9,29},{13,17},{2,22},{... | collective-permute-start | bytes 101384 | tf_op jit(solution)/shard_map/ppermute | solution.py:548
  84.3 8.1 %collective-permute-start.18 = (bf16[4,4224]{1,0:T(4,128)(2,1)S(1)}, bf16[4,4224]{1,0:T(4,128)(2,1)S(1)}, u32[]{:S(2)}, u32[]{:S(2)}) collective-permute-start(bf16[4,4224]{1,0:T(4,128)(2,1)S(1)} %get-tuple-element.44), channel_id=1, source_target_pairs={{0,24},{4,28},{8,16},{12,20},{1,25},{5,29},{9,17},{13,21},{2,26},{... | collective-permute-start | bytes 101384 | tf_op jit(solution)/shard_map/ppermute | solution.py:548
  85.6 6.8 %collective-permute-start.19 = (bf16[4,4224]{1,0:T(4,128)(2,1)S(1)}, bf16[4,4224]{1,0:T(4,128)(2,1)S(1)}, u32[]{:S(2)}, u32[]{:S(2)}) collective-permute-start(bf16[4,4224]{1,0:T(4,128)(2,1)S(1)} %get-tuple-element.44), channel_id=1, source_target_pairs={{0,28},{4,16},{8,20},{12,24},{1,29},{5,17},{9,21},{13,25},{2,30},{... | collective-permute-start | bytes 101384 | tf_op jit(solution)/shard_map/ppermute | solution.py:548
  92.5 24.0 %copy-start.2 = (bf16[1,2,4096,128]{3,2,1,0:T(8,128)(2,1)S(1)}, bf16[1,2,4096,128]{3,2,1,0:T(8,128)(2,1)}, u32[]{:S(2)}) copy-start(bf16[1,2,4096,128]{3,2,1,0:T(8,128)(2,1)} %rest_5_.3) | copy-start | bytes 6291460
  99.7 5.2 %collective-permute-start.20 = (f32[16,1280]{1,0:T(8,128)S(1)}, f32[16,1280]{1,0:T(8,128)S(1)}, u32[]{:S(2)}, u32[]{:S(2)}) collective-permute-start(f32[16,1280]{1,0:T(8,128)S(1)} %get-tuple-element.47), channel_id=1, source_target_pairs={{0,3},{1,0},{2,1},{3,2},{4,7},{5,4},{6,5},{7,6},{8,11},{9,8},{10,9... | collective-permute-start | bytes 245768 | tf_op jit(solution)/shard_map/ppermute | solution.py:458
  102.1 8.0 %collective-permute-start.21 = (f32[16,1280]{1,0:T(8,128)S(1)}, f32[16,1280]{1,0:T(8,128)S(1)}, u32[]{:S(2)}, u32[]{:S(2)}) collective-permute-start(f32[16,1280]{1,0:T(8,128)S(1)} %get-tuple-element.48), channel_id=1, source_target_pairs={{0,2},{1,3},{2,0},{3,1},{4,6},{5,7},{6,4},{7,5},{8,10},{9,11},{10,... | collective-permute-start | bytes 245768 | tf_op jit(solution)/shard_map/ppermute | solution.py:458
  102.1 8.0 %collective-permute-start.22 = (f32[16,1280]{1,0:T(8,128)S(1)}, f32[16,1280]{1,0:T(8,128)S(1)}, u32[]{:S(2)}, u32[]{:S(2)}) collective-permute-start(f32[16,1280]{1,0:T(8,128)S(1)} %get-tuple-element.49), channel_id=1, source_target_pairs={{0,1},{1,2},{2,3},{3,0},{4,5},{5,6},{6,7},{7,4},{8,9},{9,10},{10,1... | collective-permute-start | bytes 245768 | tf_op jit(solution)/shard_map/ppermute | solution.py:458
  110.2 6.0 %collective-permute-start.23 = (bf16[16,1152]{1,0:T(8,128)(2,1)S(1)}, bf16[16,1152]{1,0:T(8,128)(2,1)S(1)}, u32[]{:S(2)}, u32[]{:S(2)}) collective-permute-start(bf16[16,1152]{1,0:T(8,128)(2,1)S(1)} %shard_map.111.rest_0_), channel_id=1, source_target_pairs={{0,1},{1,2},{2,3},{3,0},{4,5},{5,6},{6,7},{7,4},{8,9},{9,10},{10,1... | collective-permute-start | bytes 110600 | tf_op jit(solution)/shard_map/ppermute | solution.py:466
  110.2 6.0 %collective-permute-start.24 = (bf16[16,1152]{1,0:T(8,128)(2,1)S(1)}, bf16[16,1152]{1,0:T(8,128)(2,1)S(1)}, u32[]{:S(2)}, u32[]{:S(2)}) collective-permute-start(bf16[16,1152]{1,0:T(8,128)(2,1)S(1)} %shard_map.111.rest_0_), channel_id=1, source_target_pairs={{0,2},{1,3},{2,0},{3,1},{4,6},{5,7},{6,4},{7,5},{8,10},{9,11},{10,... | collective-permute-start | bytes 110600 | tf_op jit(solution)/shard_map/ppermute | solution.py:466
  112.5 4.0 %collective-permute-start.25 = (bf16[16,1152]{1,0:T(8,128)(2,1)S(1)}, bf16[16,1152]{1,0:T(8,128)(2,1)S(1)}, u32[]{:S(2)}, u32[]{:S(2)}) collective-permute-start(bf16[16,1152]{1,0:T(8,128)(2,1)S(1)} %shard_map.111.rest_0_), channel_id=1, source_target_pairs={{0,3},{1,0},{2,1},{3,2},{4,7},{5,4},{6,5},{7,6},{8,11},{9,8},{10,9... | collective-permute-start | bytes 110600 | tf_op jit(solution)/shard_map/ppermute | solution.py:466
  122.6 8.9 %collective-permute-start.26 = (bf16[16,1152]{1,0:T(8,128)(2,1)S(1)}, bf16[16,1152]{1,0:T(8,128)(2,1)S(1)}, u32[]{:S(2)}, u32[]{:S(2)}) collective-permute-start(bf16[16,1152]{1,0:T(8,128)(2,1)S(1)} %get-tuple-element.51), channel_id=1, source_target_pairs={{0,3},{1,0},{2,1},{3,2},{4,7},{5,4},{6,5},{7,6},{8,11},{9,8},{10,9... | collective-permute-start | bytes 110600 | tf_op jit(solution)/shard_map/ppermute | solution.py:458
  126.7 4.9 %collective-permute-start.27 = (bf16[16,1152]{1,0:T(8,128)(2,1)S(1)}, bf16[16,1152]{1,0:T(8,128)(2,1)S(1)}, u32[]{:S(2)}, u32[]{:S(2)}) collective-permute-start(bf16[16,1152]{1,0:T(8,128)(2,1)S(1)} %get-tuple-element.52), channel_id=1, source_target_pairs={{0,2},{1,3},{2,0},{3,1},{4,6},{5,7},{6,4},{7,5},{8,10},{9,11},{10,... | collective-permute-start | bytes 110600 | tf_op jit(solution)/shard_map/ppermute | solution.py:458
  126.7 5.8 %collective-permute-start.28 = (bf16[16,1152]{1,0:T(8,128)(2,1)S(1)}, bf16[16,1152]{1,0:T(8,128)(2,1)S(1)}, u32[]{:S(2)}, u32[]{:S(2)}) collective-permute-start(bf16[16,1152]{1,0:T(8,128)(2,1)S(1)} %get-tuple-element.53), channel_id=1, source_target_pairs={{0,1},{1,2},{2,3},{3,0},{4,5},{5,6},{6,7},{7,4},{8,9},{9,10},{10,1... | collective-permute-start | bytes 110600 | tf_op jit(solution)/shard_map/ppermute | solution.py:458
  132.7 9.8 %collective-permute-start.29 = (bf16[16,1024]{1,0:T(8,128)(2,1)S(1)}, bf16[16,1024]{1,0:T(8,128)(2,1)S(1)}, u32[]{:S(2)}, u32[]{:S(2)}) collective-permute-start(bf16[16,1024]{1,0:T(8,128)(2,1)S(1)} %shard_map.114.after_ref.rest_0_), channel_id=1, source_target_pairs={{0,1},{1,2},{2,3},{3,0},{4,5},{5,6},{6,7},{7,4},{8,9},{9,10},{10,1... | collective-permute-start | bytes 98312 | tf_op jit(solution)/shard_map/ppermute | solution.py:466
  134.7 7.9 %collective-permute-start.30 = (bf16[16,1024]{1,0:T(8,128)(2,1)S(1)}, bf16[16,1024]{1,0:T(8,128)(2,1)S(1)}, u32[]{:S(2)}, u32[]{:S(2)}) collective-permute-start(bf16[16,1024]{1,0:T(8,128)(2,1)S(1)} %shard_map.114.after_ref.rest_0_), channel_id=1, source_target_pairs={{0,2},{1,3},{2,0},{3,1},{4,6},{5,7},{6,4},{7,5},{8,10},{9,11},{10,... | collective-permute-start | bytes 98312 | tf_op jit(solution)/shard_map/ppermute | solution.py:466
  135.6 7.0 %collective-permute-start.31 = (bf16[16,1024]{1,0:T(8,128)(2,1)S(1)}, bf16[16,1024]{1,0:T(8,128)(2,1)S(1)}, u32[]{:S(2)}, u32[]{:S(2)}) collective-permute-start(bf16[16,1024]{1,0:T(8,128)(2,1)S(1)} %shard_map.114.after_ref.rest_0_), channel_id=1, source_target_pairs={{0,3},{1,0},{2,1},{3,2},{4,7},{5,4},{6,5},{7,6},{8,11},{9,8},{10,9... | collective-permute-start | bytes 98312 | tf_op jit(solution)/shard_map/ppermute | solution.py:466
  137.1 14.2 %collective-permute-start.35 = (f32[4,4096]{1,0:T(4,128)S(1)}, f32[4,4096]{1,0:T(4,128)S(1)}, u32[]{:S(2)}, u32[]{:S(2)}) collective-permute-start(f32[4,4096]{1,0:T(4,128)S(1)} %get-tuple-element.45.after_ref), channel_id=1, source_target_pairs={{0,16},{1,17},{2,18},{3,19},{4,20},{5,21},{6,22},{7,23},{8,24},{9,... | collective-permute-start | bytes 196616 | tf_op jit(solution)/shard_map/ppermute | solution.py:556
  150.5 2.4 %collective-permute-start.32 = (f32[4,4096]{1,0:T(4,128)S(1)}, f32[4,4096]{1,0:T(4,128)S(1)}, u32[]{:S(2)}, u32[]{:S(2)}) collective-permute-start(f32[4,4096]{1,0:T(4,128)S(1)} %get-tuple-element.55), channel_id=1, source_target_pairs={{0,12},{4,0},{8,4},{12,8},{1,13},{5,1},{9,5},{13,9},{2,14},{6,2},{... | collective-permute-start | bytes 196616 | tf_op jit(solution)/shard_map/ppermute | solution.py:458
  150.5 5.0 %collective-permute-start.33 = (f32[4,4096]{1,0:T(4,128)S(1)}, f32[4,4096]{1,0:T(4,128)S(1)}, u32[]{:S(2)}, u32[]{:S(2)}) collective-permute-start(f32[4,4096]{1,0:T(4,128)S(1)} %get-tuple-element.56), channel_id=1, source_target_pairs={{0,8},{4,12},{8,0},{12,4},{1,9},{5,13},{9,1},{13,5},{2,10},{6,14},... | collective-permute-start | bytes 196616 | tf_op jit(solution)/shard_map/ppermute | solution.py:458
  151.2 4.6 %collective-permute-start.34 = (f32[4,4096]{1,0:T(4,128)S(1)}, f32[4,4096]{1,0:T(4,128)S(1)}, u32[]{:S(2)}, u32[]{:S(2)}) collective-permute-start(f32[4,4096]{1,0:T(4,128)S(1)} %get-tuple-element.57), channel_id=1, source_target_pairs={{0,4},{4,8},{8,12},{12,0},{1,5},{5,9},{9,13},{13,1},{2,6},{6,10},{... | collective-permute-start | bytes 196616 | tf_op jit(solution)/shard_map/ppermute | solution.py:458

commit v3 on v2

--- a/solution.py
+++ b/solution.py
@@ -28,6 +28,10 @@
     rest = value - high
     middle = rest.astype(BF16).astype(F32)
     return high, middle, rest - middle
+
+
+def stats_width(heads):
+    return -(-3 * heads // LANES) * LANES
 
 
 def block_depth(model):
@@ -167,7 +171,7 @@
 
 def normalize_kernel(model, *refs):
     total = refs[0][...]
-    for ref in refs[1:-1]:
+    for ref in refs[1:-2]:
         total = total + ref[...]
     out_ref = refs[-1]
     width = out_ref.shape[1]
@@ -175,25 +179,25 @@
     out_ref[...] = (total[:, :width] * scale).astype(BF16)
 
 
-def normalize(parts, model):
+def normalize(parts, model, after):
     rows, width = parts[0].shape
     return pl.pallas_call(
         functools.partial(normalize_kernel, model),
         out_shape=jax.ShapeDtypeStruct((rows, width - LANES), BF16),
+        in_specs=[vmem()] * len(parts) + [pl.BlockSpec(memory_space=pl.ANY)],
         compiler_params=params(8),
         cost_estimate=pl.CostEstimate(
             flops=rows * width * 4, bytes_accessed=rows * width * 16, transcendentals=0
         ),
-    )(*parts)
+    )(*parts, after)
 
 
 def attend_kernel(
-    blocks, chunks, batch, group, me_ref, order_ref, lengths_ref, *rest
+    blocks, batch, group, me_ref, order_ref, lengths_ref, *rest
 ):
     parts = rest[:blocks]
     pre_k, pre_v, suf_k, suf_v = rest[blocks : blocks + 4]
-    outs = rest[blocks + 4 : blocks + 4 + chunks]
-    q_ref, s_ref, o_ref = rest[blocks + 4 + chunks :]
+    out_ref, q_ref, s_ref, stats_ref = rest[blocks + 4 :]
     head = pl.program_id(0)
     me = me_ref[0]
     rows, hd = q_ref.shape[1], pre_k.shape[1]
@@ -287,45 +291,45 @@
     level = row_max + jnp.log2(total)
     terms = split3(level)
 
-    per = o_ref.shape[2] // hd - 1
-    lane = lax.broadcasted_iota(jnp.int32, (rows, LANES), 1)
-    for first_head in range(0, group, per):
-        at = head * (group // per) + first_head // per
-        stats = jnp.zeros((rows, LANES), F32)
-        for i in range(per):
-            g = first_head + i
-            o_ref[at, :, i * hd : (i + 1) * hd] = mixed[g * rows : (g + 1) * rows].astype(BF16)
-            for n in range(3):
-                stats = jnp.where(lane == n * per + i, terms[n][g * rows : (g + 1) * rows], stats)
-        o_ref[at, :, per * hd :] = stats.astype(BF16)
-
-    @pl.when(head == pl.num_programs(0) - 1)
-    def _():
-        for k in range(chunks):
-            outs[k][...] = o_ref[lax.rem(me - k + chunks, chunks)]
-
-
-def attend(parts, keys, values, suffix_keys, suffix_values, me, order, lengths, chunks, group):
+    heads = pl.num_programs(0) * group
+    mixed = mixed.astype(BF16)
+    lane = lax.broadcasted_iota(jnp.int32, stats_ref.shape, 1) - first_lane(head, group)
+    stats = jnp.where(head == 0, 0.0, stats_ref[...])
+    for g in range(group):
+        at = pl.multiple_of((head * group + g) * hd, hd)
+        out_ref[:, pl.ds(at, hd)] = mixed[g * rows : (g + 1) * rows]
+        for n in range(3):
+            stats = jnp.where(lane == n * heads + g, terms[n][g * rows : (g + 1) * rows], stats)
+    stats_ref[...] = stats
+    out_ref[:, out_ref.shape[1] - stats.shape[1] :] = stats.astype(BF16)
+
+
+def first_lane(head, group):
+    return head * group
+
+
+def attend(parts, keys, values, suffix_keys, suffix_values, me, order, lengths, group):
     rows = parts[0].shape[0]
     heads, positions, hd = keys.shape[1:]
     samples, depth = suffix_keys.shape[2:4]
-    width = heads * group * hd // chunks + LANES
+    stats = stats_width(heads * group)
+    width = heads * group * hd + stats
     total = positions + samples * depth + rows + (-rows % LANES)
     shape = jax.ShapeDtypeStruct((rows, width), BF16)
     cache = pl.BlockSpec((None, None, positions, hd), lambda h, *_: (0, h, 0, 0))
     suffix = pl.BlockSpec((None, None, samples, depth, hd), lambda h, *_: (0, h, 0, 0, 0))
     return pl.pallas_call(
-        functools.partial(attend_kernel, len(parts), chunks, order.shape[0], group),
-        out_shape=[shape] * chunks,
+        functools.partial(attend_kernel, len(parts), order.shape[0], group),
+        out_shape=shape,
         grid_spec=pltpu.PrefetchScalarGridSpec(
             num_scalar_prefetch=3,
             grid=(heads,),
             in_specs=[whole(part.shape) for part in parts] + [cache, cache, suffix, suffix],
-            out_specs=[whole(shape.shape)] * chunks,
+            out_specs=whole(shape.shape),
             scratch_shapes=[
                 pltpu.VMEM((heads * (group + 2), rows, hd), BF16),
                 pltpu.VMEM((group * rows, total), F32),
-                pltpu.VMEM((chunks, rows, width), BF16),
+                pltpu.VMEM((rows, stats), F32),
             ],
         ),
         compiler_params=params(20 if group * rows * total < 1 << 21 else 48),
@@ -337,50 +341,38 @@
     )(me, order, lengths, *parts, keys, values, suffix_keys, suffix_values)
 
 
-def merge_kernel(hd, *refs):
-    parts, out_ref = refs[:-2], refs[-1]
-    per = out_ref.shape[1] // hd
-    stats = [ref[:, per * hd :].astype(F32) for ref in parts]
-    for i in range(per):
-        levels = [
-            s[:, i : i + 1] + s[:, per + i : per + i + 1] + s[:, 2 * per + i : 2 * per + i + 1]
-            for s in stats
-        ]
-        top = functools.reduce(jnp.maximum, levels)
-        shares = [jnp.exp2(level - top) for level in levels]
-        inverse = 1.0 / functools.reduce(jnp.add, shares)
+def merge(parts, heads, hd, store):
+    stats = [ref[:, heads * hd :].astype(F32) for ref in parts]
+    levels = [
+        s[:, :heads] + s[:, heads : 2 * heads] + s[:, 2 * heads : 3 * heads] for s in stats
+    ]
+    top = functools.reduce(jnp.maximum, levels)
+    shares = [jnp.exp2(level - top) for level in levels]
+    inverse = 1.0 / functools.reduce(jnp.add, shares)
+    shares = [share * inverse for share in shares]
+    for h in range(heads):
         mixed = 0.0
         for ref, share in zip(parts, shares):
-            mixed = mixed + ref[:, i * hd : (i + 1) * hd].astype(F32) * (share * inverse)
-        out_ref[:, i * hd : (i + 1) * hd] = mixed.astype(BF16)
-
-
-def merge(parts, hd, after):
-    rows, width = parts[0].shape
-    return pl.pallas_call(
-        functools.partial(merge_kernel, hd),
-        out_shape=jax.ShapeDtypeStruct((rows, width - LANES), BF16),
-        in_specs=[vmem()] * len(parts) + [pl.BlockSpec(memory_space=pl.ANY)],
-        compiler_params=params(8),
-        cost_estimate=pl.CostEstimate(
-            flops=rows * width * 8, bytes_accessed=rows * width * 10, transcendentals=rows * LANES
-        ),
-    )(*parts, after)
-
-
-def output_kernel(blocks, groups, parts, me_ref, turn_ref, w_ref, *rest):
+            mixed = mixed + ref[:, h * hd : (h + 1) * hd].astype(F32) * share[:, h : h + 1]
+        store(h, mixed.astype(BF16))
+
+
+def output_kernel(blocks, groups, parts, hd, turn_ref, w_ref, *rest):
     mixed, held = rest[:blocks], rest[blocks : blocks + parts]
     outs = rest[blocks + parts : blocks + parts + groups]
-    a_ref, acc_ref, buffer_ref, sem_ref = rest[blocks + parts + groups :]
+    m_ref, a_ref, acc_ref, buffer_ref, sem_ref = rest[blocks + parts + groups :]
     start_blocks(held, w_ref, buffer_ref, sem_ref)
     depth = a_ref.shape[2]
-    per = mixed[0].shape[1] // depth
-    me = me_ref[0]
-    for k in range(blocks):
-        turned = jnp.dot(turn_ref[...], mixed[k][...], preferred_element_type=F32).astype(BF16)
-        at = lax.rem(me - k + blocks, blocks) * per
-        for i in range(per):
-            a_ref[at + i] = turned[:, i * depth : (i + 1) * depth]
+
+    def store(h, value):
+        m_ref[:, h * hd : (h + 1) * hd] = value
+
+    merge(mixed, m_ref.shape[1] // hd, hd, store)
+    for i in range(a_ref.shape[0]):
+        turned = jnp.dot(
+            turn_ref[...], m_ref[:, i * depth : (i + 1) * depth], preferred_element_type=F32
+        )
+        a_ref[i] = turned.astype(BF16)
     acc_ref[...] = jnp.zeros_like(acc_ref)
 
     def apply(i, w):
@@ -388,26 +380,26 @@
 
     each_block(apply, held, w_ref, buffer_ref, sem_ref)
     size = outs[0].shape[0]
-    stride = acc_ref.shape[0] // groups
     for k in range(groups):
-        outs[k][...] = acc_ref[k * stride : k * stride + size, :]
-
-
-def output(mixed, turn, w, held, me, groups, size, depth):
+        outs[k][...] = acc_ref[k * size : (k + 1) * size, :].astype(BF16)
+
+
+def output(mixed, turn, w, held, groups, hd):
     blocks = len(mixed)
     rows = mixed[0].shape[0]
     model, columns = w.shape[1:]
+    depth = block_depth(model)
     left = model // depth - sum(part.shape[0] for part in held)
-    padded = turn.shape[0]
-    shape = jax.ShapeDtypeStruct((size, columns), F32)
-    return pl.pallas_call(
-        functools.partial(output_kernel, blocks, groups, len(held)),
+    shape = jax.ShapeDtypeStruct((rows // groups, columns), BF16)
+    return pl.pallas_call(
+        functools.partial(output_kernel, blocks, groups, len(held), hd),
         out_shape=[shape] * groups,
-        in_specs=[smem(), vmem(), hbm()] + [vmem()] * (blocks + len(held)),
+        in_specs=[vmem(), hbm()] + [vmem()] * (blocks + len(held)),
         out_specs=[vmem()] * groups,
         scratch_shapes=[
-            pltpu.VMEM((model // depth, padded, depth), BF16),
-            pltpu.VMEM((padded, columns), F32),
+            pltpu.VMEM((rows, model), BF16),
+            pltpu.VMEM((model // depth, rows, depth), BF16),
+            pltpu.VMEM((rows, columns), F32),
             pltpu.VMEM((left, depth, columns), BF16),
             pltpu.SemaphoreType.DMA((left,)),
         ],
@@ -417,14 +409,26 @@
             bytes_accessed=2 * left * depth * columns,
             transcendentals=0,
         ),
-    )(me, turn, w, *mixed, *held)
-
-
-def add_kernel(*refs):
-    parts, (gain_ref, _, y_ref, out_ref) = refs[:-4], refs[-4:]
-    total = parts[0][...]
+    )(turn, w, *mixed, *held)
+
+
+def add(parts, residual):
+    total = parts[0][...].astype(F32)
     for ref in parts[1:]:
-        total = total + ref[...]
+        total = total + ref[...].astype(F32)
+    return total + residual
+
+
+def residual_of(refs, size):
+    if len(refs) == 1:
+        return refs[0][...]
+    turn_ref, tokens_ref = refs
+    return jnp.dot(turn_ref[:size], tokens_ref[...], preferred_element_type=F32)
+
+
+def add_kernel(count, *refs):
+    parts, rest, (gain_ref, _, y_ref, out_ref) = refs[:count], refs[count:-4], refs[-4:]
+    total = add(parts, residual_of(rest, y_ref.shape[0]))
     y_ref[...] = total
     wide = total.shape[1]
     out_ref[:, :wide] = (total * gain_ref[...].astype(F32)).astype(BF16)
@@ -436,20 +440,45 @@
     out_ref[:, wide:] = terms.astype(BF16)
 
 
-def add_up(parts, gain, after):
+def add_up(parts, residual, gain, after):
     rows, width = parts[0].shape
     return pl.pallas_call(
-        add_kernel,
+        functools.partial(add_kernel, len(parts)),
         out_shape=[
             jax.ShapeDtypeStruct((rows, width), F32),
             jax.ShapeDtypeStruct((rows, width + LANES), BF16),
         ],
-        in_specs=[vmem()] * (len(parts) + 1) + [pl.BlockSpec(memory_space=pl.ANY)],
+        in_specs=[vmem()] * (len(parts) + len(residual) + 1)
+        + [pl.BlockSpec(memory_space=pl.ANY)],
         compiler_params=params(8),
         cost_estimate=pl.CostEstimate(
-            flops=rows * width * 8, bytes_accessed=rows * width * 24, transcendentals=0
-        ),
-    )(*parts, gain, after)
+            flops=rows * width * 8, bytes_accessed=rows * width * 16, transcendentals=0
+        ),
+    )(*parts, *residual, gain, after)
+
+
+def finish_kernel(count, place_ref, *refs):
+    parts, rest, (earlier_ref, out_ref) = refs[:count], refs[count:-2], refs[-2:]
+    total = add(parts, residual_of(rest, earlier_ref.shape[0]))
+    total = jnp.where(place_ref[0] == 1, total, earlier_ref[...])
+    _, steps, share, _ = out_ref.shape
+    for t in range(steps):
+        first, second = (total[(2 * t + n) * share : (2 * t + n + 1) * share] for n in range(2))
+        out_ref[0, t] = jnp.where(place_ref[1] == 0, first, second)
+
+
+def finish(parts, residual, earlier, place, steps):
+    rows, width = parts[0].shape
+    return pl.pallas_call(
+        functools.partial(finish_kernel, len(parts)),
+        out_shape=jax.ShapeDtypeStruct((1, steps, rows // steps // 2, width), F32),
+        in_specs=[smem()] + [vmem()] * (len(parts) + len(residual) + 1),
+        out_specs=vmem(),
+        compiler_params=params(8),
+        cost_estimate=pl.CostEstimate(
+            flops=rows * width * 8, bytes_accessed=rows * width * 16, transcendentals=0
+        ),
+    )(place, *parts, *residual, earlier)
 
 
 def back(parts, axis):
@@ -489,34 +518,28 @@
     group = slots - 2
     model = w_qkv.shape[1] * ctx
     share = batch // tp
-    size = steps * share
+    groups = tp // 2
+    size = rows // groups
     section, tp_me = lax.axis_index("section"), lax.axis_index("tp")
+    pair = tp_me // 2
     me = lax.axis_index("ctx").astype(jnp.int32).reshape(1)
     even = (heads * slots) % ctx == 0
     zero = jnp.zeros((1,), jnp.int32)
 
-    stride = size + (-size % 8)
-    i = jnp.arange(tp * stride)
-    k, j = i // stride, i % stride
-    owner = lax.rem(tp_me - k + tp, tp)
-    natural = jnp.where(j < size, (j // share) * batch + owner * share + j % share, -1)
+    i = jnp.arange(rows)
+    owner, j = jnp.bitwise_xor(pair, i // size), i % size
+    natural = (j // (2 * share)) * batch + owner * 2 * share + j % (2 * share)
     turn = (natural[:, None] == jnp.arange(rows)[None, :]).astype(BF16)
-    i = jnp.arange(tp * size)
-    k, j = i // size, i % size
-    owner = lax.rem(tp_me - k + tp, tp)
-    natural = (j // share) * batch + owner * share + j % share
     unturn = (jnp.arange(rows)[:, None] == natural[None, :]).astype(BF16)
 
-    mine = lax.dynamic_slice_in_dim(tokens_in, tp_me * share, share, 1)
-    residual = mine.astype(F32).reshape(size, columns)
-    gain = norm_gain
     next_gain = lax.ppermute(
         norm_gain, "section", [(s, (s - 1) % sections) for s in range(sections)]
     )
 
-    x, aux = tokens_in.reshape(rows, columns), gain
+    x, aux, after = tokens_in.reshape(rows, columns), norm_gain, next_gain
+    residual = (turn, x)
     result = None
-    in_depth, out_depth = block_depth(columns), divisor(w_out.shape[1] // ctx, 256)
+    in_depth, out_depth = block_depth(columns), block_depth(w_out.shape[1])
     in_blocks, out_blocks = columns // in_depth, w_out.shape[1] // out_depth
     ready = []
     for layer in range(sections):
@@ -524,37 +547,36 @@
         if even:
             sent = project(x, aux, w_qkv, ready, me, ctx, fresh)
             parts = back(sent, "ctx")
-            parts = around(normalize(parts, model), "ctx")
+            parts = around(normalize(parts, model, after), "ctx")
         else:
             part = project(x, aux, w_qkv, ready, zero, 1, fresh)[0]
-            parts = [normalize([lax.psum(part, "ctx")], model)]
+            parts = [normalize([lax.psum(part, "ctx")], model, after)]
         sent = attend(
             parts, prefix_keys, prefix_values, suffix_keys, suffix_values,
-            me, order, lengths, ctx, group,
+            me, order, lengths, group,
         )
-        first = load(w_out, 0, out_blocks * 5 // 16, out_depth, sent[0])
-        mixed = merge(back(sent, "ctx"), hd, first)
-        second = load(w_out, first.shape[0], out_blocks * 5 // 16, out_depth, mixed)
-        parts = around(mixed, "ctx")
-        sent = output(parts, turn, w_out, [first, second], me, tp, size, out_depth)
-        first = sent[0]
-        if layer + 1 < sections:
-            first = load(w_qkv, 0, in_blocks * 5 // 16, in_depth, sent[0])
-        y, message = add_up(back(sent, "tp") + [residual], next_gain, first)
+        held = load(w_out, 0, max(1, out_blocks * 10 // 16), out_depth, sent)
+        sent = output(around(sent, "ctx"), turn, w_out, [held], groups, hd)
+        parts = [sent[0]] + [
+            lax.ppermute(sent[k // 2], "tp", [(n, n ^ k) for n in range(tp)]) for k in range(1, tp)
+        ]
+        if layer + 1 == sections:
+            place = jnp.stack([section == layer, tp_me % 2]).astype(jnp.int32)
+            return finish(parts, residual, result, place, steps)
+        first = load(w_qkv, 0, max(1, in_blocks * 5 // 16), in_depth, sent[0])
+        y, message = add_up(parts, residual, next_gain, first)
         result = y if result is None else jnp.where(section == layer, y, result)
-        if layer + 1 < sections:
-            here, there = layer * tp, (layer + 1) * tp
-            received = [
-                lax.ppermute(
-                    message, ("section", "tp"), [(here + n, there + (n + k) % tp) for n in range(tp)]
-                )
-                for k in range(tp)
-            ]
-            second = load(w_qkv, first.shape[0], in_blocks * 5 // 16, in_depth, y)
-            ready = [first, second]
-            x, aux = jnp.concatenate(received, axis=0), unturn
-            residual = lax.ppermute(y, "section", [(layer, layer + 1)])
-    return result.reshape(1, steps, share, columns)
+        here, there = layer * tp, (layer + 1) * tp
+        received = []
+        for k in range(0, tp, 2):
+            pairs = [(here + n, there + (n ^ k)) for n in range(tp)]
+            pairs += [(b, a) for a, b in pairs]
+            received.append(lax.ppermute(message, ("section", "tp"), pairs))
+        second = load(w_qkv, first.shape[0], max(1, in_blocks * 3 // 16), in_depth, y)
+        ready = [first, second]
+        x, aux = jnp.concatenate(received, axis=0), unturn
+        residual = (lax.ppermute(y, "section", [(layer, layer + 1), (layer + 1, layer)]),)
+        after = residual[0]
 
 
 def solution(mesh):

time: 158 us -> 133 us (0.84)
  starting transfers between devices: 50.9 us -> 33 us
  Pallas kernels: 78 us -> 70.5 us
  waiting for transfers between devices: 22.2 us -> 26.2 us
  other arithmetic: 2.25 us -> 0.18 us
    ppermute x18 -> x6, starting transfers between devices: 21.4 us -> 9.7 us  [back(): lax.ppermute(parts[k], axis, [(i, (i - k) % count) for i in range(count)])]
    ppermute x18 -> x6, waiting for transfers between devices: 19 us -> 8.43 us  [back(): lax.ppermute(parts[k], axis, [(i, (i - k) % count) for i in range(count)])]
    ppermute x12, waiting for transfers between devices: 3.23 us -> 12.3 us  [around(): lax.ppermute(part, axis, [(i, (i + k) % count) for i in range(count)])]
    ppermute x12, starting transfers between devices: 18.5 us -> 13.4 us  [around(): lax.ppermute(part, axis, [(i, (i + k) % count) for i in range(count)])]
    pallas_call x6 -> x4, Pallas kernels: 25.4 us -> 21.9 us  [load(): pl.pallas_call(functools.partial(load_kernel, first), out_shape=jax.Shape...]
    ppermute x5 -> x9, waiting for transfers between devices: 0.01 us -> 3.07 us  [the longest x6 3.07 us: on_device(): lax.ppermute(sent[k // 2], 'tp', [(n, n ^ k) for n in range(tp)])]
    ppermute x1, waiting for transfers between devices: 0.01 us -> 2.46 us  [on_device(): lax.ppermute(norm_gain, 'section', [(s, (s - 1) % sections) for s in rang...]
    pallas_call x2, Pallas kernels: 16.5 us -> 14 us  [output(): pl.pallas_call(functools.partial(output_kernel, blocks, groups, len(held)...]
  transfers between devices with their start and end apart: 36 -> 28, of which waited for: 15 -> 14; matrix products, arithmetic and copies ran while one was open for 2% -> 0% of each run, Pallas kernels for 31% -> 22%
where the time goes in v3:
time: 133 us
  Pallas kernels  70.5 us (53%)
  starting transfers between devices  33 us (25%)
  waiting for transfers between devices  26.2 us (20%)
  local copies, waits for them, and re-layouts  2.67 us (2%)
    pallas_call x4, Pallas kernels, load(): pl.pallas_call(functools.partial(load_kernel, first), out_shape=jax.Shape...  21.9 us
    pallas_call x2, Pallas kernels, project(): pl.pallas_call(functools.partial(project_kernel, chunks, len(held), fresh...  21 us
    pallas_call x2, Pallas kernels, output(): pl.pallas_call(functools.partial(output_kernel, blocks, groups, len(held)...  14 us
    ppermute x12, starting transfers between devices, around(): lax.ppermute(part, axis, [(i, (i + k) % count) for i in range(count)])  13.4 us
    ppermute x12, waiting for transfers between devices, around(): lax.ppermute(part, axis, [(i, (i + k) % count) for i in range(count)])  12.3 us
    pallas_call x2, Pallas kernels, attend(): pl.pallas_call(functools.partial(attend_kernel, len(parts), order.shape[0...  11.9 us
    ppermute x6, starting transfers between devices, back(): lax.ppermute(parts[k], axis, [(i, (i - k) % count) for i in range(count)])  9.7 us
    ppermute x6, waiting for transfers between devices, back(): lax.ppermute(parts[k], axis, [(i, (i - k) % count) for i in range(count)])  8.43 us
  transfers between devices with their start and end apart: 28, of which 14 were waited for; matrix products, arithmetic and copies ran while one was open for 0% of the time, Pallas kernels for 22%

profile of v3, /device:TPU:0, one launch (start us, length us, event | category | flops | bytes accessed | tf_op | source)
XLA Modules:
  0.0 132.7 jit_solution(14117153429247092108)
XLA Ops:
  0.0 1.1 copy-done.5
  1.1 13.8 %shard_map.100 = (f32[16,1280]{1,0:T(8,128)S(1)}, f32[16,1280]{1,0:T(8,128)}, f32[16,1280]{1,0:T(8,128)}, f32[16,1280]{1,0:T(8,128)}) custom-call(s32[1]{0:T(128)} %bitcast.2.me_ref, bf16[16,4096]{1,0:T(8,128)(2,1)S(1)} %bitcast.4, bf16[1,4096]{1,0:T(2,128)(2,1)} %aux_ref.1, bf16[1,4096,4608]{2,1,0:T(8,128)(2,1)} %w_ref.13), custom_call_target="tpu_custom_call" | custom-call | flops 603979776 | bytes 37748736 | tf_op jit(solution)/shard_map/pallas_call | solution.py:151
  14.9 5.1 %collective-permute-start = (f32[16,1280]{1,0:T(8,128)}, f32[16,1280]{1,0:T(8,128)S(1)}, u32[]{:S(2)}, u32[]{:S(2)}) collective-permute-start(f32[16,1280]{1,0:T(8,128)} %get-tuple-element.20), channel_id=1, source_target_pairs={{0,3},{1,0},{2,1},{3,2},{4,7},{5,4},{6,5},{7,6},{8,11},{9,8},{10,9... | collective-permute-start | bytes 245768 | tf_op jit(solution)/shard_map/ppermute | solution.py:487
  20.0 1.0 collective-permute-start.2
  21.1 1.5 %collective-permute-start.3 = (bf16[1,4096]{1,0:T(2,128)(2,1)}, bf16[1,4096]{1,0:T(2,128)(2,1)S(1)}, u32[]{:S(2)}, u32[]{:S(2)}) collective-permute-start(bf16[1,4096]{1,0:T(2,128)(2,1)} %aux_ref.1), channel_id=1, source_target_pairs={{0,16},{16,0},{1,17},{17,1},{2,18},{18,2},{3,19},{19,3},{4,20},{20... | collective-permute-start | bytes 24584 | tf_op jit(solution)/shard_map/ppermute | solution.py:535
  22.5 2.5 %collective-permute-done.3.refs_4_.refs_6_ = bf16[1,4096]{1,0:T(2,128)(2,1)S(1)} collective-permute-done((bf16[1,4096]{1,0:T(2,128)(2,1)}, bf16[1,4096]{1,0:T(2,128)(2,1)S(1)}, u32[]{:S(2)}, u32[]{:S(2)}) %collective-permute-start.3) | collective-permute-done | bytes 8224 | tf_op jit(solution)/shard_map/ppermute | solution.py:535
  25.0 2.8 %collective-permute-done.1.refs_2_ = f32[16,1280]{1,0:T(8,128)S(1)} collective-permute-done((f32[16,1280]{1,0:T(8,128)}, f32[16,1280]{1,0:T(8,128)S(1)}, u32[]{:S(2)}, u32[]{:S(2)}) %collective-permute-start.1) | collective-permute-done | bytes 81952 | tf_op jit(solution)/shard_map/ppermute | solution.py:487
  27.9 2.1 %collective-permute-start.6 = (bf16[16,1152]{1,0:T(8,128)(2,1)S(1)}, bf16[16,1152]{1,0:T(8,128)(2,1)S(1)}, u32[]{:S(2)}, u32[]{:S(2)}) collective-permute-start(bf16[16,1152]{1,0:T(8,128)(2,1)S(1)} %shard_map.101.rest_0_), channel_id=1, source_target_pairs={{0,3},{1,0},{2,1},{3,2},{4,7},{5,4},{6,5},{7,6},{8,11},{9,8},{10,9... | collective-permute-start | bytes 110600 | tf_op jit(solution)/shard_map/ppermute | solution.py:495
  30.0 2.0 %collective-permute-start.4 = (bf16[16,1152]{1,0:T(8,128)(2,1)S(1)}, bf16[16,1152]{1,0:T(8,128)(2,1)S(1)}, u32[]{:S(2)}, u32[]{:S(2)}) collective-permute-start(bf16[16,1152]{1,0:T(8,128)(2,1)S(1)} %shard_map.101.rest_0_), channel_id=1, source_target_pairs={{0,1},{1,2},{2,3},{3,0},{4,5},{5,6},{6,7},{7,4},{8,9},{9,10},{10,1... | collective-permute-start | bytes 110600 | tf_op jit(solution)/shard_map/ppermute | solution.py:495
  32.0 2.8 %collective-permute-done.5.rest_2_ = bf16[16,1152]{1,0:T(8,128)(2,1)S(1)} collective-permute-done((bf16[16,1152]{1,0:T(8,128)(2,1)S(1)}, bf16[16,1152]{1,0:T(8,128)(2,1)S(1)}, u32[]{:S(2)}, u32[]{:S(2)}) %collective-permute-start.5) | collective-permute-done | bytes 36896 | tf_op jit(solution)/shard_map/ppermute | solution.py:495
  34.8 0.9 collective-permute-done.4.rest_1_
  35.8 1.6 %copy-done.1 = bf16[1,2,4096,128]{3,2,1,0:T(8,128)(2,1)S(1)} copy-done((bf16[1,2,4096,128]{3,2,1,0:T(8,128)(2,1)S(1)}, bf16[1,2,4096,128]{3,2,1,0:T(8,128)(2,1)}, u32[]{:S(2)}) %copy-start.1) | copy-done | bytes 2097176
  37.4 5.9 %shard_map.102.after_ref.rest_0_ = bf16[16,4224]{1,0:T(8,128)(2,1)S(1)} custom-call(s32[1]{0:T(128)} %bitcast.2.me_ref, s32[8]{0:T(128)S(1)} %copy-done.7, s32[8]{0:T(128)S(1)} %copy-done.8, bf16[16,1152]{1,0:T(8,128)(2,1)S(1)} %shard_map.101.rest_0_, bf16[16,1152]{1,0:T(8,128)(2,1)S(1)} %collective-permute-done.4.rest_1_, ...), custom_call_target="tpu_custom_call" | custom-call | flops 1375731712 | bytes 5373952 | tf_op jit(solution)/shard_map/pallas_call | solution.py:321
  43.4 1.0 collective-permute-start.9
  44.3 0.7 collective-permute-start.8
  45.0 1.5 %collective-permute-start.7 = (bf16[16,4224]{1,0:T(8,128)(2,1)S(1)}, bf16[16,4224]{1,0:T(8,128)(2,1)S(1)}, u32[]{:S(2)}, u32[]{:S(2)}) collective-permute-start(bf16[16,4224]{1,0:T(8,128)(2,1)S(1)} %shard_map.102.after_ref.rest_0_), channel_id=1, source_target_pairs={{0,1},{1,2},{2,3},{3,0},{4,5},{5,6},{6,7},{7,4},{8,9},{9,10},{10,1... | collective-permute-start | bytes 405512 | tf_op jit(solution)/shard_map/ppermute | solution.py:495
  46.6 7.1 %shard_map.103.rest_4_ = bf16[10,256,4096]{2,1,0:T(8,128)(2,1)S(1)} custom-call(bf16[1,4096,4096]{2,1,0:T(8,128)(2,1)} %w_ref.15, bf16[16,4224]{1,0:T(8,128)(2,1)S(1)} %shard_map.102.after_ref.rest_0_), custom_call_target="tpu_custom_call" | custom-call | bytes 20971520 | tf_op jit(solution)/shard_map/pallas_call | solution.py:75
  53.8 1.6 %collective-permute-done.8.rest_2_ = bf16[16,4224]{1,0:T(8,128)(2,1)S(1)} collective-permute-done((bf16[16,4224]{1,0:T(8,128)(2,1)S(1)}, bf16[16,4224]{1,0:T(8,128)(2,1)S(1)}, u32[]{:S(2)}, u32[]{:S(2)}) %collective-permute-start.8) | collective-permute-done | bytes 135200 | tf_op jit(solution)/shard_map/ppermute | solution.py:495
  55.3 7.0 %shard_map.104 = (bf16[8,4096]{1,0:T(8,128)(2,1)S(1)}, bf16[8,4096]{1,0:T(8,128)(2,1)S(1)}) custom-call(bf16[16,16]{1,0:T(8,128)(2,1)S(1)} %get-tuple-element.34.turn_ref.refs_4_, bf16[1,4096,4096]{2,1,0:T(8,128)(2,1)} %w_ref.15, bf16[16,4224]{1,0:T(8,128)(2,1)S(1)} %shard_map.102.after_ref.rest_0_, bf16[16,4224]{1,0:T(8,128)(2,1)S(1)} %collective-permute-done.7.rest_1_, ...), custom_call_target="tpu_custom_call" | custom-call | flops 536870912 | bytes 12582912 | tf_op jit(solution)/shard_map/pallas_call | solution.py:394
  62.5 1.6 %collective-permute-start.11 = (bf16[8,4096]{1,0:T(8,128)(2,1)S(1)}, bf16[8,4096]{1,0:T(8,128)(2,1)S(1)}, u32[]{:S(2)}, u32[]{:S(2)}) collective-permute-start(bf16[8,4096]{1,0:T(8,128)(2,1)S(1)} %get-tuple-element.24), channel_id=1, source_target_pairs={{0,8},{4,12},{8,0},{12,4},{1,9},{5,13},{9,1},{13,5},{2,10},{6,14},... | collective-permute-start | bytes 196616 | tf_op jit(solution)/shard_map/ppermute | solution.py:561
  64.3 4.5 %shard_map.105.refs_7_.rest_0_ = bf16[5,256,4608]{2,1,0:T(8,128)(2,1)S(1)} custom-call(bf16[1,4096,4608]{2,1,0:T(8,128)(2,1)} %w_ref.13, bf16[8,4096]{1,0:T(8,128)(2,1)S(1)} %get-tuple-element.23.after_ref.refs_0_), custom_call_target="tpu_custom_call" | custom-call | bytes 11796480 | tf_op jit(solution)/shard_map/pallas_call | solution.py:75
  69.1 2.5 %collective-permute-start.14 = (bf16[8,4224]{1,0:T(8,128)(2,1)S(1)}, bf16[8,4224]{1,0:T(8,128)(2,1)S(1)}, u32[]{:S(2)}, u32[]{:S(2)}) collective-permute-start(bf16[8,4224]{1,0:T(8,128)(2,1)S(1)} %get-tuple-element.25), channel_id=1, source_target_pairs={{0,24},{4,28},{8,16},{12,20},{24,0},{28,4},{16,8},{20,12},{1,25},{... | collective-permute-start | bytes 202760 | tf_op jit(solution)/shard_map/ppermute | solution.py:574
  71.5 0.5 collective-permute-start.13
  72.1 1.5 %collective-permute-start.18 = (f32[8,4096]{1,0:T(8,128)S(1)}, f32[8,4096]{1,0:T(8,128)S(1)}, u32[]{:S(2)}, u32[]{:S(2)}) collective-permute-start(f32[8,4096]{1,0:T(8,128)S(1)} %get-tuple-element.26.after_ref.refs_5_), channel_id=1, source_target_pairs={{0,16},{16,0},{1,17},{17,1},{2,18},{18,2},{3,19},{19,3},{4,20},{20... | collective-permute-start | bytes 393224 | tf_op jit(solution)/shard_map/ppermute | solution.py:578
  73.6 3.1 %shard_map.107.rest_1_ = bf16[3,256,4608]{2,1,0:T(8,128)(2,1)S(1)} custom-call(bf16[1,4096,4608]{2,1,0:T(8,128)(2,1)} %w_ref.13, f32[8,4096]{1,0:T(8,128)S(1)} %get-tuple-element.26.after_ref.refs_5_), custom_call_target="tpu_custom_call" | custom-call | bytes 7077888 | tf_op jit(solution)/shard_map/pallas_call | solution.py:75
  76.7 7.2 %shard_map.108 = (f32[16,1280]{1,0:T(8,128)S(1)}, f32[16,1280]{1,0:T(8,128)S(1)}, f32[16,1280]{1,0:T(8,128)S(1)}, f32[16,1280]{1,0:T(8,128)S(1)}) custom-call(s32[1]{0:T(128)} %bitcast.2.me_ref, bf16[16,4224]{1,0:T(8,128)(2,1)S(1)} %pad_maximum_fusion.x_ref, bf16[16,16]{1,0:T(8,128)(2,1)S(1)} %get-tuple-element.33.aux_ref, bf16[1,4096,4608]{2,1,0:T(8,128)(2,1)} %w_ref.13, ...), custom_call_target="tpu_custom_call" | custom-call | flops 603979776 | bytes 18874368 | tf_op jit(solution)/shard_map/pallas_call | solution.py:151
  83.9 0.8 collective-permute-start.15
  84.8 0.8 collective-permute-start.16
  85.6 1.9 %collective-permute-start.17 = (f32[16,1280]{1,0:T(8,128)S(1)}, f32[16,1280]{1,0:T(8,128)S(1)}, u32[]{:S(2)}, u32[]{:S(2)}) collective-permute-start(f32[16,1280]{1,0:T(8,128)S(1)} %get-tuple-element.30), channel_id=1, source_target_pairs={{0,1},{1,2},{2,3},{3,0},{4,5},{5,6},{6,7},{7,4},{8,9},{9,10},{10,1... | collective-permute-start | bytes 245768 | tf_op jit(solution)/shard_map/ppermute | solution.py:487
  87.5 1.1 collective-permute-done.15.refs_1_
  88.6 4.5 %collective-permute-done.16.refs_2_ = f32[16,1280]{1,0:T(8,128)S(1)} collective-permute-done((f32[16,1280]{1,0:T(8,128)S(1)}, f32[16,1280]{1,0:T(8,128)S(1)}, u32[]{:S(2)}, u32[]{:S(2)}) %collective-permute-start.16) | collective-permute-done | bytes 81952 | tf_op jit(solution)/shard_map/ppermute | solution.py:487
  93.3 1.0 collective-permute-start.21
  94.7 2.0 %collective-permute-start.19 = (bf16[16,1152]{1,0:T(8,128)(2,1)S(1)}, bf16[16,1152]{1,0:T(8,128)(2,1)S(1)}, u32[]{:S(2)}, u32[]{:S(2)}) collective-permute-start(bf16[16,1152]{1,0:T(8,128)(2,1)S(1)} %shard_map.109.rest_0_), channel_id=1, source_target_pairs={{0,1},{1,2},{2,3},{3,0},{4,5},{5,6},{6,7},{7,4},{8,9},{9,10},{10,1... | collective-permute-start | bytes 110600 | tf_op jit(solution)/shard_map/ppermute | solution.py:495
  96.6 0.7 collective-permute-done.21.rest_3_
  97.3 1.8 %collective-permute-done.20.rest_2_ = bf16[16,1152]{1,0:T(8,128)(2,1)S(1)} collective-permute-done((bf16[16,1152]{1,0:T(8,128)(2,1)S(1)}, bf16[16,1152]{1,0:T(8,128)(2,1)S(1)}, u32[]{:S(2)}, u32[]{:S(2)}) %collective-permute-start.20) | collective-permute-done | bytes 36896 | tf_op jit(solution)/shard_map/ppermute | solution.py:495
  99.2 1.3 collective-permute-done.19.rest_1_
  100.4 5.9 %shard_map.110.after_ref.rest_0_ = bf16[16,4224]{1,0:T(8,128)(2,1)S(1)} custom-call(s32[1]{0:T(128)} %bitcast.2.me_ref, s32[8]{0:T(128)S(1)} %copy-done.7, s32[8]{0:T(128)S(1)} %copy-done.8, bf16[16,1152]{1,0:T(8,128)(2,1)S(1)} %shard_map.109.rest_0_, bf16[16,1152]{1,0:T(8,128)(2,1)S(1)} %collective-permute-done.19.rest_1_, ...), custom_call_target="tpu_custom_call" | custom-call | flops 1375731712 | bytes 5373952 | tf_op jit(solution)/shard_map/pallas_call | solution.py:321
  106.4 1.2 collective-permute-start.24
  108.1 1.1 collective-permute-start.22
  109.2 7.1 %shard_map.111.rest_4_ = bf16[10,256,4096]{2,1,0:T(8,128)(2,1)S(1)} custom-call(bf16[1,4096,4096]{2,1,0:T(8,128)(2,1)} %w_ref.15, bf16[16,4224]{1,0:T(8,128)(2,1)S(1)} %shard_map.110.after_ref.rest_0_), custom_call_target="tpu_custom_call" | custom-call | bytes 20971520 | tf_op jit(solution)/shard_map/pallas_call | solution.py:75
  116.3 3.1 %collective-permute-done.23.rest_2_ = bf16[16,4224]{1,0:T(8,128)(2,1)S(1)} collective-permute-done((bf16[16,4224]{1,0:T(8,128)(2,1)S(1)}, bf16[16,4224]{1,0:T(8,128)(2,1)S(1)}, u32[]{:S(2)}, u32[]{:S(2)}) %collective-permute-start.23) | collective-permute-done | bytes 135200 | tf_op jit(solution)/shard_map/ppermute | solution.py:495
  119.4 7.0 %shard_map.112 = (bf16[8,4096]{1,0:T(8,128)(2,1)S(1)}, bf16[8,4096]{1,0:T(8,128)(2,1)S(1)}) custom-call(bf16[16,16]{1,0:T(8,128)(2,1)S(1)} %get-tuple-element.34.turn_ref.refs_4_, bf16[1,4096,4096]{2,1,0:T(8,128)(2,1)} %w_ref.15, bf16[16,4224]{1,0:T(8,128)(2,1)S(1)} %shard_map.110.after_ref.rest_0_, bf16[16,4224]{1,0:T(8,128)(2,1)S(1)} %collective-permute-done.22.rest_1_, ...), custom_call_target="tpu_custom_call" | custom-call | flops 536870912 | bytes 12582912 | tf_op jit(solution)/shard_map/pallas_call | solution.py:394
  126.5 0.7 collective-permute-start.26
  127.3 1.1 collective-permute-start.25
  128.4 0.8 collective-permute-done.25.refs_1_
  129.3 1.0 collective-permute-done.27.refs_3_
  130.3 1.2 collective-permute-done.26.refs_2_
  131.5 1.2 shard_map.113
  (44 shorter events, 2.0 us)
Async XLA Ops:
  0.0 35.8 %copy-start.4 = (bf16[1,2,2,512,128]{4,3,2,1,0:T(8,128)(2,1)S(1)}, bf16[1,2,2,512,128]{4,3,2,1,0:T(8,128)(2,1)}, u32[]{:S(2)}) copy-start(bf16[1,2,2,512,128]{4,3,2,1,0:T(8,128)(2,1)} %rest_7_.3) | copy-start | bytes 1572868
  0.0 35.8 %copy-start.3 = (bf16[1,2,2,512,128]{4,3,2,1,0:T(8,128)(2,1)S(1)}, bf16[1,2,2,512,128]{4,3,2,1,0:T(8,128)(2,1)}, u32[]{:S(2)}) copy-start(bf16[1,2,2,512,128]{4,3,2,1,0:T(8,128)(2,1)} %rest_6_.3) | copy-start | bytes 1572868
  0.0 35.8 %copy-start = (bf16[1,2,4096,128]{3,2,1,0:T(8,128)(2,1)S(1)}, bf16[1,2,4096,128]{3,2,1,0:T(8,128)(2,1)}, u32[]{:S(2)}) copy-start(bf16[1,2,4096,128]{3,2,1,0:T(8,128)(2,1)} %rest_4_.3) | copy-start | bytes 6291460
  0.0 1.1 copy-start.5
  1.1 34.7 %copy-start.7 = (s32[8]{0:T(128)S(1)}, s32[8]{0:T(128)}, u32[]{:S(2)}) copy-start(s32[8]{0:T(128)} %order_ref.3) | copy-start | bytes 100
  1.1 34.7 %copy-start.8 = (s32[8]{0:T(128)S(1)}, s32[8]{0:T(128)}, u32[]{:S(2)}) copy-start(s32[8]{0:T(128)} %lengths_ref.3) | copy-start | bytes 100
  14.9 10.1 %collective-permute-start = (f32[16,1280]{1,0:T(8,128)}, f32[16,1280]{1,0:T(8,128)S(1)}, u32[]{:S(2)}, u32[]{:S(2)}) collective-permute-start(f32[16,1280]{1,0:T(8,128)} %get-tuple-element.20), channel_id=1, source_target_pairs={{0,3},{1,0},{2,1},{3,2},{4,7},{5,4},{6,5},{7,6},{8,11},{9,8},{10,9... | collective-permute-start | bytes 245768 | tf_op jit(solution)/shard_map/ppermute | solution.py:487
  20.0 7.7 %collective-permute-start.1 = (f32[16,1280]{1,0:T(8,128)}, f32[16,1280]{1,0:T(8,128)S(1)}, u32[]{:S(2)}, u32[]{:S(2)}) collective-permute-start(f32[16,1280]{1,0:T(8,128)} %get-tuple-element.21), channel_id=1, source_target_pairs={{0,2},{1,3},{2,0},{3,1},{4,6},{5,7},{6,4},{7,5},{8,10},{9,11},{10,... | collective-permute-start | bytes 245768 | tf_op jit(solution)/shard_map/ppermute | solution.py:487
  20.0 7.7 %collective-permute-start.2 = (f32[16,1280]{1,0:T(8,128)}, f32[16,1280]{1,0:T(8,128)S(1)}, u32[]{:S(2)}, u32[]{:S(2)}) collective-permute-start(f32[16,1280]{1,0:T(8,128)} %get-tuple-element.22), channel_id=1, source_target_pairs={{0,1},{1,2},{2,3},{3,0},{4,5},{5,6},{6,7},{7,4},{8,9},{9,10},{10,1... | collective-permute-start | bytes 245768 | tf_op jit(solution)/shard_map/ppermute | solution.py:487
  21.1 3.9 %collective-permute-start.3 = (bf16[1,4096]{1,0:T(2,128)(2,1)}, bf16[1,4096]{1,0:T(2,128)(2,1)S(1)}, u32[]{:S(2)}, u32[]{:S(2)}) collective-permute-start(bf16[1,4096]{1,0:T(2,128)(2,1)} %aux_ref.1), channel_id=1, source_target_pairs={{0,16},{16,0},{1,17},{17,1},{2,18},{18,2},{3,19},{19,3},{4,20},{20... | collective-permute-start | bytes 24584 | tf_op jit(solution)/shard_map/ppermute | solution.py:535
  27.9 4.1 %collective-permute-start.6 = (bf16[16,1152]{1,0:T(8,128)(2,1)S(1)}, bf16[16,1152]{1,0:T(8,128)(2,1)S(1)}, u32[]{:S(2)}, u32[]{:S(2)}) collective-permute-start(bf16[16,1152]{1,0:T(8,128)(2,1)S(1)} %shard_map.101.rest_0_), channel_id=1, source_target_pairs={{0,3},{1,0},{2,1},{3,2},{4,7},{5,4},{6,5},{7,6},{8,11},{9,8},{10,9... | collective-permute-start | bytes 110600 | tf_op jit(solution)/shard_map/ppermute | solution.py:495
  30.0 4.9 %collective-permute-start.5 = (bf16[16,1152]{1,0:T(8,128)(2,1)S(1)}, bf16[16,1152]{1,0:T(8,128)(2,1)S(1)}, u32[]{:S(2)}, u32[]{:S(2)}) collective-permute-start(bf16[16,1152]{1,0:T(8,128)(2,1)S(1)} %shard_map.101.rest_0_), channel_id=1, source_target_pairs={{0,2},{1,3},{2,0},{3,1},{4,6},{5,7},{6,4},{7,5},{8,10},{9,11},{10,... | collective-permute-start | bytes 110600 | tf_op jit(solution)/shard_map/ppermute | solution.py:495
  30.0 5.8 %collective-permute-start.4 = (bf16[16,1152]{1,0:T(8,128)(2,1)S(1)}, bf16[16,1152]{1,0:T(8,128)(2,1)S(1)}, u32[]{:S(2)}, u32[]{:S(2)}) collective-permute-start(bf16[16,1152]{1,0:T(8,128)(2,1)S(1)} %shard_map.101.rest_0_), channel_id=1, source_target_pairs={{0,1},{1,2},{2,3},{3,0},{4,5},{5,6},{6,7},{7,4},{8,9},{9,10},{10,1... | collective-permute-start | bytes 110600 | tf_op jit(solution)/shard_map/ppermute | solution.py:495
  35.8 1.6 %copy-start.1 = (bf16[1,2,4096,128]{3,2,1,0:T(8,128)(2,1)S(1)}, bf16[1,2,4096,128]{3,2,1,0:T(8,128)(2,1)}, u32[]{:S(2)}) copy-start(bf16[1,2,4096,128]{3,2,1,0:T(8,128)(2,1)} %rest_5_.3) | copy-start | bytes 6291460
  43.4 10.4 %collective-permute-start.9 = (bf16[16,4224]{1,0:T(8,128)(2,1)S(1)}, bf16[16,4224]{1,0:T(8,128)(2,1)S(1)}, u32[]{:S(2)}, u32[]{:S(2)}) collective-permute-start(bf16[16,4224]{1,0:T(8,128)(2,1)S(1)} %shard_map.102.after_ref.rest_0_), channel_id=1, source_target_pairs={{0,3},{1,0},{2,1},{3,2},{4,7},{5,4},{6,5},{7,6},{8,11},{9,8},{10,9... | collective-permute-start | bytes 405512 | tf_op jit(solution)/shard_map/ppermute | solution.py:495
  44.3 11.0 %collective-permute-start.8 = (bf16[16,4224]{1,0:T(8,128)(2,1)S(1)}, bf16[16,4224]{1,0:T(8,128)(2,1)S(1)}, u32[]{:S(2)}, u32[]{:S(2)}) collective-permute-start(bf16[16,4224]{1,0:T(8,128)(2,1)S(1)} %shard_map.102.after_ref.rest_0_), channel_id=1, source_target_pairs={{0,2},{1,3},{2,0},{3,1},{4,6},{5,7},{6,4},{7,5},{8,10},{9,11},{10,... | collective-permute-start | bytes 405512 | tf_op jit(solution)/shard_map/ppermute | solution.py:495
  45.0 10.3 %collective-permute-start.7 = (bf16[16,4224]{1,0:T(8,128)(2,1)S(1)}, bf16[16,4224]{1,0:T(8,128)(2,1)S(1)}, u32[]{:S(2)}, u32[]{:S(2)}) collective-permute-start(bf16[16,4224]{1,0:T(8,128)(2,1)S(1)} %shard_map.102.after_ref.rest_0_), channel_id=1, source_target_pairs={{0,1},{1,2},{2,3},{3,0},{4,5},{5,6},{6,7},{7,4},{8,9},{9,10},{10,1... | collective-permute-start | bytes 405512 | tf_op jit(solution)/shard_map/ppermute | solution.py:495
  62.4 6.4 %collective-permute-start.12 = (bf16[8,4096]{1,0:T(8,128)(2,1)S(1)}, bf16[8,4096]{1,0:T(8,128)(2,1)S(1)}, u32[]{:S(2)}, u32[]{:S(2)}) collective-permute-start(bf16[8,4096]{1,0:T(8,128)(2,1)S(1)} %get-tuple-element.24), channel_id=1, source_target_pairs={{0,12},{4,8},{8,4},{12,0},{1,13},{5,9},{9,5},{13,1},{2,14},{6,10},... | collective-permute-start | bytes 196616 | tf_op jit(solution)/shard_map/ppermute | solution.py:561
  62.5 6.4 %collective-permute-start.11 = (bf16[8,4096]{1,0:T(8,128)(2,1)S(1)}, bf16[8,4096]{1,0:T(8,128)(2,1)S(1)}, u32[]{:S(2)}, u32[]{:S(2)}) collective-permute-start(bf16[8,4096]{1,0:T(8,128)(2,1)S(1)} %get-tuple-element.24), channel_id=1, source_target_pairs={{0,8},{4,12},{8,0},{12,4},{1,9},{5,13},{9,1},{13,5},{2,10},{6,14},... | collective-permute-start | bytes 196616 | tf_op jit(solution)/shard_map/ppermute | solution.py:561
  64.0 4.8 %copy-start.6 = (bf16[2,8,4096]{2,1,0:T(8,128)(2,1)S(1)}, bf16[2,8,4096]{2,1,0:T(8,128)(2,1)}, u32[]{:S(2)}) copy-start(bf16[2,8,4096]{2,1,0:T(8,128)(2,1)} %param.10) | copy-start | bytes 393220
  64.0 4.8 %collective-permute-start.10 = (bf16[8,4096]{1,0:T(8,128)(2,1)S(1)}, bf16[8,4096]{1,0:T(8,128)(2,1)S(1)}, u32[]{:S(2)}, u32[]{:S(2)}) collective-permute-start(bf16[8,4096]{1,0:T(8,128)(2,1)S(1)} %get-tuple-element.23.after_ref.refs_0_), channel_id=1, source_target_pairs={{0,4},{4,0},{8,12},{12,8},{1,5},{5,1},{9,13},{13,9},{2,6},{6,2},{1... | collective-permute-start | bytes 196616 | tf_op jit(solution)/shard_map/ppermute | solution.py:561
  69.1 7.6 %collective-permute-start.14 = (bf16[8,4224]{1,0:T(8,128)(2,1)S(1)}, bf16[8,4224]{1,0:T(8,128)(2,1)S(1)}, u32[]{:S(2)}, u32[]{:S(2)}) collective-permute-start(bf16[8,4224]{1,0:T(8,128)(2,1)S(1)} %get-tuple-element.25), channel_id=1, source_target_pairs={{0,24},{4,28},{8,16},{12,20},{24,0},{28,4},{16,8},{20,12},{1,25},{... | collective-permute-start | bytes 202760 | tf_op jit(solution)/shard_map/ppermute | solution.py:574
  71.5 5.2 %collective-permute-start.13 = (bf16[8,4224]{1,0:T(8,128)(2,1)S(1)}, bf16[8,4224]{1,0:T(8,128)(2,1)S(1)}, u32[]{:S(2)}, u32[]{:S(2)}) collective-permute-start(bf16[8,4224]{1,0:T(8,128)(2,1)S(1)} %get-tuple-element.25), channel_id=1, source_target_pairs={{0,16},{4,20},{8,24},{12,28},{16,0},{20,4},{24,8},{28,12},{1,17},{... | collective-permute-start | bytes 202760 | tf_op jit(solution)/shard_map/ppermute | solution.py:574
  72.1 15.4 %collective-permute-start.18 = (f32[8,4096]{1,0:T(8,128)S(1)}, f32[8,4096]{1,0:T(8,128)S(1)}, u32[]{:S(2)}, u32[]{:S(2)}) collective-permute-start(f32[8,4096]{1,0:T(8,128)S(1)} %get-tuple-element.26.after_ref.refs_5_), channel_id=1, source_target_pairs={{0,16},{16,0},{1,17},{17,1},{2,18},{18,2},{3,19},{19,3},{4,20},{20... | collective-permute-start | bytes 393224 | tf_op jit(solution)/shard_map/ppermute | solution.py:578
  76.7 23.7 %copy-start.2 = (bf16[1,2,4096,128]{3,2,1,0:T(8,128)(2,1)S(1)}, bf16[1,2,4096,128]{3,2,1,0:T(8,128)(2,1)}, u32[]{:S(2)}) copy-start(bf16[1,2,4096,128]{3,2,1,0:T(8,128)(2,1)} %rest_5_.3) | copy-start | bytes 6291460
  83.9 4.7 %collective-permute-start.15 = (f32[16,1280]{1,0:T(8,128)S(1)}, f32[16,1280]{1,0:T(8,128)S(1)}, u32[]{:S(2)}, u32[]{:S(2)}) collective-permute-start(f32[16,1280]{1,0:T(8,128)S(1)} %get-tuple-element.28), channel_id=1, source_target_pairs={{0,3},{1,0},{2,1},{3,2},{4,7},{5,4},{6,5},{7,6},{8,11},{9,8},{10,9... | collective-permute-start | bytes 245768 | tf_op jit(solution)/shard_map/ppermute | solution.py:487
  84.8 8.4 %collective-permute-start.16 = (f32[16,1280]{1,0:T(8,128)S(1)}, f32[16,1280]{1,0:T(8,128)S(1)}, u32[]{:S(2)}, u32[]{:S(2)}) collective-permute-start(f32[16,1280]{1,0:T(8,128)S(1)} %get-tuple-element.29), channel_id=1, source_target_pairs={{0,2},{1,3},{2,0},{3,1},{4,6},{5,7},{6,4},{7,5},{8,10},{9,11},{10,... | collective-permute-start | bytes 245768 | tf_op jit(solution)/shard_map/ppermute | solution.py:487
  85.6 7.6 %collective-permute-start.17 = (f32[16,1280]{1,0:T(8,128)S(1)}, f32[16,1280]{1,0:T(8,128)S(1)}, u32[]{:S(2)}, u32[]{:S(2)}) collective-permute-start(f32[16,1280]{1,0:T(8,128)S(1)} %get-tuple-element.30), channel_id=1, source_target_pairs={{0,1},{1,2},{2,3},{3,0},{4,5},{5,6},{6,7},{7,4},{8,9},{9,10},{10,1... | collective-permute-start | bytes 245768 | tf_op jit(solution)/shard_map/ppermute | solution.py:487
  93.3 4.1 %collective-permute-start.21 = (bf16[16,1152]{1,0:T(8,128)(2,1)S(1)}, bf16[16,1152]{1,0:T(8,128)(2,1)S(1)}, u32[]{:S(2)}, u32[]{:S(2)}) collective-permute-start(bf16[16,1152]{1,0:T(8,128)(2,1)S(1)} %shard_map.109.rest_0_), channel_id=1, source_target_pairs={{0,3},{1,0},{2,1},{3,2},{4,7},{5,4},{6,5},{7,6},{8,11},{9,8},{10,9... | collective-permute-start | bytes 110600 | tf_op jit(solution)/shard_map/ppermute | solution.py:495
  94.3 4.9 %collective-permute-start.20 = (bf16[16,1152]{1,0:T(8,128)(2,1)S(1)}, bf16[16,1152]{1,0:T(8,128)(2,1)S(1)}, u32[]{:S(2)}, u32[]{:S(2)}) collective-permute-start(bf16[16,1152]{1,0:T(8,128)(2,1)S(1)} %shard_map.109.rest_0_), channel_id=1, source_target_pairs={{0,2},{1,3},{2,0},{3,1},{4,6},{5,7},{6,4},{7,5},{8,10},{9,11},{10,... | collective-permute-start | bytes 110600 | tf_op jit(solution)/shard_map/ppermute | solution.py:495
  94.7 5.8 %collective-permute-start.19 = (bf16[16,1152]{1,0:T(8,128)(2,1)S(1)}, bf16[16,1152]{1,0:T(8,128)(2,1)S(1)}, u32[]{:S(2)}, u32[]{:S(2)}) collective-permute-start(bf16[16,1152]{1,0:T(8,128)(2,1)S(1)} %shard_map.109.rest_0_), channel_id=1, source_target_pairs={{0,1},{1,2},{2,3},{3,0},{4,5},{5,6},{6,7},{7,4},{8,9},{9,10},{10,1... | collective-permute-start | bytes 110600 | tf_op jit(solution)/shard_map/ppermute | solution.py:495
  106.4 9.9 %collective-permute-start.24 = (bf16[16,4224]{1,0:T(8,128)(2,1)S(1)}, bf16[16,4224]{1,0:T(8,128)(2,1)S(1)}, u32[]{:S(2)}, u32[]{:S(2)}) collective-permute-start(bf16[16,4224]{1,0:T(8,128)(2,1)S(1)} %shard_map.110.after_ref.rest_0_), channel_id=1, source_target_pairs={{0,3},{1,0},{2,1},{3,2},{4,7},{5,4},{6,5},{7,6},{8,11},{9,8},{10,9... | collective-permute-start | bytes 405512 | tf_op jit(solution)/shard_map/ppermute | solution.py:495
  107.6 11.8 %collective-permute-start.23 = (bf16[16,4224]{1,0:T(8,128)(2,1)S(1)}, bf16[16,4224]{1,0:T(8,128)(2,1)S(1)}, u32[]{:S(2)}, u32[]{:S(2)}) collective-permute-start(bf16[16,4224]{1,0:T(8,128)(2,1)S(1)} %shard_map.110.after_ref.rest_0_), channel_id=1, source_target_pairs={{0,2},{1,3},{2,0},{3,1},{4,6},{5,7},{6,4},{7,5},{8,10},{9,11},{10,... | collective-permute-start | bytes 405512 | tf_op jit(solution)/shard_map/ppermute | solution.py:495
  108.1 11.4 %collective-permute-start.22 = (bf16[16,4224]{1,0:T(8,128)(2,1)S(1)}, bf16[16,4224]{1,0:T(8,128)(2,1)S(1)}, u32[]{:S(2)}, u32[]{:S(2)}) collective-permute-start(bf16[16,4224]{1,0:T(8,128)(2,1)S(1)} %shard_map.110.after_ref.rest_0_), channel_id=1, source_target_pairs={{0,1},{1,2},{2,3},{3,0},{4,5},{5,6},{6,7},{7,4},{8,9},{9,10},{10,1... | collective-permute-start | bytes 405512 | tf_op jit(solution)/shard_map/ppermute | solution.py:495
  126.4 3.8 %collective-permute-start.27 = (bf16[8,4096]{1,0:T(8,128)(2,1)S(1)}, bf16[8,4096]{1,0:T(8,128)(2,1)S(1)}, u32[]{:S(2)}, u32[]{:S(2)}) collective-permute-start(bf16[8,4096]{1,0:T(8,128)(2,1)S(1)} %get-tuple-element.32), channel_id=1, source_target_pairs={{0,12},{4,8},{8,4},{12,0},{1,13},{5,9},{9,5},{13,1},{2,14},{6,10},... | collective-permute-start | bytes 196616 | tf_op jit(solution)/shard_map/ppermute | solution.py:561
  126.5 5.0 %collective-permute-start.26 = (bf16[8,4096]{1,0:T(8,128)(2,1)S(1)}, bf16[8,4096]{1,0:T(8,128)(2,1)S(1)}, u32[]{:S(2)}, u32[]{:S(2)}) collective-permute-start(bf16[8,4096]{1,0:T(8,128)(2,1)S(1)} %get-tuple-element.32), channel_id=1, source_target_pairs={{0,8},{4,12},{8,0},{12,4},{1,9},{5,13},{9,1},{13,5},{2,10},{6,14},... | collective-permute-start | bytes 196616 | tf_op jit(solution)/shard_map/ppermute | solution.py:561
  127.3 2.0 %collective-permute-start.25 = (bf16[8,4096]{1,0:T(8,128)(2,1)S(1)}, bf16[8,4096]{1,0:T(8,128)(2,1)S(1)}, u32[]{:S(2)}, u32[]{:S(2)}) collective-permute-start(bf16[8,4096]{1,0:T(8,128)(2,1)S(1)} %get-tuple-element.31.refs_0_), channel_id=1, source_target_pairs={{0,4},{4,0},{8,12},{12,8},{1,5},{5,1},{9,13},{13,9},{2,6},{6,2},{1... | collective-permute-start | bytes 196616 | tf_op jit(solution)/shard_map/ppermute | solution.py:561

commit v4 on v3

--- a/solution.py
+++ b/solution.py
@@ -160,7 +160,7 @@
             pltpu.VMEM((left, depth, columns), BF16),
             pltpu.SemaphoreType.DMA((left,)),
         ],
-        compiler_params=params(6 + (2 * left * depth * columns >> 20)),
+        compiler_params=params(3 + (2 * left * depth * columns >> 20)),
         cost_estimate=pl.CostEstimate(
             flops=2 * rows * model * columns,
             bytes_accessed=2 * left * depth * columns,
@@ -196,22 +196,46 @@
     blocks, batch, group, me_ref, order_ref, lengths_ref, *rest
 ):
     parts = rest[:blocks]
-    pre_k, pre_v, suf_k, suf_v = rest[blocks : blocks + 4]
-    out_ref, q_ref, s_ref, stats_ref = rest[blocks + 4 :]
-    head = pl.program_id(0)
+    sources = rest[blocks : blocks + 4]
+    out_ref, q_ref, s_ref, stats_ref, *caches, sem_ref = rest[blocks + 4 :]
+    heads = caches[0].shape[0]
+
+    def cache_copy(n, head):
+        return pltpu.make_async_copy(sources[n].at[0, head], caches[n].at[head], sem_ref.at[n, head])
+
+    for n in range(4):
+        cache_copy(n, 0).start()
     me = me_ref[0]
+    hd = q_ref.shape[2]
+    own = parts[0].shape[1] // hd
+    for k in range(blocks):
+        at = lax.rem(me - k + blocks, blocks)
+        for i in range(own):
+            q_ref[at * own + i] = parts[k][:, i * hd : (i + 1) * hd]
+
+    @pl.loop(0, heads)
+    def _(head):
+        def following():
+            @pl.when(head + 1 < heads)
+            def _():
+                for n in range(4):
+                    cache_copy(n, head + 1).start()
+
+        attend_head(
+            head, me, batch, group, order_ref, lengths_ref, *[cache.at[head] for cache in caches],
+            lambda n: cache_copy(n, head).wait(),
+            following,
+            heads * group, out_ref, q_ref, s_ref, stats_ref,
+        )
+
+
+def attend_head(
+    head, me, batch, group, order_ref, lengths_ref, pre_k, suf_k, pre_v, suf_v, wait, following,
+    heads, out_ref, q_ref, s_ref, stats_ref,
+):
     rows, hd = q_ref.shape[1], pre_k.shape[1]
+    scale = hd**-0.5 * math.log2(math.e)
     slots = group + 2
-    own = parts[0].shape[1] // hd
-    scale = hd**-0.5 * math.log2(math.e)
-
-    @pl.when(head == 0)
-    def _():
-        for k in range(blocks):
-            at = lax.rem(me - k + blocks, blocks)
-            for i in range(own):
-                q_ref[at * own + i] = parts[k][:, i * hd : (i + 1) * hd]
-
     first = head * slots
     q = jnp.concatenate([q_ref[first + g] for g in range(group)], axis=0)
     count = group * rows
@@ -243,10 +267,12 @@
 
     pieces = []
     start = 0
+    wait(0)
     for i in range(0, positions, step):
         top = keep(top, dot_t(q, pre_k[i : i + step]), start)
         pieces.append((start, step, pre_v, None, i))
         start += step
+    wait(1)
     for s in range(samples):
         sample = me * samples + s
         row = jnp.int32(0)
@@ -275,6 +301,9 @@
     row_max = jnp.max(top, axis=1, keepdims=True) * scale
     total = jnp.zeros((count, LANES), F32)
     mixed = jnp.zeros((count, hd), F32)
+    wait(2)
+    wait(3)
+    following()
     for start, size, values, s, i in pieces:
         weights = jnp.exp2(s_ref[:, start : start + size] * scale - row_max)
         for lane in range(0, size, LANES):
@@ -291,7 +320,6 @@
     level = row_max + jnp.log2(total)
     terms = split3(level)
 
-    heads = pl.num_programs(0) * group
     mixed = mixed.astype(BF16)
     lane = lax.broadcasted_iota(jnp.int32, stats_ref.shape, 1) - first_lane(head, group)
     stats = jnp.where(head == 0, 0.0, stats_ref[...])
@@ -308,7 +336,7 @@
     return head * group
 
 
-def attend(parts, keys, values, suffix_keys, suffix_values, me, order, lengths, group):
+def attend(parts, keys, values, suffix_keys, suffix_values, me, order, lengths, group, limit):
     rows = parts[0].shape[0]
     heads, positions, hd = keys.shape[1:]
     samples, depth = suffix_keys.shape[2:4]
@@ -316,29 +344,28 @@
     width = heads * group * hd + stats
     total = positions + samples * depth + rows + (-rows % LANES)
     shape = jax.ShapeDtypeStruct((rows, width), BF16)
-    cache = pl.BlockSpec((None, None, positions, hd), lambda h, *_: (0, h, 0, 0))
-    suffix = pl.BlockSpec((None, None, samples, depth, hd), lambda h, *_: (0, h, 0, 0, 0))
     return pl.pallas_call(
         functools.partial(attend_kernel, len(parts), order.shape[0], group),
         out_shape=shape,
-        grid_spec=pltpu.PrefetchScalarGridSpec(
-            num_scalar_prefetch=3,
-            grid=(heads,),
-            in_specs=[whole(part.shape) for part in parts] + [cache, cache, suffix, suffix],
-            out_specs=whole(shape.shape),
-            scratch_shapes=[
-                pltpu.VMEM((heads * (group + 2), rows, hd), BF16),
-                pltpu.VMEM((group * rows, total), F32),
-                pltpu.VMEM((rows, stats), F32),
-            ],
-        ),
-        compiler_params=params(20 if group * rows * total < 1 << 21 else 48),
+        in_specs=[smem()] * 3 + [vmem()] * len(parts) + [hbm()] * 4,
+        out_specs=vmem(),
+        scratch_shapes=[
+            pltpu.VMEM((heads * (group + 2), rows, hd), BF16),
+            pltpu.VMEM((group * rows, total), F32),
+            pltpu.VMEM((rows, stats), F32),
+            pltpu.VMEM((heads, positions, hd), BF16),
+            pltpu.VMEM((heads, samples, depth, hd), BF16),
+            pltpu.VMEM((heads, positions, hd), BF16),
+            pltpu.VMEM((heads, samples, depth, hd), BF16),
+            pltpu.SemaphoreType.DMA((4, heads)),
+        ],
+        compiler_params=params(limit),
         cost_estimate=pl.CostEstimate(
             flops=4 * heads * group * rows * total * hd,
             bytes_accessed=4 * heads * total * hd,
             transcendentals=heads * group * rows * total,
         ),
-    )(me, order, lengths, *parts, keys, values, suffix_keys, suffix_values)
+    )(me, order, lengths, *parts, keys, suffix_keys, values, suffix_values)
 
 
 def merge(parts, heads, hd, store):
@@ -535,7 +562,6 @@
     next_gain = lax.ppermute(
         norm_gain, "section", [(s, (s - 1) % sections) for s in range(sections)]
     )
-
     x, aux, after = tokens_in.reshape(rows, columns), norm_gain, next_gain
     residual = (turn, x)
     result = None
@@ -544,26 +570,32 @@
     ready = []
     for layer in range(sections):
         fresh = layer == 0
+        last = layer + 1 == sections
+        parts = project(x, aux, w_qkv, ready, me if even else zero, ctx if even else 1, fresh)
+        if not fresh:
+            y, own = lax.optimization_barrier((y, parts[0]))
+            parts = [own, *parts[1:]]
+            after = own
+            residual = (
+                lax.ppermute(y, "section", [(layer - 1, layer), (layer, layer - 1)]),
+            )
         if even:
-            sent = project(x, aux, w_qkv, ready, me, ctx, fresh)
-            parts = back(sent, "ctx")
-            parts = around(normalize(parts, model, after), "ctx")
+            parts = around(normalize(back(parts, "ctx"), model, after), "ctx")
         else:
-            part = project(x, aux, w_qkv, ready, zero, 1, fresh)[0]
-            parts = [normalize([lax.psum(part, "ctx")], model, after)]
+            parts = [normalize([lax.psum(parts[0], "ctx")], model, after)]
         sent = attend(
             parts, prefix_keys, prefix_values, suffix_keys, suffix_values,
-            me, order, lengths, group,
+            me, order, lengths, group, 52 if fresh else 34,
         )
         held = load(w_out, 0, max(1, out_blocks * 10 // 16), out_depth, sent)
         sent = output(around(sent, "ctx"), turn, w_out, [held], groups, hd)
         parts = [sent[0]] + [
             lax.ppermute(sent[k // 2], "tp", [(n, n ^ k) for n in range(tp)]) for k in range(1, tp)
         ]
-        if layer + 1 == sections:
+        if last:
             place = jnp.stack([section == layer, tp_me % 2]).astype(jnp.int32)
             return finish(parts, residual, result, place, steps)
-        first = load(w_qkv, 0, max(1, in_blocks * 5 // 16), in_depth, sent[0])
+        first = load(w_qkv, 0, max(1, in_blocks * 4 // 16), in_depth, sent[0])
         y, message = add_up(parts, residual, next_gain, first)
         result = y if result is None else jnp.where(section == layer, y, result)
         here, there = layer * tp, (layer + 1) * tp
@@ -575,8 +607,6 @@
         second = load(w_qkv, first.shape[0], max(1, in_blocks * 3 // 16), in_depth, y)
         ready = [first, second]
         x, aux = jnp.concatenate(received, axis=0), unturn
-        residual = (lax.ppermute(y, "section", [(layer, layer + 1), (layer + 1, layer)]),)
-        after = residual[0]
 
 
 def solution(mesh):

time: 133 us -> 131 us (0.985)
  waiting for transfers between devices: 26.2 us -> 20 us
  starting transfers between devices: 33 us -> 38.8 us
  local copies, waits for them, and re-layouts: 2.67 us -> 1.03 us
    ppermute x12, waiting for transfers between devices: 12.3 us -> 4.12 us  [around(): lax.ppermute(part, axis, [(i, (i + k) % count) for i in range(count)])]
    ppermute x12, starting transfers between devices: 13.4 us -> 18.1 us  [around(): lax.ppermute(part, axis, [(i, (i + k) % count) for i in range(count)])]
    unnamed x18 -> x16, local copies, waits for them, and re-layouts: 2.67 us -> 1.03 us
    ppermute x6, waiting for transfers between devices: 8.43 us -> 9.98 us  [back(): lax.ppermute(parts[k], axis, [(i, (i - k) % count) for i in range(count)])]
  transfers between devices with their start and end apart: 28 -> 28, of which waited for: 14 -> 11; matrix products, arithmetic and copies ran while one was open for 0% -> 0% of each run, Pallas kernels for 22% -> 22%
where the time goes in v4:
time: 131 us
  Pallas kernels  70.5 us (54%)
  starting transfers between devices  38.8 us (30%)
  waiting for transfers between devices  20 us (15%)
    pallas_call x4, Pallas kernels, load(): pl.pallas_call(functools.partial(load_kernel, first), out_shape=jax.Shape...  21.2 us
    pallas_call x2, Pallas kernels, project(): pl.pallas_call(functools.partial(project_kernel, chunks, len(held), fresh...  21 us
    ppermute x12, starting transfers between devices, around(): lax.ppermute(part, axis, [(i, (i + k) % count) for i in range(count)])  18.1 us
    pallas_call x2, Pallas kernels, output(): pl.pallas_call(functools.partial(output_kernel, blocks, groups, len(held)...  14.1 us
    pallas_call x2, Pallas kernels, attend(): pl.pallas_call(functools.partial(attend_kernel, len(parts), order.shape[0...  12.7 us
    ppermute x6, starting transfers between devices, back(): lax.ppermute(parts[k], axis, [(i, (i - k) % count) for i in range(count)])  10.6 us
    ppermute x6, waiting for transfers between devices, back(): lax.ppermute(parts[k], axis, [(i, (i - k) % count) for i in range(count)])  9.98 us
    ppermute x6, starting transfers between devices, on_device(): lax.ppermute(sent[k // 2], 'tp', [(n, n ^ k) for n in range(tp)])  4.13 us
  transfers between devices with their start and end apart: 28, of which 11 were waited for; matrix products, arithmetic and copies ran while one was open for 0% of the time, Pallas kernels for 22%

profile of v4, /device:TPU:0, one launch (start us, length us, event | category | flops | bytes accessed | tf_op | source)
XLA Modules:
  0.0 130.8 jit_solution(14268793489789693106)
XLA Ops:
  0.0 1.0 copy-done.4
  1.0 13.2 %shard_map.100 = (f32[16,1280]{1,0:T(8,128)S(1)}, f32[16,1280]{1,0:T(8,128)S(1)}, f32[16,1280]{1,0:T(8,128)S(1)}, f32[16,1280]{1,0:T(8,128)S(1)}) custom-call(s32[1]{0:T(128)} %bitcast.2.me_ref, bf16[16,4096]{1,0:T(8,128)(2,1)S(1)} %bitcast.4, bf16[1,4096]{1,0:T(2,128)(2,1)} %aux_ref.1, bf16[1,4096,4608]{2,1,0:T(8,128)(2,1)} %w_ref.13), custom_call_target="tpu_custom_call" | custom-call | flops 603979776 | bytes 37748736 | tf_op jit(solution)/shard_map/pallas_call | solution.py:151
  14.2 5.1 %collective-permute-start = (f32[16,1280]{1,0:T(8,128)S(1)}, f32[16,1280]{1,0:T(8,128)S(1)}, u32[]{:S(2)}, u32[]{:S(2)}) collective-permute-start(f32[16,1280]{1,0:T(8,128)S(1)} %get-tuple-element.22), channel_id=1, source_target_pairs={{0,3},{1,0},{2,1},{3,2},{4,7},{5,4},{6,5},{7,6},{8,11},{9,8},{10,9... | collective-permute-start | bytes 245768 | tf_op jit(solution)/shard_map/ppermute | solution.py:514
  19.3 1.0 collective-permute-start.2
  20.3 1.5 %collective-permute-start.3 = (bf16[1,4096]{1,0:T(2,128)(2,1)}, bf16[1,4096]{1,0:T(2,128)(2,1)S(1)}, u32[]{:S(2)}, u32[]{:S(2)}) collective-permute-start(bf16[1,4096]{1,0:T(2,128)(2,1)} %aux_ref.1), channel_id=1, source_target_pairs={{0,16},{16,0},{1,17},{17,1},{2,18},{18,2},{3,19},{19,3},{4,20},{20... | collective-permute-start | bytes 24584 | tf_op jit(solution)/shard_map/ppermute | solution.py:562
  21.8 2.5 %collective-permute-done.3.refs_4_.refs_6_ = bf16[1,4096]{1,0:T(2,128)(2,1)S(1)} collective-permute-done((bf16[1,4096]{1,0:T(2,128)(2,1)}, bf16[1,4096]{1,0:T(2,128)(2,1)S(1)}, u32[]{:S(2)}, u32[]{:S(2)}) %collective-permute-start.3) | collective-permute-done | bytes 8224 | tf_op jit(solution)/shard_map/ppermute | solution.py:562
  24.2 2.6 %collective-permute-done.1.refs_2_ = f32[16,1280]{1,0:T(8,128)S(1)} collective-permute-done((f32[16,1280]{1,0:T(8,128)S(1)}, f32[16,1280]{1,0:T(8,128)S(1)}, u32[]{:S(2)}, u32[]{:S(2)}) %collective-permute-start.1) | collective-permute-done | bytes 81952 | tf_op jit(solution)/shard_map/ppermute | solution.py:514
  26.8 0.1 shard_map.101.rest_0_
  26.9 0.2 collective-permute-start.4
  27.1 2.5 %collective-permute-start.5 = (bf16[16,1152]{1,0:T(8,128)(2,1)S(1)}, bf16[16,1152]{1,0:T(8,128)(2,1)S(1)}, u32[]{:S(2)}, u32[]{:S(2)}) collective-permute-start(bf16[16,1152]{1,0:T(8,128)(2,1)S(1)} %shard_map.101.rest_0_), channel_id=1, source_target_pairs={{0,2},{1,3},{2,0},{3,1},{4,6},{5,7},{6,4},{7,5},{8,10},{9,11},{10,... | collective-permute-start | bytes 110600 | tf_op jit(solution)/shard_map/ppermute | solution.py:522
  29.6 2.3 %collective-permute-start.6 = (bf16[16,1152]{1,0:T(8,128)(2,1)S(1)}, bf16[16,1152]{1,0:T(8,128)(2,1)S(1)}, u32[]{:S(2)}, u32[]{:S(2)}) collective-permute-start(bf16[16,1152]{1,0:T(8,128)(2,1)S(1)} %shard_map.101.rest_0_), channel_id=1, source_target_pairs={{0,3},{1,0},{2,1},{3,2},{4,7},{5,4},{6,5},{7,6},{8,11},{9,8},{10,9... | collective-permute-start | bytes 110600 | tf_op jit(solution)/shard_map/ppermute | solution.py:522
  31.9 0.7 collective-permute-done.4.rest_1_
  32.7 0.9 collective-permute-done.6.rest_3_
  33.6 6.8 %shard_map.102.after_ref.rest_0_ = bf16[16,4224]{1,0:T(8,128)(2,1)S(1)} custom-call(s32[1]{0:T(128)} %bitcast.2.me_ref, s32[8]{0:T(128)S(1)} %copy-done.6, s32[8]{0:T(128)S(1)} %copy-done.7, bf16[16,1152]{1,0:T(8,128)(2,1)S(1)} %shard_map.101.rest_0_, bf16[16,1152]{1,0:T(8,128)(2,1)S(1)} %collective-permute-done.4.rest_1_, ...), custom_call_target="tpu_custom_call" | custom-call | flops 1375731712 | bytes 5373952 | tf_op jit(solution)/shard_map/pallas_call | solution.py:347
  40.3 1.7 %collective-permute-start.7 = (bf16[16,4224]{1,0:T(8,128)(2,1)S(1)}, bf16[16,4224]{1,0:T(8,128)(2,1)S(1)}, u32[]{:S(2)}, u32[]{:S(2)}) collective-permute-start(bf16[16,4224]{1,0:T(8,128)(2,1)S(1)} %shard_map.102.after_ref.rest_0_), channel_id=1, source_target_pairs={{0,1},{1,2},{2,3},{3,0},{4,5},{5,6},{6,7},{7,4},{8,9},{9,10},{10,1... | collective-permute-start | bytes 405512 | tf_op jit(solution)/shard_map/ppermute | solution.py:522
  42.1 3.0 %collective-permute-start.8 = (bf16[16,4224]{1,0:T(8,128)(2,1)S(1)}, bf16[16,4224]{1,0:T(8,128)(2,1)S(1)}, u32[]{:S(2)}, u32[]{:S(2)}) collective-permute-start(bf16[16,4224]{1,0:T(8,128)(2,1)S(1)} %shard_map.102.after_ref.rest_0_), channel_id=1, source_target_pairs={{0,2},{1,3},{2,0},{3,1},{4,6},{5,7},{6,4},{7,5},{8,10},{9,11},{10,... | collective-permute-start | bytes 405512 | tf_op jit(solution)/shard_map/ppermute | solution.py:522
  45.2 7.1 %shard_map.103.rest_4_ = bf16[10,256,4096]{2,1,0:T(8,128)(2,1)S(1)} custom-call(bf16[1,4096,4096]{2,1,0:T(8,128)(2,1)} %w_ref.15, bf16[16,4224]{1,0:T(8,128)(2,1)S(1)} %shard_map.102.after_ref.rest_0_), custom_call_target="tpu_custom_call" | custom-call | bytes 20971520 | tf_op jit(solution)/shard_map/pallas_call | solution.py:75
  52.3 7.0 %shard_map.104 = (bf16[8,4096]{1,0:T(8,128)(2,1)S(1)}, bf16[8,4096]{1,0:T(8,128)(2,1)S(1)}) custom-call(bf16[16,16]{1,0:T(8,128)(2,1)S(1)} %get-tuple-element.38.turn_ref.refs_4_, bf16[1,4096,4096]{2,1,0:T(8,128)(2,1)} %w_ref.15, bf16[16,4224]{1,0:T(8,128)(2,1)S(1)} %shard_map.102.after_ref.rest_0_, bf16[16,4224]{1,0:T(8,128)(2,1)S(1)} %collective-permute-done.7.rest_1_, ...), custom_call_target="tpu_custom_call" | custom-call | flops 536870912 | bytes 12582912 | tf_op jit(solution)/shard_map/pallas_call | solution.py:421
  59.5 1.6 %collective-permute-start.11 = (bf16[8,4096]{1,0:T(8,128)(2,1)S(1)}, bf16[8,4096]{1,0:T(8,128)(2,1)S(1)}, u32[]{:S(2)}, u32[]{:S(2)}) collective-permute-start(bf16[8,4096]{1,0:T(8,128)(2,1)S(1)} %get-tuple-element.26), channel_id=1, source_target_pairs={{0,8},{4,12},{8,0},{12,4},{1,9},{5,13},{9,1},{13,5},{2,10},{6,14},... | collective-permute-start | bytes 196616 | tf_op jit(solution)/shard_map/ppermute | solution.py:593
  61.0 0.3 collective-permute-start.12
  61.3 3.8 %shard_map.105.refs_7_.rest_0_ = bf16[4,256,4608]{2,1,0:T(8,128)(2,1)S(1)} custom-call(bf16[1,4096,4608]{2,1,0:T(8,128)(2,1)} %w_ref.13, bf16[8,4096]{1,0:T(8,128)(2,1)S(1)} %get-tuple-element.25.after_ref.refs_0_), custom_call_target="tpu_custom_call" | custom-call | bytes 9437184 | tf_op jit(solution)/shard_map/pallas_call | solution.py:75
  65.2 0.2 shard_map.106
  65.4 2.4 %collective-permute-start.14 = (bf16[8,4224]{1,0:T(8,128)(2,1)S(1)}, bf16[8,4224]{1,0:T(8,128)(2,1)S(1)}, u32[]{:S(2)}, u32[]{:S(2)}) collective-permute-start(bf16[8,4224]{1,0:T(8,128)(2,1)S(1)} %get-tuple-element.28), channel_id=1, source_target_pairs={{0,24},{4,28},{8,16},{12,20},{24,0},{28,4},{16,8},{20,12},{1,25},{... | collective-permute-start | bytes 202760 | tf_op jit(solution)/shard_map/ppermute | solution.py:606
  67.9 0.5 collective-permute-start.13
  68.4 3.1 %shard_map.107.rest_1_ = bf16[3,256,4608]{2,1,0:T(8,128)(2,1)S(1)} custom-call(bf16[1,4096,4608]{2,1,0:T(8,128)(2,1)} %w_ref.13, f32[8,4096]{1,0:T(8,128)S(1)} %get-tuple-element.36.after_ref.refs_5_), custom_call_target="tpu_custom_call" | custom-call | bytes 7077888 | tf_op jit(solution)/shard_map/pallas_call | solution.py:75
  71.5 0.7 collective-permute-done.13
  72.2 7.8 %shard_map.108 = (f32[16,1280]{1,0:T(8,128)S(1)}, f32[16,1280]{1,0:T(8,128)S(1)}, f32[16,1280]{1,0:T(8,128)S(1)}, f32[16,1280]{1,0:T(8,128)S(1)}) custom-call(s32[1]{0:T(128)} %bitcast.2.me_ref, bf16[16,4224]{1,0:T(8,128)(2,1)S(1)} %pad_maximum_fusion.x_ref, bf16[16,16]{1,0:T(8,128)(2,1)S(1)} %get-tuple-element.37.aux_ref, bf16[1,4096,4608]{2,1,0:T(8,128)(2,1)} %w_ref.13, ...), custom_call_target="tpu_custom_call" | custom-call | flops 603979776 | bytes 21233664 | tf_op jit(solution)/shard_map/pallas_call | solution.py:151
  80.1 3.7 %collective-permute-start.15 = (f32[16,1280]{1,0:T(8,128)S(1)}, f32[16,1280]{1,0:T(8,128)S(1)}, u32[]{:S(2)}, u32[]{:S(2)}) collective-permute-start(f32[16,1280]{1,0:T(8,128)S(1)} %get-tuple-element.31), channel_id=1, source_target_pairs={{0,3},{1,0},{2,1},{3,2},{4,7},{5,4},{6,5},{7,6},{8,11},{9,8},{10,9... | collective-permute-start | bytes 245768 | tf_op jit(solution)/shard_map/ppermute | solution.py:514
  83.7 0.8 collective-permute-start.16
  84.5 2.1 %collective-permute-done.15.refs_1_ = f32[16,1280]{1,0:T(8,128)S(1)} collective-permute-done((f32[16,1280]{1,0:T(8,128)S(1)}, f32[16,1280]{1,0:T(8,128)S(1)}, u32[]{:S(2)}, u32[]{:S(2)}) %collective-permute-start.15) | collective-permute-done | bytes 81952 | tf_op jit(solution)/shard_map/ppermute | solution.py:514
  86.7 5.3 %collective-permute-done.16.refs_2_ = f32[16,1280]{1,0:T(8,128)S(1)} collective-permute-done((f32[16,1280]{1,0:T(8,128)S(1)}, f32[16,1280]{1,0:T(8,128)S(1)}, u32[]{:S(2)}, u32[]{:S(2)}) %collective-permute-start.16) | collective-permute-done | bytes 81952 | tf_op jit(solution)/shard_map/ppermute | solution.py:514
  92.0 0.1 shard_map.109.rest_0_
  92.1 1.5 %collective-permute-start.19 = (bf16[16,1152]{1,0:T(8,128)(2,1)S(1)}, bf16[16,1152]{1,0:T(8,128)(2,1)S(1)}, u32[]{:S(2)}, u32[]{:S(2)}) collective-permute-start(bf16[16,1152]{1,0:T(8,128)(2,1)S(1)} %shard_map.109.rest_0_), channel_id=1, source_target_pairs={{0,2},{1,3},{2,0},{3,1},{4,6},{5,7},{6,4},{7,5},{8,10},{9,11},{10,... | collective-permute-start | bytes 110600 | tf_op jit(solution)/shard_map/ppermute | solution.py:522
  93.5 2.4 %collective-permute-start.20 = (bf16[16,1152]{1,0:T(8,128)(2,1)S(1)}, bf16[16,1152]{1,0:T(8,128)(2,1)S(1)}, u32[]{:S(2)}, u32[]{:S(2)}) collective-permute-start(bf16[16,1152]{1,0:T(8,128)(2,1)S(1)} %shard_map.109.rest_0_), channel_id=1, source_target_pairs={{0,3},{1,0},{2,1},{3,2},{4,7},{5,4},{6,5},{7,6},{8,11},{9,8},{10,9... | collective-permute-start | bytes 110600 | tf_op jit(solution)/shard_map/ppermute | solution.py:522
  95.9 2.0 %collective-permute-done.18.rest_1_ = bf16[16,1152]{1,0:T(8,128)(2,1)S(1)} collective-permute-done((bf16[16,1152]{1,0:T(8,128)(2,1)S(1)}, bf16[16,1152]{1,0:T(8,128)(2,1)S(1)}, u32[]{:S(2)}, u32[]{:S(2)}) %collective-permute-start.18) | collective-permute-done | bytes 36896 | tf_op jit(solution)/shard_map/ppermute | solution.py:522
  97.9 0.5 collective-permute-done.20.rest_3_
  98.4 5.9 %shard_map.110.after_ref.rest_0_ = bf16[16,4224]{1,0:T(8,128)(2,1)S(1)} custom-call(s32[1]{0:T(128)} %bitcast.2.me_ref, s32[8]{0:T(128)S(1)} %copy-done.6, s32[8]{0:T(128)S(1)} %copy-done.7, bf16[16,1152]{1,0:T(8,128)(2,1)S(1)} %shard_map.109.rest_0_, bf16[16,1152]{1,0:T(8,128)(2,1)S(1)} %collective-permute-done.18.rest_1_, ...), custom_call_target="tpu_custom_call" | custom-call | flops 1375731712 | bytes 5373952 | tf_op jit(solution)/shard_map/pallas_call | solution.py:347
  104.3 2.1 %collective-permute-start.21 = (bf16[16,4224]{1,0:T(8,128)(2,1)S(1)}, bf16[16,4224]{1,0:T(8,128)(2,1)S(1)}, u32[]{:S(2)}, u32[]{:S(2)}) collective-permute-start(bf16[16,4224]{1,0:T(8,128)(2,1)S(1)} %shard_map.110.after_ref.rest_0_), channel_id=1, source_target_pairs={{0,1},{1,2},{2,3},{3,0},{4,5},{5,6},{6,7},{7,4},{8,9},{9,10},{10,1... | collective-permute-start | bytes 405512 | tf_op jit(solution)/shard_map/ppermute | solution.py:522
  106.4 1.8 %collective-permute-start.22 = (bf16[16,4224]{1,0:T(8,128)(2,1)S(1)}, bf16[16,4224]{1,0:T(8,128)(2,1)S(1)}, u32[]{:S(2)}, u32[]{:S(2)}) collective-permute-start(bf16[16,4224]{1,0:T(8,128)(2,1)S(1)} %shard_map.110.after_ref.rest_0_), channel_id=1, source_target_pairs={{0,2},{1,3},{2,0},{3,1},{4,6},{5,7},{6,4},{7,5},{8,10},{9,11},{10,... | collective-permute-start | bytes 405512 | tf_op jit(solution)/shard_map/ppermute | solution.py:522
  108.2 0.6 collective-permute-start.23
  108.8 1.5 %collective-permute-start.27 = (f32[8,4096]{1,0:T(8,128)S(1)}, f32[8,4096]{1,0:T(8,128)S(1)}, u32[]{:S(2)}, u32[]{:S(2)}) collective-permute-start(f32[8,4096]{1,0:T(8,128)S(1)} %get-tuple-element.36.after_ref.refs_5_), channel_id=1, source_target_pairs={{0,16},{16,0},{1,17},{17,1},{2,18},{18,2},{3,19},{19,3},{4,20},{20... | collective-permute-start | bytes 393224 | tf_op jit(solution)/shard_map/ppermute | solution.py:580
  110.3 7.1 %shard_map.111.rest_4_ = bf16[10,256,4096]{2,1,0:T(8,128)(2,1)S(1)} custom-call(bf16[1,4096,4096]{2,1,0:T(8,128)(2,1)} %w_ref.15, bf16[16,4224]{1,0:T(8,128)(2,1)S(1)} %shard_map.110.after_ref.rest_0_), custom_call_target="tpu_custom_call" | custom-call | bytes 20971520 | tf_op jit(solution)/shard_map/pallas_call | solution.py:75
  117.5 7.0 %shard_map.112 = (bf16[8,4096]{1,0:T(8,128)(2,1)S(1)}, bf16[8,4096]{1,0:T(8,128)(2,1)S(1)}) custom-call(bf16[16,16]{1,0:T(8,128)(2,1)S(1)} %get-tuple-element.38.turn_ref.refs_4_, bf16[1,4096,4096]{2,1,0:T(8,128)(2,1)} %w_ref.15, bf16[16,4224]{1,0:T(8,128)(2,1)S(1)} %shard_map.110.after_ref.rest_0_, bf16[16,4224]{1,0:T(8,128)(2,1)S(1)} %collective-permute-done.21.rest_1_, ...), custom_call_target="tpu_custom_call" | custom-call | flops 536870912 | bytes 12582912 | tf_op jit(solution)/shard_map/pallas_call | solution.py:421
  124.5 0.6 collective-permute-start.25
  125.1 1.6 %collective-permute-start.24 = (bf16[8,4096]{1,0:T(8,128)(2,1)S(1)}, bf16[8,4096]{1,0:T(8,128)(2,1)S(1)}, u32[]{:S(2)}, u32[]{:S(2)}) collective-permute-start(bf16[8,4096]{1,0:T(8,128)(2,1)S(1)} %get-tuple-element.34.refs_0_), channel_id=1, source_target_pairs={{0,4},{4,0},{8,12},{12,8},{1,5},{5,1},{9,13},{13,9},{2,6},{6,2},{1... | collective-permute-start | bytes 196616 | tf_op jit(solution)/shard_map/ppermute | solution.py:593
  126.8 0.8 collective-permute-done.24.refs_1_
  127.6 1.9 %collective-permute-done.25.refs_2_ = bf16[8,4096]{1,0:T(8,128)(2,1)S(1)} collective-permute-done((bf16[8,4096]{1,0:T(8,128)(2,1)S(1)}, bf16[8,4096]{1,0:T(8,128)(2,1)S(1)}, u32[]{:S(2)}, u32[]{:S(2)}) %collective-permute-start.25) | collective-permute-done | bytes 65568 | tf_op jit(solution)/shard_map/ppermute | solution.py:593
  129.5 1.2 shard_map.113
  (42 shorter events, 0.3 us)
Async XLA Ops:
  0.0 33.5 %copy-start.2 = (bf16[1,2,2,512,128]{4,3,2,1,0:T(8,128)(2,1)S(1)}, bf16[1,2,2,512,128]{4,3,2,1,0:T(8,128)(2,1)}, u32[]{:S(2)}) copy-start(bf16[1,2,2,512,128]{4,3,2,1,0:T(8,128)(2,1)} %rest_5_.3) | copy-start | bytes 1572868
  0.0 33.5 %copy-start.3 = (bf16[1,2,2,512,128]{4,3,2,1,0:T(8,128)(2,1)S(1)}, bf16[1,2,2,512,128]{4,3,2,1,0:T(8,128)(2,1)}, u32[]{:S(2)}) copy-start(bf16[1,2,2,512,128]{4,3,2,1,0:T(8,128)(2,1)} %rest_7_.3) | copy-start | bytes 1572868
  0.0 1.0 copy-start.4
  1.0 32.5 %copy-start.6 = (s32[8]{0:T(128)S(1)}, s32[8]{0:T(128)}, u32[]{:S(2)}) copy-start(s32[8]{0:T(128)} %order_ref.3) | copy-start | bytes 100
  1.0 32.5 %copy-start.7 = (s32[8]{0:T(128)S(1)}, s32[8]{0:T(128)}, u32[]{:S(2)}) copy-start(s32[8]{0:T(128)} %lengths_ref.3) | copy-start | bytes 100
  14.2 10.1 %collective-permute-start = (f32[16,1280]{1,0:T(8,128)S(1)}, f32[16,1280]{1,0:T(8,128)S(1)}, u32[]{:S(2)}, u32[]{:S(2)}) collective-permute-start(f32[16,1280]{1,0:T(8,128)S(1)} %get-tuple-element.22), channel_id=1, source_target_pairs={{0,3},{1,0},{2,1},{3,2},{4,7},{5,4},{6,5},{7,6},{8,11},{9,8},{10,9... | collective-permute-start | bytes 245768 | tf_op jit(solution)/shard_map/ppermute | solution.py:514
  19.3 7.5 %collective-permute-start.1 = (f32[16,1280]{1,0:T(8,128)S(1)}, f32[16,1280]{1,0:T(8,128)S(1)}, u32[]{:S(2)}, u32[]{:S(2)}) collective-permute-start(f32[16,1280]{1,0:T(8,128)S(1)} %get-tuple-element.23), channel_id=1, source_target_pairs={{0,2},{1,3},{2,0},{3,1},{4,6},{5,7},{6,4},{7,5},{8,10},{9,11},{10,... | collective-permute-start | bytes 245768 | tf_op jit(solution)/shard_map/ppermute | solution.py:514
  19.3 7.5 %collective-permute-start.2 = (f32[16,1280]{1,0:T(8,128)S(1)}, f32[16,1280]{1,0:T(8,128)S(1)}, u32[]{:S(2)}, u32[]{:S(2)}) collective-permute-start(f32[16,1280]{1,0:T(8,128)S(1)} %get-tuple-element.24), channel_id=1, source_target_pairs={{0,1},{1,2},{2,3},{3,0},{4,5},{5,6},{6,7},{7,4},{8,9},{9,10},{10,1... | collective-permute-start | bytes 245768 | tf_op jit(solution)/shard_map/ppermute | solution.py:514
  20.3 3.9 %collective-permute-start.3 = (bf16[1,4096]{1,0:T(2,128)(2,1)}, bf16[1,4096]{1,0:T(2,128)(2,1)S(1)}, u32[]{:S(2)}, u32[]{:S(2)}) collective-permute-start(bf16[1,4096]{1,0:T(2,128)(2,1)} %aux_ref.1), channel_id=1, source_target_pairs={{0,16},{16,0},{1,17},{17,1},{2,18},{18,2},{3,19},{19,3},{4,20},{20... | collective-permute-start | bytes 24584 | tf_op jit(solution)/shard_map/ppermute | solution.py:562
  26.9 5.8 %collective-permute-start.4 = (bf16[16,1152]{1,0:T(8,128)(2,1)S(1)}, bf16[16,1152]{1,0:T(8,128)(2,1)S(1)}, u32[]{:S(2)}, u32[]{:S(2)}) collective-permute-start(bf16[16,1152]{1,0:T(8,128)(2,1)S(1)} %shard_map.101.rest_0_), channel_id=1, source_target_pairs={{0,1},{1,2},{2,3},{3,0},{4,5},{5,6},{6,7},{7,4},{8,9},{9,10},{10,1... | collective-permute-start | bytes 110600 | tf_op jit(solution)/shard_map/ppermute | solution.py:522
  27.1 5.6 %collective-permute-start.5 = (bf16[16,1152]{1,0:T(8,128)(2,1)S(1)}, bf16[16,1152]{1,0:T(8,128)(2,1)S(1)}, u32[]{:S(2)}, u32[]{:S(2)}) collective-permute-start(bf16[16,1152]{1,0:T(8,128)(2,1)S(1)} %shard_map.101.rest_0_), channel_id=1, source_target_pairs={{0,2},{1,3},{2,0},{3,1},{4,6},{5,7},{6,4},{7,5},{8,10},{9,11},{10,... | collective-permute-start | bytes 110600 | tf_op jit(solution)/shard_map/ppermute | solution.py:522
  29.6 4.0 %collective-permute-start.6 = (bf16[16,1152]{1,0:T(8,128)(2,1)S(1)}, bf16[16,1152]{1,0:T(8,128)(2,1)S(1)}, u32[]{:S(2)}, u32[]{:S(2)}) collective-permute-start(bf16[16,1152]{1,0:T(8,128)(2,1)S(1)} %shard_map.101.rest_0_), channel_id=1, source_target_pairs={{0,3},{1,0},{2,1},{3,2},{4,7},{5,4},{6,5},{7,6},{8,11},{9,8},{10,9... | collective-permute-start | bytes 110600 | tf_op jit(solution)/shard_map/ppermute | solution.py:522
  40.3 12.0 %collective-permute-start.7 = (bf16[16,4224]{1,0:T(8,128)(2,1)S(1)}, bf16[16,4224]{1,0:T(8,128)(2,1)S(1)}, u32[]{:S(2)}, u32[]{:S(2)}) collective-permute-start(bf16[16,4224]{1,0:T(8,128)(2,1)S(1)} %shard_map.102.after_ref.rest_0_), channel_id=1, source_target_pairs={{0,1},{1,2},{2,3},{3,0},{4,5},{5,6},{6,7},{7,4},{8,9},{9,10},{10,1... | collective-permute-start | bytes 405512 | tf_op jit(solution)/shard_map/ppermute | solution.py:522
  42.1 10.2 %collective-permute-start.8 = (bf16[16,4224]{1,0:T(8,128)(2,1)S(1)}, bf16[16,4224]{1,0:T(8,128)(2,1)S(1)}, u32[]{:S(2)}, u32[]{:S(2)}) collective-permute-start(bf16[16,4224]{1,0:T(8,128)(2,1)S(1)} %shard_map.102.after_ref.rest_0_), channel_id=1, source_target_pairs={{0,2},{1,3},{2,0},{3,1},{4,6},{5,7},{6,4},{7,5},{8,10},{9,11},{10,... | collective-permute-start | bytes 405512 | tf_op jit(solution)/shard_map/ppermute | solution.py:522
  45.1 7.2 %collective-permute-start.9 = (bf16[16,4224]{1,0:T(8,128)(2,1)S(1)}, bf16[16,4224]{1,0:T(8,128)(2,1)S(1)}, u32[]{:S(2)}, u32[]{:S(2)}) collective-permute-start(bf16[16,4224]{1,0:T(8,128)(2,1)S(1)} %shard_map.102.after_ref.rest_0_), channel_id=1, source_target_pairs={{0,3},{1,0},{2,1},{3,2},{4,7},{5,4},{6,5},{7,6},{8,11},{9,8},{10,9... | collective-permute-start | bytes 405512 | tf_op jit(solution)/shard_map/ppermute | solution.py:522
  59.4 5.8 %collective-permute-start.10 = (bf16[8,4096]{1,0:T(8,128)(2,1)S(1)}, bf16[8,4096]{1,0:T(8,128)(2,1)S(1)}, u32[]{:S(2)}, u32[]{:S(2)}) collective-permute-start(bf16[8,4096]{1,0:T(8,128)(2,1)S(1)} %get-tuple-element.25.after_ref.refs_0_), channel_id=1, source_target_pairs={{0,4},{4,0},{8,12},{12,8},{1,5},{5,1},{9,13},{13,9},{2,6},{6,2},{1... | collective-permute-start | bytes 196616 | tf_op jit(solution)/shard_map/ppermute | solution.py:593
  59.4 5.7 %copy-start.5 = (bf16[2,8,4096]{2,1,0:T(8,128)(2,1)S(1)}, bf16[2,8,4096]{2,1,0:T(8,128)(2,1)}, u32[]{:S(2)}) copy-start(bf16[2,8,4096]{2,1,0:T(8,128)(2,1)} %param.10) | copy-start | bytes 393220
  59.5 5.7 %collective-permute-start.11 = (bf16[8,4096]{1,0:T(8,128)(2,1)S(1)}, bf16[8,4096]{1,0:T(8,128)(2,1)S(1)}, u32[]{:S(2)}, u32[]{:S(2)}) collective-permute-start(bf16[8,4096]{1,0:T(8,128)(2,1)S(1)} %get-tuple-element.26), channel_id=1, source_target_pairs={{0,8},{4,12},{8,0},{12,4},{1,9},{5,13},{9,1},{13,5},{2,10},{6,14},... | collective-permute-start | bytes 196616 | tf_op jit(solution)/shard_map/ppermute | solution.py:593
  61.0 4.1 %collective-permute-start.12 = (bf16[8,4096]{1,0:T(8,128)(2,1)S(1)}, bf16[8,4096]{1,0:T(8,128)(2,1)S(1)}, u32[]{:S(2)}, u32[]{:S(2)}) collective-permute-start(bf16[8,4096]{1,0:T(8,128)(2,1)S(1)} %get-tuple-element.26), channel_id=1, source_target_pairs={{0,12},{4,8},{8,4},{12,0},{1,13},{5,9},{9,5},{13,1},{2,14},{6,10},... | collective-permute-start | bytes 196616 | tf_op jit(solution)/shard_map/ppermute | solution.py:593
  65.4 6.1 %collective-permute-start.14 = (bf16[8,4224]{1,0:T(8,128)(2,1)S(1)}, bf16[8,4224]{1,0:T(8,128)(2,1)S(1)}, u32[]{:S(2)}, u32[]{:S(2)}) collective-permute-start(bf16[8,4224]{1,0:T(8,128)(2,1)S(1)} %get-tuple-element.28), channel_id=1, source_target_pairs={{0,24},{4,28},{8,16},{12,20},{24,0},{28,4},{16,8},{20,12},{1,25},{... | collective-permute-start | bytes 202760 | tf_op jit(solution)/shard_map/ppermute | solution.py:606
  67.9 4.4 %collective-permute-start.13 = (bf16[8,4224]{1,0:T(8,128)(2,1)S(1)}, bf16[8,4224]{1,0:T(8,128)(2,1)S(1)}, u32[]{:S(2)}, u32[]{:S(2)}) collective-permute-start(bf16[8,4224]{1,0:T(8,128)(2,1)S(1)} %get-tuple-element.28), channel_id=1, source_target_pairs={{0,16},{4,20},{8,24},{12,28},{16,0},{20,4},{24,8},{28,12},{1,17},{... | collective-permute-start | bytes 202760 | tf_op jit(solution)/shard_map/ppermute | solution.py:606
  72.2 26.2 %copy-start = (bf16[1,2,4096,128]{3,2,1,0:T(8,128)(2,1)S(1)}, bf16[1,2,4096,128]{3,2,1,0:T(8,128)(2,1)}, u32[]{:S(2)}) copy-start(bf16[1,2,4096,128]{3,2,1,0:T(8,128)(2,1)} %rest_4_.3) | copy-start | bytes 6291460
  72.2 26.2 %copy-start.1 = (bf16[1,2,4096,128]{3,2,1,0:T(8,128)(2,1)S(1)}, bf16[1,2,4096,128]{3,2,1,0:T(8,128)(2,1)}, u32[]{:S(2)}) copy-start(bf16[1,2,4096,128]{3,2,1,0:T(8,128)(2,1)} %rest_6_.3) | copy-start | bytes 6291460
  80.1 6.6 %collective-permute-start.15 = (f32[16,1280]{1,0:T(8,128)S(1)}, f32[16,1280]{1,0:T(8,128)S(1)}, u32[]{:S(2)}, u32[]{:S(2)}) collective-permute-start(f32[16,1280]{1,0:T(8,128)S(1)} %get-tuple-element.31), channel_id=1, source_target_pairs={{0,3},{1,0},{2,1},{3,2},{4,7},{5,4},{6,5},{7,6},{8,11},{9,8},{10,9... | collective-permute-start | bytes 245768 | tf_op jit(solution)/shard_map/ppermute | solution.py:514
  83.7 8.2 %collective-permute-start.16 = (f32[16,1280]{1,0:T(8,128)S(1)}, f32[16,1280]{1,0:T(8,128)S(1)}, u32[]{:S(2)}, u32[]{:S(2)}) collective-permute-start(f32[16,1280]{1,0:T(8,128)S(1)} %get-tuple-element.32), channel_id=1, source_target_pairs={{0,2},{1,3},{2,0},{3,1},{4,6},{5,7},{6,4},{7,5},{8,10},{9,11},{10,... | collective-permute-start | bytes 245768 | tf_op jit(solution)/shard_map/ppermute | solution.py:514
  84.5 7.4 %collective-permute-start.17 = (f32[16,1280]{1,0:T(8,128)S(1)}, f32[16,1280]{1,0:T(8,128)S(1)}, u32[]{:S(2)}, u32[]{:S(2)}) collective-permute-start(f32[16,1280]{1,0:T(8,128)S(1)} %get-tuple-element.33), channel_id=1, source_target_pairs={{0,1},{1,2},{2,3},{3,0},{4,5},{5,6},{6,7},{7,4},{8,9},{9,10},{10,1... | collective-permute-start | bytes 245768 | tf_op jit(solution)/shard_map/ppermute | solution.py:514
  92.1 5.9 %collective-permute-start.18 = (bf16[16,1152]{1,0:T(8,128)(2,1)S(1)}, bf16[16,1152]{1,0:T(8,128)(2,1)S(1)}, u32[]{:S(2)}, u32[]{:S(2)}) collective-permute-start(bf16[16,1152]{1,0:T(8,128)(2,1)S(1)} %shard_map.109.rest_0_), channel_id=1, source_target_pairs={{0,1},{1,2},{2,3},{3,0},{4,5},{5,6},{6,7},{7,4},{8,9},{9,10},{10,1... | collective-permute-start | bytes 110600 | tf_op jit(solution)/shard_map/ppermute | solution.py:522
  92.1 5.9 %collective-permute-start.19 = (bf16[16,1152]{1,0:T(8,128)(2,1)S(1)}, bf16[16,1152]{1,0:T(8,128)(2,1)S(1)}, u32[]{:S(2)}, u32[]{:S(2)}) collective-permute-start(bf16[16,1152]{1,0:T(8,128)(2,1)S(1)} %shard_map.109.rest_0_), channel_id=1, source_target_pairs={{0,2},{1,3},{2,0},{3,1},{4,6},{5,7},{6,4},{7,5},{8,10},{9,11},{10,... | collective-permute-start | bytes 110600 | tf_op jit(solution)/shard_map/ppermute | solution.py:522
  93.5 4.9 %collective-permute-start.20 = (bf16[16,1152]{1,0:T(8,128)(2,1)S(1)}, bf16[16,1152]{1,0:T(8,128)(2,1)S(1)}, u32[]{:S(2)}, u32[]{:S(2)}) collective-permute-start(bf16[16,1152]{1,0:T(8,128)(2,1)S(1)} %shard_map.109.rest_0_), channel_id=1, source_target_pairs={{0,3},{1,0},{2,1},{3,2},{4,7},{5,4},{6,5},{7,6},{8,11},{9,8},{10,9... | collective-permute-start | bytes 110600 | tf_op jit(solution)/shard_map/ppermute | solution.py:522
  104.3 13.1 %collective-permute-start.21 = (bf16[16,4224]{1,0:T(8,128)(2,1)S(1)}, bf16[16,4224]{1,0:T(8,128)(2,1)S(1)}, u32[]{:S(2)}, u32[]{:S(2)}) collective-permute-start(bf16[16,4224]{1,0:T(8,128)(2,1)S(1)} %shard_map.110.after_ref.rest_0_), channel_id=1, source_target_pairs={{0,1},{1,2},{2,3},{3,0},{4,5},{5,6},{6,7},{7,4},{8,9},{9,10},{10,1... | collective-permute-start | bytes 405512 | tf_op jit(solution)/shard_map/ppermute | solution.py:522
  106.4 11.1 %collective-permute-start.22 = (bf16[16,4224]{1,0:T(8,128)(2,1)S(1)}, bf16[16,4224]{1,0:T(8,128)(2,1)S(1)}, u32[]{:S(2)}, u32[]{:S(2)}) collective-permute-start(bf16[16,4224]{1,0:T(8,128)(2,1)S(1)} %shard_map.110.after_ref.rest_0_), channel_id=1, source_target_pairs={{0,2},{1,3},{2,0},{3,1},{4,6},{5,7},{6,4},{7,5},{8,10},{9,11},{10,... | collective-permute-start | bytes 405512 | tf_op jit(solution)/shard_map/ppermute | solution.py:522
  108.2 9.3 %collective-permute-start.23 = (bf16[16,4224]{1,0:T(8,128)(2,1)S(1)}, bf16[16,4224]{1,0:T(8,128)(2,1)S(1)}, u32[]{:S(2)}, u32[]{:S(2)}) collective-permute-start(bf16[16,4224]{1,0:T(8,128)(2,1)S(1)} %shard_map.110.after_ref.rest_0_), channel_id=1, source_target_pairs={{0,3},{1,0},{2,1},{3,2},{4,7},{5,4},{6,5},{7,6},{8,11},{9,8},{10,9... | collective-permute-start | bytes 405512 | tf_op jit(solution)/shard_map/ppermute | solution.py:522
  108.8 18.0 %collective-permute-start.27 = (f32[8,4096]{1,0:T(8,128)S(1)}, f32[8,4096]{1,0:T(8,128)S(1)}, u32[]{:S(2)}, u32[]{:S(2)}) collective-permute-start(f32[8,4096]{1,0:T(8,128)S(1)} %get-tuple-element.36.after_ref.refs_5_), channel_id=1, source_target_pairs={{0,16},{16,0},{1,17},{17,1},{2,18},{18,2},{3,19},{19,3},{4,20},{20... | collective-permute-start | bytes 393224 | tf_op jit(solution)/shard_map/ppermute | solution.py:580
  124.5 5.0 %collective-permute-start.25 = (bf16[8,4096]{1,0:T(8,128)(2,1)S(1)}, bf16[8,4096]{1,0:T(8,128)(2,1)S(1)}, u32[]{:S(2)}, u32[]{:S(2)}) collective-permute-start(bf16[8,4096]{1,0:T(8,128)(2,1)S(1)} %get-tuple-element.35), channel_id=1, source_target_pairs={{0,8},{4,12},{8,0},{12,4},{1,9},{5,13},{9,1},{13,5},{2,10},{6,14},... | collective-permute-start | bytes 196616 | tf_op jit(solution)/shard_map/ppermute | solution.py:593
  125.1 4.4 %collective-permute-start.26 = (bf16[8,4096]{1,0:T(8,128)(2,1)S(1)}, bf16[8,4096]{1,0:T(8,128)(2,1)S(1)}, u32[]{:S(2)}, u32[]{:S(2)}) collective-permute-start(bf16[8,4096]{1,0:T(8,128)(2,1)S(1)} %get-tuple-element.35), channel_id=1, source_target_pairs={{0,12},{4,8},{8,4},{12,0},{1,13},{5,9},{9,5},{13,1},{2,14},{6,10},... | collective-permute-start | bytes 196616 | tf_op jit(solution)/shard_map/ppermute | solution.py:593
  125.1 2.5 %collective-permute-start.24 = (bf16[8,4096]{1,0:T(8,128)(2,1)S(1)}, bf16[8,4096]{1,0:T(8,128)(2,1)S(1)}, u32[]{:S(2)}, u32[]{:S(2)}) collective-permute-start(bf16[8,4096]{1,0:T(8,128)(2,1)S(1)} %get-tuple-element.34.refs_0_), channel_id=1, source_target_pairs={{0,4},{4,0},{8,12},{12,8},{1,5},{5,1},{9,13},{13,9},{2,6},{6,2},{1... | collective-permute-start | bytes 196616 | tf_op jit(solution)/shard_map/ppermute | solution.py:593

commit v5 on v4

--- a/solution.py
+++ b/solution.py
@@ -587,7 +587,7 @@
             parts, prefix_keys, prefix_values, suffix_keys, suffix_values,
             me, order, lengths, group, 52 if fresh else 34,
         )
-        held = load(w_out, 0, max(1, out_blocks * 10 // 16), out_depth, sent)
+        held = load(w_out, 0, max(1, out_blocks * 8 // 16), out_depth, sent)
         sent = output(around(sent, "ctx"), turn, w_out, [held], groups, hd)
         parts = [sent[0]] + [
             lax.ppermute(sent[k // 2], "tp", [(n, n ^ k) for n in range(tp)]) for k in range(1, tp)
@@ -595,7 +595,7 @@
         if last:
             place = jnp.stack([section == layer, tp_me % 2]).astype(jnp.int32)
             return finish(parts, residual, result, place, steps)
-        first = load(w_qkv, 0, max(1, in_blocks * 4 // 16), in_depth, sent[0])
+        first = load(w_qkv, 0, max(1, in_blocks * 3 // 16), in_depth, sent[0])
         y, message = add_up(parts, residual, next_gain, first)
         result = y if result is None else jnp.where(section == layer, y, result)
         here, there = layer * tp, (layer + 1) * tp

time: 131 us -> 130 us (level)
  Pallas kernels: 70.5 us -> 68.2 us
  waiting for transfers between devices: 20 us -> 21.5 us
    pallas_call x4, Pallas kernels: 21.2 us -> 18.1 us  [load(): pl.pallas_call(functools.partial(load_kernel, first), out_shape=jax.Shape...]
  transfers between devices with their start and end apart: 28 -> 28, of which waited for: 11 -> 13; matrix products, arithmetic and copies ran while one was open for 0% -> 0% of each run, Pallas kernels for 22% -> 19%
where the time goes in v5:
time: 130 us
  Pallas kernels  68.2 us (52%)
  starting transfers between devices  38.9 us (30%)
  waiting for transfers between devices  21.5 us (17%)
    pallas_call x2, Pallas kernels, project(): pl.pallas_call(functools.partial(project_kernel, chunks, len(held), fresh...  21.7 us
    ppermute x12, starting transfers between devices, around(): lax.ppermute(part, axis, [(i, (i + k) % count) for i in range(count)])  18.1 us
    pallas_call x4, Pallas kernels, load(): pl.pallas_call(functools.partial(load_kernel, first), out_shape=jax.Shape...  18.1 us
    pallas_call x2, Pallas kernels, output(): pl.pallas_call(functools.partial(output_kernel, blocks, groups, len(held)...  14.1 us
    pallas_call x2, Pallas kernels, attend(): pl.pallas_call(functools.partial(attend_kernel, len(parts), order.shape[0...  12.7 us
    ppermute x6, starting transfers between devices, back(): lax.ppermute(parts[k], axis, [(i, (i - k) % count) for i in range(count)])  10.8 us
    ppermute x6, waiting for transfers between devices, back(): lax.ppermute(parts[k], axis, [(i, (i - k) % count) for i in range(count)])  9.83 us
    ppermute x12, waiting for transfers between devices, around(): lax.ppermute(part, axis, [(i, (i + k) % count) for i in range(count)])  5.19 us
  transfers between devices with their start and end apart: 28, of which 13 were waited for; matrix products, arithmetic and copies ran while one was open for 0% of the time, Pallas kernels for 19%

profile of v5, /device:TPU:0, one launch (start us, length us, event | category | flops | bytes accessed | tf_op | source)
XLA Modules:
  0.0 129.9 jit_solution(14487494423195618580)
XLA Ops:
  0.0 0.9 copy-done.4
  0.9 13.2 %shard_map.100 = (f32[16,1280]{1,0:T(8,128)S(1)}, f32[16,1280]{1,0:T(8,128)S(1)}, f32[16,1280]{1,0:T(8,128)S(1)}, f32[16,1280]{1,0:T(8,128)S(1)}) custom-call(s32[1]{0:T(128)} %bitcast.2.me_ref, bf16[16,4096]{1,0:T(8,128)(2,1)S(1)} %bitcast.4, bf16[1,4096]{1,0:T(2,128)(2,1)} %aux_ref.1, bf16[1,4096,4608]{2,1,0:T(8,128)(2,1)} %w_ref.13), custom_call_target="tpu_custom_call" | custom-call | flops 603979776 | bytes 37748736 | tf_op jit(solution)/shard_map/pallas_call | solution.py:151
  14.1 5.1 %collective-permute-start = (f32[16,1280]{1,0:T(8,128)S(1)}, f32[16,1280]{1,0:T(8,128)S(1)}, u32[]{:S(2)}, u32[]{:S(2)}) collective-permute-start(f32[16,1280]{1,0:T(8,128)S(1)} %get-tuple-element.22), channel_id=1, source_target_pairs={{0,3},{1,0},{2,1},{3,2},{4,7},{5,4},{6,5},{7,6},{8,11},{9,8},{10,9... | collective-permute-start | bytes 245768 | tf_op jit(solution)/shard_map/ppermute | solution.py:514
  19.3 1.0 collective-permute-start.2
  20.3 1.5 %collective-permute-start.3 = (bf16[1,4096]{1,0:T(2,128)(2,1)}, bf16[1,4096]{1,0:T(2,128)(2,1)S(1)}, u32[]{:S(2)}, u32[]{:S(2)}) collective-permute-start(bf16[1,4096]{1,0:T(2,128)(2,1)} %aux_ref.1), channel_id=1, source_target_pairs={{0,16},{16,0},{1,17},{17,1},{2,18},{18,2},{3,19},{19,3},{4,20},{20... | collective-permute-start | bytes 24584 | tf_op jit(solution)/shard_map/ppermute | solution.py:562
  21.8 2.5 %collective-permute-done.3.refs_4_.refs_6_ = bf16[1,4096]{1,0:T(2,128)(2,1)S(1)} collective-permute-done((bf16[1,4096]{1,0:T(2,128)(2,1)}, bf16[1,4096]{1,0:T(2,128)(2,1)S(1)}, u32[]{:S(2)}, u32[]{:S(2)}) %collective-permute-start.3) | collective-permute-done | bytes 8224 | tf_op jit(solution)/shard_map/ppermute | solution.py:562
  24.2 2.6 %collective-permute-done.1.refs_2_ = f32[16,1280]{1,0:T(8,128)S(1)} collective-permute-done((f32[16,1280]{1,0:T(8,128)S(1)}, f32[16,1280]{1,0:T(8,128)S(1)}, u32[]{:S(2)}, u32[]{:S(2)}) %collective-permute-start.1) | collective-permute-done | bytes 81952 | tf_op jit(solution)/shard_map/ppermute | solution.py:514
  26.9 0.2 collective-permute-start.4
  27.1 2.5 %collective-permute-start.5 = (bf16[16,1152]{1,0:T(8,128)(2,1)S(1)}, bf16[16,1152]{1,0:T(8,128)(2,1)S(1)}, u32[]{:S(2)}, u32[]{:S(2)}) collective-permute-start(bf16[16,1152]{1,0:T(8,128)(2,1)S(1)} %shard_map.101.rest_0_), channel_id=1, source_target_pairs={{0,2},{1,3},{2,0},{3,1},{4,6},{5,7},{6,4},{7,5},{8,10},{9,11},{10,... | collective-permute-start | bytes 110600 | tf_op jit(solution)/shard_map/ppermute | solution.py:522
  29.5 2.3 %collective-permute-start.6 = (bf16[16,1152]{1,0:T(8,128)(2,1)S(1)}, bf16[16,1152]{1,0:T(8,128)(2,1)S(1)}, u32[]{:S(2)}, u32[]{:S(2)}) collective-permute-start(bf16[16,1152]{1,0:T(8,128)(2,1)S(1)} %shard_map.101.rest_0_), channel_id=1, source_target_pairs={{0,3},{1,0},{2,1},{3,2},{4,7},{5,4},{6,5},{7,6},{8,11},{9,8},{10,9... | collective-permute-start | bytes 110600 | tf_op jit(solution)/shard_map/ppermute | solution.py:522
  31.9 0.7 collective-permute-done.4.rest_1_
  32.6 0.9 collective-permute-done.6.rest_3_
  33.5 6.8 %shard_map.102.after_ref.rest_0_ = bf16[16,4224]{1,0:T(8,128)(2,1)S(1)} custom-call(s32[1]{0:T(128)} %bitcast.2.me_ref, s32[8]{0:T(128)S(1)} %copy-done.6, s32[8]{0:T(128)S(1)} %copy-done.7, bf16[16,1152]{1,0:T(8,128)(2,1)S(1)} %shard_map.101.rest_0_, bf16[16,1152]{1,0:T(8,128)(2,1)S(1)} %collective-permute-done.4.rest_1_, ...), custom_call_target="tpu_custom_call" | custom-call | flops 1375731712 | bytes 5373952 | tf_op jit(solution)/shard_map/pallas_call | solution.py:347
  40.3 1.7 %collective-permute-start.7 = (bf16[16,4224]{1,0:T(8,128)(2,1)S(1)}, bf16[16,4224]{1,0:T(8,128)(2,1)S(1)}, u32[]{:S(2)}, u32[]{:S(2)}) collective-permute-start(bf16[16,4224]{1,0:T(8,128)(2,1)S(1)} %shard_map.102.after_ref.rest_0_), channel_id=1, source_target_pairs={{0,1},{1,2},{2,3},{3,0},{4,5},{5,6},{6,7},{7,4},{8,9},{9,10},{10,1... | collective-permute-start | bytes 405512 | tf_op jit(solution)/shard_map/ppermute | solution.py:522
  42.1 3.0 %collective-permute-start.8 = (bf16[16,4224]{1,0:T(8,128)(2,1)S(1)}, bf16[16,4224]{1,0:T(8,128)(2,1)S(1)}, u32[]{:S(2)}, u32[]{:S(2)}) collective-permute-start(bf16[16,4224]{1,0:T(8,128)(2,1)S(1)} %shard_map.102.after_ref.rest_0_), channel_id=1, source_target_pairs={{0,2},{1,3},{2,0},{3,1},{4,6},{5,7},{6,4},{7,5},{8,10},{9,11},{10,... | collective-permute-start | bytes 405512 | tf_op jit(solution)/shard_map/ppermute | solution.py:522
  45.1 5.9 %shard_map.103.rest_4_ = bf16[8,256,4096]{2,1,0:T(8,128)(2,1)S(1)} custom-call(bf16[1,4096,4096]{2,1,0:T(8,128)(2,1)} %w_ref.15, bf16[16,4224]{1,0:T(8,128)(2,1)S(1)} %shard_map.102.after_ref.rest_0_), custom_call_target="tpu_custom_call" | custom-call | bytes 16777216 | tf_op jit(solution)/shard_map/pallas_call | solution.py:75
  51.1 1.1 collective-permute-done.8.rest_2_
  52.1 7.0 %shard_map.104 = (bf16[8,4096]{1,0:T(8,128)(2,1)S(1)}, bf16[8,4096]{1,0:T(8,128)(2,1)S(1)}) custom-call(bf16[16,16]{1,0:T(8,128)(2,1)S(1)} %get-tuple-element.38.turn_ref.refs_4_, bf16[1,4096,4096]{2,1,0:T(8,128)(2,1)} %w_ref.15, bf16[16,4224]{1,0:T(8,128)(2,1)S(1)} %shard_map.102.after_ref.rest_0_, bf16[16,4224]{1,0:T(8,128)(2,1)S(1)} %collective-permute-done.7.rest_1_, ...), custom_call_target="tpu_custom_call" | custom-call | flops 536870912 | bytes 16777216 | tf_op jit(solution)/shard_map/pallas_call | solution.py:421
  59.3 1.6 %collective-permute-start.11 = (bf16[8,4096]{1,0:T(8,128)(2,1)S(1)}, bf16[8,4096]{1,0:T(8,128)(2,1)S(1)}, u32[]{:S(2)}, u32[]{:S(2)}) collective-permute-start(bf16[8,4096]{1,0:T(8,128)(2,1)S(1)} %get-tuple-element.26), channel_id=1, source_target_pairs={{0,8},{4,12},{8,0},{12,4},{1,9},{5,13},{9,1},{13,5},{2,10},{6,14},... | collective-permute-start | bytes 196616 | tf_op jit(solution)/shard_map/ppermute | solution.py:593
  60.9 0.3 collective-permute-start.12
  61.1 3.1 %shard_map.105.refs_7_.rest_0_ = bf16[3,256,4608]{2,1,0:T(8,128)(2,1)S(1)} custom-call(bf16[1,4096,4608]{2,1,0:T(8,128)(2,1)} %w_ref.13, bf16[8,4096]{1,0:T(8,128)(2,1)S(1)} %get-tuple-element.25.after_ref.refs_0_), custom_call_target="tpu_custom_call" | custom-call | bytes 7077888 | tf_op jit(solution)/shard_map/pallas_call | solution.py:75
  64.3 0.6 collective-permute-done.12.refs_3_
  64.9 0.2 shard_map.106
  65.2 2.2 %collective-permute-start.14 = (bf16[8,4224]{1,0:T(8,128)(2,1)S(1)}, bf16[8,4224]{1,0:T(8,128)(2,1)S(1)}, u32[]{:S(2)}, u32[]{:S(2)}) collective-permute-start(bf16[8,4224]{1,0:T(8,128)(2,1)S(1)} %get-tuple-element.28), channel_id=1, source_target_pairs={{0,24},{4,28},{8,16},{12,20},{24,0},{28,4},{16,8},{20,12},{1,25},{... | collective-permute-start | bytes 202760 | tf_op jit(solution)/shard_map/ppermute | solution.py:606
  67.4 0.5 collective-permute-start.13
  67.9 3.1 %shard_map.107.rest_1_ = bf16[3,256,4608]{2,1,0:T(8,128)(2,1)S(1)} custom-call(bf16[1,4096,4608]{2,1,0:T(8,128)(2,1)} %w_ref.13, f32[8,4096]{1,0:T(8,128)S(1)} %get-tuple-element.36.after_ref.refs_5_), custom_call_target="tpu_custom_call" | custom-call | bytes 7077888 | tf_op jit(solution)/shard_map/pallas_call | solution.py:75
  71.1 0.6 collective-permute-done.13
  71.7 8.5 %shard_map.108 = (f32[16,1280]{1,0:T(8,128)S(1)}, f32[16,1280]{1,0:T(8,128)S(1)}, f32[16,1280]{1,0:T(8,128)S(1)}, f32[16,1280]{1,0:T(8,128)S(1)}) custom-call(s32[1]{0:T(128)} %bitcast.2.me_ref, bf16[16,4224]{1,0:T(8,128)(2,1)S(1)} %pad_maximum_fusion.x_ref, bf16[16,16]{1,0:T(8,128)(2,1)S(1)} %get-tuple-element.37.aux_ref, bf16[1,4096,4608]{2,1,0:T(8,128)(2,1)} %w_ref.13, ...), custom_call_target="tpu_custom_call" | custom-call | flops 603979776 | bytes 23592960 | tf_op jit(solution)/shard_map/pallas_call | solution.py:151
  80.2 3.8 %collective-permute-start.15 = (f32[16,1280]{1,0:T(8,128)S(1)}, f32[16,1280]{1,0:T(8,128)S(1)}, u32[]{:S(2)}, u32[]{:S(2)}) collective-permute-start(f32[16,1280]{1,0:T(8,128)S(1)} %get-tuple-element.31), channel_id=1, source_target_pairs={{0,3},{1,0},{2,1},{3,2},{4,7},{5,4},{6,5},{7,6},{8,11},{9,8},{10,9... | collective-permute-start | bytes 245768 | tf_op jit(solution)/shard_map/ppermute | solution.py:514
  84.1 0.8 collective-permute-start.16
  84.9 2.0 %collective-permute-done.15.refs_1_ = f32[16,1280]{1,0:T(8,128)S(1)} collective-permute-done((f32[16,1280]{1,0:T(8,128)S(1)}, f32[16,1280]{1,0:T(8,128)S(1)}, u32[]{:S(2)}, u32[]{:S(2)}) %collective-permute-start.15) | collective-permute-done | bytes 81952 | tf_op jit(solution)/shard_map/ppermute | solution.py:514
  86.9 5.3 %collective-permute-done.16.refs_2_ = f32[16,1280]{1,0:T(8,128)S(1)} collective-permute-done((f32[16,1280]{1,0:T(8,128)S(1)}, f32[16,1280]{1,0:T(8,128)S(1)}, u32[]{:S(2)}, u32[]{:S(2)}) %collective-permute-start.16) | collective-permute-done | bytes 81952 | tf_op jit(solution)/shard_map/ppermute | solution.py:514
  92.3 1.3 %collective-permute-start.19 = (bf16[16,1152]{1,0:T(8,128)(2,1)S(1)}, bf16[16,1152]{1,0:T(8,128)(2,1)S(1)}, u32[]{:S(2)}, u32[]{:S(2)}) collective-permute-start(bf16[16,1152]{1,0:T(8,128)(2,1)S(1)} %shard_map.109.rest_0_), channel_id=1, source_target_pairs={{0,2},{1,3},{2,0},{3,1},{4,6},{5,7},{6,4},{7,5},{8,10},{9,11},{10,... | collective-permute-start | bytes 110600 | tf_op jit(solution)/shard_map/ppermute | solution.py:522
  93.6 2.5 %collective-permute-start.20 = (bf16[16,1152]{1,0:T(8,128)(2,1)S(1)}, bf16[16,1152]{1,0:T(8,128)(2,1)S(1)}, u32[]{:S(2)}, u32[]{:S(2)}) collective-permute-start(bf16[16,1152]{1,0:T(8,128)(2,1)S(1)} %shard_map.109.rest_0_), channel_id=1, source_target_pairs={{0,3},{1,0},{2,1},{3,2},{4,7},{5,4},{6,5},{7,6},{8,11},{9,8},{10,9... | collective-permute-start | bytes 110600 | tf_op jit(solution)/shard_map/ppermute | solution.py:522
  96.1 2.0 %collective-permute-done.18.rest_1_ = bf16[16,1152]{1,0:T(8,128)(2,1)S(1)} collective-permute-done((bf16[16,1152]{1,0:T(8,128)(2,1)S(1)}, bf16[16,1152]{1,0:T(8,128)(2,1)S(1)}, u32[]{:S(2)}, u32[]{:S(2)}) %collective-permute-start.18) | collective-permute-done | bytes 36896 | tf_op jit(solution)/shard_map/ppermute | solution.py:522
  98.1 0.5 collective-permute-done.20.rest_3_
  98.6 5.9 %shard_map.110.after_ref.rest_0_ = bf16[16,4224]{1,0:T(8,128)(2,1)S(1)} custom-call(s32[1]{0:T(128)} %bitcast.2.me_ref, s32[8]{0:T(128)S(1)} %copy-done.6, s32[8]{0:T(128)S(1)} %copy-done.7, bf16[16,1152]{1,0:T(8,128)(2,1)S(1)} %shard_map.109.rest_0_, bf16[16,1152]{1,0:T(8,128)(2,1)S(1)} %collective-permute-done.18.rest_1_, ...), custom_call_target="tpu_custom_call" | custom-call | flops 1375731712 | bytes 5373952 | tf_op jit(solution)/shard_map/pallas_call | solution.py:347
  104.5 2.1 %collective-permute-start.21 = (bf16[16,4224]{1,0:T(8,128)(2,1)S(1)}, bf16[16,4224]{1,0:T(8,128)(2,1)S(1)}, u32[]{:S(2)}, u32[]{:S(2)}) collective-permute-start(bf16[16,4224]{1,0:T(8,128)(2,1)S(1)} %shard_map.110.after_ref.rest_0_), channel_id=1, source_target_pairs={{0,1},{1,2},{2,3},{3,0},{4,5},{5,6},{6,7},{7,4},{8,9},{9,10},{10,1... | collective-permute-start | bytes 405512 | tf_op jit(solution)/shard_map/ppermute | solution.py:522
  106.6 1.8 %collective-permute-start.22 = (bf16[16,4224]{1,0:T(8,128)(2,1)S(1)}, bf16[16,4224]{1,0:T(8,128)(2,1)S(1)}, u32[]{:S(2)}, u32[]{:S(2)}) collective-permute-start(bf16[16,4224]{1,0:T(8,128)(2,1)S(1)} %shard_map.110.after_ref.rest_0_), channel_id=1, source_target_pairs={{0,2},{1,3},{2,0},{3,1},{4,6},{5,7},{6,4},{7,5},{8,10},{9,11},{10,... | collective-permute-start | bytes 405512 | tf_op jit(solution)/shard_map/ppermute | solution.py:522
  108.4 0.6 collective-permute-start.23
  109.0 1.6 %collective-permute-start.27 = (f32[8,4096]{1,0:T(8,128)S(1)}, f32[8,4096]{1,0:T(8,128)S(1)}, u32[]{:S(2)}, u32[]{:S(2)}) collective-permute-start(f32[8,4096]{1,0:T(8,128)S(1)} %get-tuple-element.36.after_ref.refs_5_), channel_id=1, source_target_pairs={{0,16},{16,0},{1,17},{17,1},{2,18},{18,2},{3,19},{19,3},{4,20},{20... | collective-permute-start | bytes 393224 | tf_op jit(solution)/shard_map/ppermute | solution.py:580
  110.6 5.9 %shard_map.111.rest_4_ = bf16[8,256,4096]{2,1,0:T(8,128)(2,1)S(1)} custom-call(bf16[1,4096,4096]{2,1,0:T(8,128)(2,1)} %w_ref.15, bf16[16,4224]{1,0:T(8,128)(2,1)S(1)} %shard_map.110.after_ref.rest_0_), custom_call_target="tpu_custom_call" | custom-call | bytes 16777216 | tf_op jit(solution)/shard_map/pallas_call | solution.py:75
  116.6 7.0 %shard_map.112 = (bf16[8,4096]{1,0:T(8,128)(2,1)S(1)}, bf16[8,4096]{1,0:T(8,128)(2,1)S(1)}) custom-call(bf16[16,16]{1,0:T(8,128)(2,1)S(1)} %get-tuple-element.38.turn_ref.refs_4_, bf16[1,4096,4096]{2,1,0:T(8,128)(2,1)} %w_ref.15, bf16[16,4224]{1,0:T(8,128)(2,1)S(1)} %shard_map.110.after_ref.rest_0_, bf16[16,4224]{1,0:T(8,128)(2,1)S(1)} %collective-permute-done.21.rest_1_, ...), custom_call_target="tpu_custom_call" | custom-call | flops 536870912 | bytes 16777216 | tf_op jit(solution)/shard_map/pallas_call | solution.py:421
  123.6 0.6 collective-permute-start.25
  124.3 1.6 %collective-permute-start.24 = (bf16[8,4096]{1,0:T(8,128)(2,1)S(1)}, bf16[8,4096]{1,0:T(8,128)(2,1)S(1)}, u32[]{:S(2)}, u32[]{:S(2)}) collective-permute-start(bf16[8,4096]{1,0:T(8,128)(2,1)S(1)} %get-tuple-element.34.refs_0_), channel_id=1, source_target_pairs={{0,4},{4,0},{8,12},{12,8},{1,5},{5,1},{9,13},{13,9},{2,6},{6,2},{1... | collective-permute-start | bytes 196616 | tf_op jit(solution)/shard_map/ppermute | solution.py:593
  125.9 0.8 collective-permute-done.24.refs_1_
  126.8 1.9 %collective-permute-done.25.refs_2_ = bf16[8,4096]{1,0:T(8,128)(2,1)S(1)} collective-permute-done((bf16[8,4096]{1,0:T(8,128)(2,1)S(1)}, bf16[8,4096]{1,0:T(8,128)(2,1)S(1)}, u32[]{:S(2)}, u32[]{:S(2)}) %collective-permute-start.25) | collective-permute-done | bytes 65568 | tf_op jit(solution)/shard_map/ppermute | solution.py:593
  128.7 1.2 shard_map.113
  (42 shorter events, 0.5 us)
Async XLA Ops:
  0.0 0.9 copy-start.4
  0.9 32.6 %copy-start.2 = (bf16[1,2,2,512,128]{4,3,2,1,0:T(8,128)(2,1)S(1)}, bf16[1,2,2,512,128]{4,3,2,1,0:T(8,128)(2,1)}, u32[]{:S(2)}) copy-start(bf16[1,2,2,512,128]{4,3,2,1,0:T(8,128)(2,1)} %rest_5_.3) | copy-start | bytes 1572868
  0.9 32.6 %copy-start.3 = (bf16[1,2,2,512,128]{4,3,2,1,0:T(8,128)(2,1)S(1)}, bf16[1,2,2,512,128]{4,3,2,1,0:T(8,128)(2,1)}, u32[]{:S(2)}) copy-start(bf16[1,2,2,512,128]{4,3,2,1,0:T(8,128)(2,1)} %rest_7_.3) | copy-start | bytes 1572868
  0.9 32.6 %copy-start.6 = (s32[8]{0:T(128)S(1)}, s32[8]{0:T(128)}, u32[]{:S(2)}) copy-start(s32[8]{0:T(128)} %order_ref.3) | copy-start | bytes 100
  0.9 32.6 %copy-start.7 = (s32[8]{0:T(128)S(1)}, s32[8]{0:T(128)}, u32[]{:S(2)}) copy-start(s32[8]{0:T(128)} %lengths_ref.3) | copy-start | bytes 100
  14.1 10.1 %collective-permute-start = (f32[16,1280]{1,0:T(8,128)S(1)}, f32[16,1280]{1,0:T(8,128)S(1)}, u32[]{:S(2)}, u32[]{:S(2)}) collective-permute-start(f32[16,1280]{1,0:T(8,128)S(1)} %get-tuple-element.22), channel_id=1, source_target_pairs={{0,3},{1,0},{2,1},{3,2},{4,7},{5,4},{6,5},{7,6},{8,11},{9,8},{10,9... | collective-permute-start | bytes 245768 | tf_op jit(solution)/shard_map/ppermute | solution.py:514
  19.3 7.5 %collective-permute-start.1 = (f32[16,1280]{1,0:T(8,128)S(1)}, f32[16,1280]{1,0:T(8,128)S(1)}, u32[]{:S(2)}, u32[]{:S(2)}) collective-permute-start(f32[16,1280]{1,0:T(8,128)S(1)} %get-tuple-element.23), channel_id=1, source_target_pairs={{0,2},{1,3},{2,0},{3,1},{4,6},{5,7},{6,4},{7,5},{8,10},{9,11},{10,... | collective-permute-start | bytes 245768 | tf_op jit(solution)/shard_map/ppermute | solution.py:514
  19.3 7.5 %collective-permute-start.2 = (f32[16,1280]{1,0:T(8,128)S(1)}, f32[16,1280]{1,0:T(8,128)S(1)}, u32[]{:S(2)}, u32[]{:S(2)}) collective-permute-start(f32[16,1280]{1,0:T(8,128)S(1)} %get-tuple-element.24), channel_id=1, source_target_pairs={{0,1},{1,2},{2,3},{3,0},{4,5},{5,6},{6,7},{7,4},{8,9},{9,10},{10,1... | collective-permute-start | bytes 245768 | tf_op jit(solution)/shard_map/ppermute | solution.py:514
  20.3 3.9 %collective-permute-start.3 = (bf16[1,4096]{1,0:T(2,128)(2,1)}, bf16[1,4096]{1,0:T(2,128)(2,1)S(1)}, u32[]{:S(2)}, u32[]{:S(2)}) collective-permute-start(bf16[1,4096]{1,0:T(2,128)(2,1)} %aux_ref.1), channel_id=1, source_target_pairs={{0,16},{16,0},{1,17},{17,1},{2,18},{18,2},{3,19},{19,3},{4,20},{20... | collective-permute-start | bytes 24584 | tf_op jit(solution)/shard_map/ppermute | solution.py:562
  26.9 5.8 %collective-permute-start.4 = (bf16[16,1152]{1,0:T(8,128)(2,1)S(1)}, bf16[16,1152]{1,0:T(8,128)(2,1)S(1)}, u32[]{:S(2)}, u32[]{:S(2)}) collective-permute-start(bf16[16,1152]{1,0:T(8,128)(2,1)S(1)} %shard_map.101.rest_0_), channel_id=1, source_target_pairs={{0,1},{1,2},{2,3},{3,0},{4,5},{5,6},{6,7},{7,4},{8,9},{9,10},{10,1... | collective-permute-start | bytes 110600 | tf_op jit(solution)/shard_map/ppermute | solution.py:522
  27.1 5.6 %collective-permute-start.5 = (bf16[16,1152]{1,0:T(8,128)(2,1)S(1)}, bf16[16,1152]{1,0:T(8,128)(2,1)S(1)}, u32[]{:S(2)}, u32[]{:S(2)}) collective-permute-start(bf16[16,1152]{1,0:T(8,128)(2,1)S(1)} %shard_map.101.rest_0_), channel_id=1, source_target_pairs={{0,2},{1,3},{2,0},{3,1},{4,6},{5,7},{6,4},{7,5},{8,10},{9,11},{10,... | collective-permute-start | bytes 110600 | tf_op jit(solution)/shard_map/ppermute | solution.py:522
  29.5 4.0 %collective-permute-start.6 = (bf16[16,1152]{1,0:T(8,128)(2,1)S(1)}, bf16[16,1152]{1,0:T(8,128)(2,1)S(1)}, u32[]{:S(2)}, u32[]{:S(2)}) collective-permute-start(bf16[16,1152]{1,0:T(8,128)(2,1)S(1)} %shard_map.101.rest_0_), channel_id=1, source_target_pairs={{0,3},{1,0},{2,1},{3,2},{4,7},{5,4},{6,5},{7,6},{8,11},{9,8},{10,9... | collective-permute-start | bytes 110600 | tf_op jit(solution)/shard_map/ppermute | solution.py:522
  40.3 10.8 %collective-permute-start.7 = (bf16[16,4224]{1,0:T(8,128)(2,1)S(1)}, bf16[16,4224]{1,0:T(8,128)(2,1)S(1)}, u32[]{:S(2)}, u32[]{:S(2)}) collective-permute-start(bf16[16,4224]{1,0:T(8,128)(2,1)S(1)} %shard_map.102.after_ref.rest_0_), channel_id=1, source_target_pairs={{0,1},{1,2},{2,3},{3,0},{4,5},{5,6},{6,7},{7,4},{8,9},{9,10},{10,1... | collective-permute-start | bytes 405512 | tf_op jit(solution)/shard_map/ppermute | solution.py:522
  42.1 10.1 %collective-permute-start.8 = (bf16[16,4224]{1,0:T(8,128)(2,1)S(1)}, bf16[16,4224]{1,0:T(8,128)(2,1)S(1)}, u32[]{:S(2)}, u32[]{:S(2)}) collective-permute-start(bf16[16,4224]{1,0:T(8,128)(2,1)S(1)} %shard_map.102.after_ref.rest_0_), channel_id=1, source_target_pairs={{0,2},{1,3},{2,0},{3,1},{4,6},{5,7},{6,4},{7,5},{8,10},{9,11},{10,... | collective-permute-start | bytes 405512 | tf_op jit(solution)/shard_map/ppermute | solution.py:522
  45.1 7.1 %collective-permute-start.9 = (bf16[16,4224]{1,0:T(8,128)(2,1)S(1)}, bf16[16,4224]{1,0:T(8,128)(2,1)S(1)}, u32[]{:S(2)}, u32[]{:S(2)}) collective-permute-start(bf16[16,4224]{1,0:T(8,128)(2,1)S(1)} %shard_map.102.after_ref.rest_0_), channel_id=1, source_target_pairs={{0,3},{1,0},{2,1},{3,2},{4,7},{5,4},{6,5},{7,6},{8,11},{9,8},{10,9... | collective-permute-start | bytes 405512 | tf_op jit(solution)/shard_map/ppermute | solution.py:522
  59.2 5.1 %collective-permute-start.10 = (bf16[8,4096]{1,0:T(8,128)(2,1)S(1)}, bf16[8,4096]{1,0:T(8,128)(2,1)S(1)}, u32[]{:S(2)}, u32[]{:S(2)}) collective-permute-start(bf16[8,4096]{1,0:T(8,128)(2,1)S(1)} %get-tuple-element.25.after_ref.refs_0_), channel_id=1, source_target_pairs={{0,4},{4,0},{8,12},{12,8},{1,5},{5,1},{9,13},{13,9},{2,6},{6,2},{1... | collective-permute-start | bytes 196616 | tf_op jit(solution)/shard_map/ppermute | solution.py:593
  59.3 5.7 %copy-start.5 = (bf16[2,8,4096]{2,1,0:T(8,128)(2,1)S(1)}, bf16[2,8,4096]{2,1,0:T(8,128)(2,1)}, u32[]{:S(2)}) copy-start(bf16[2,8,4096]{2,1,0:T(8,128)(2,1)} %param.10) | copy-start | bytes 393220
  59.3 5.0 %collective-permute-start.11 = (bf16[8,4096]{1,0:T(8,128)(2,1)S(1)}, bf16[8,4096]{1,0:T(8,128)(2,1)S(1)}, u32[]{:S(2)}, u32[]{:S(2)}) collective-permute-start(bf16[8,4096]{1,0:T(8,128)(2,1)S(1)} %get-tuple-element.26), channel_id=1, source_target_pairs={{0,8},{4,12},{8,0},{12,4},{1,9},{5,13},{9,1},{13,5},{2,10},{6,14},... | collective-permute-start | bytes 196616 | tf_op jit(solution)/shard_map/ppermute | solution.py:593
  60.9 4.1 %collective-permute-start.12 = (bf16[8,4096]{1,0:T(8,128)(2,1)S(1)}, bf16[8,4096]{1,0:T(8,128)(2,1)S(1)}, u32[]{:S(2)}, u32[]{:S(2)}) collective-permute-start(bf16[8,4096]{1,0:T(8,128)(2,1)S(1)} %get-tuple-element.26), channel_id=1, source_target_pairs={{0,12},{4,8},{8,4},{12,0},{1,13},{5,9},{9,5},{13,1},{2,14},{6,10},... | collective-permute-start | bytes 196616 | tf_op jit(solution)/shard_map/ppermute | solution.py:593
  65.2 5.9 %collective-permute-start.14 = (bf16[8,4224]{1,0:T(8,128)(2,1)S(1)}, bf16[8,4224]{1,0:T(8,128)(2,1)S(1)}, u32[]{:S(2)}, u32[]{:S(2)}) collective-permute-start(bf16[8,4224]{1,0:T(8,128)(2,1)S(1)} %get-tuple-element.28), channel_id=1, source_target_pairs={{0,24},{4,28},{8,16},{12,20},{24,0},{28,4},{16,8},{20,12},{1,25},{... | collective-permute-start | bytes 202760 | tf_op jit(solution)/shard_map/ppermute | solution.py:606
  67.4 4.3 %collective-permute-start.13 = (bf16[8,4224]{1,0:T(8,128)(2,1)S(1)}, bf16[8,4224]{1,0:T(8,128)(2,1)S(1)}, u32[]{:S(2)}, u32[]{:S(2)}) collective-permute-start(bf16[8,4224]{1,0:T(8,128)(2,1)S(1)} %get-tuple-element.28), channel_id=1, source_target_pairs={{0,16},{4,20},{8,24},{12,28},{16,0},{20,4},{24,8},{28,12},{1,17},{... | collective-permute-start | bytes 202760 | tf_op jit(solution)/shard_map/ppermute | solution.py:606
  71.7 26.9 %copy-start = (bf16[1,2,4096,128]{3,2,1,0:T(8,128)(2,1)S(1)}, bf16[1,2,4096,128]{3,2,1,0:T(8,128)(2,1)}, u32[]{:S(2)}) copy-start(bf16[1,2,4096,128]{3,2,1,0:T(8,128)(2,1)} %rest_4_.3) | copy-start | bytes 6291460
  71.7 26.9 %copy-start.1 = (bf16[1,2,4096,128]{3,2,1,0:T(8,128)(2,1)S(1)}, bf16[1,2,4096,128]{3,2,1,0:T(8,128)(2,1)}, u32[]{:S(2)}) copy-start(bf16[1,2,4096,128]{3,2,1,0:T(8,128)(2,1)} %rest_6_.3) | copy-start | bytes 6291460
  80.2 6.6 %collective-permute-start.15 = (f32[16,1280]{1,0:T(8,128)S(1)}, f32[16,1280]{1,0:T(8,128)S(1)}, u32[]{:S(2)}, u32[]{:S(2)}) collective-permute-start(f32[16,1280]{1,0:T(8,128)S(1)} %get-tuple-element.31), channel_id=1, source_target_pairs={{0,3},{1,0},{2,1},{3,2},{4,7},{5,4},{6,5},{7,6},{8,11},{9,8},{10,9... | collective-permute-start | bytes 245768 | tf_op jit(solution)/shard_map/ppermute | solution.py:514
  84.1 8.1 %collective-permute-start.16 = (f32[16,1280]{1,0:T(8,128)S(1)}, f32[16,1280]{1,0:T(8,128)S(1)}, u32[]{:S(2)}, u32[]{:S(2)}) collective-permute-start(f32[16,1280]{1,0:T(8,128)S(1)} %get-tuple-element.32), channel_id=1, source_target_pairs={{0,2},{1,3},{2,0},{3,1},{4,6},{5,7},{6,4},{7,5},{8,10},{9,11},{10,... | collective-permute-start | bytes 245768 | tf_op jit(solution)/shard_map/ppermute | solution.py:514
  84.9 7.3 %collective-permute-start.17 = (f32[16,1280]{1,0:T(8,128)S(1)}, f32[16,1280]{1,0:T(8,128)S(1)}, u32[]{:S(2)}, u32[]{:S(2)}) collective-permute-start(f32[16,1280]{1,0:T(8,128)S(1)} %get-tuple-element.33), channel_id=1, source_target_pairs={{0,1},{1,2},{2,3},{3,0},{4,5},{5,6},{6,7},{7,4},{8,9},{9,10},{10,1... | collective-permute-start | bytes 245768 | tf_op jit(solution)/shard_map/ppermute | solution.py:514
  92.2 5.9 %collective-permute-start.18 = (bf16[16,1152]{1,0:T(8,128)(2,1)S(1)}, bf16[16,1152]{1,0:T(8,128)(2,1)S(1)}, u32[]{:S(2)}, u32[]{:S(2)}) collective-permute-start(bf16[16,1152]{1,0:T(8,128)(2,1)S(1)} %shard_map.109.rest_0_), channel_id=1, source_target_pairs={{0,1},{1,2},{2,3},{3,0},{4,5},{5,6},{6,7},{7,4},{8,9},{9,10},{10,1... | collective-permute-start | bytes 110600 | tf_op jit(solution)/shard_map/ppermute | solution.py:522
  92.3 5.9 %collective-permute-start.19 = (bf16[16,1152]{1,0:T(8,128)(2,1)S(1)}, bf16[16,1152]{1,0:T(8,128)(2,1)S(1)}, u32[]{:S(2)}, u32[]{:S(2)}) collective-permute-start(bf16[16,1152]{1,0:T(8,128)(2,1)S(1)} %shard_map.109.rest_0_), channel_id=1, source_target_pairs={{0,2},{1,3},{2,0},{3,1},{4,6},{5,7},{6,4},{7,5},{8,10},{9,11},{10,... | collective-permute-start | bytes 110600 | tf_op jit(solution)/shard_map/ppermute | solution.py:522
  93.6 5.0 %collective-permute-start.20 = (bf16[16,1152]{1,0:T(8,128)(2,1)S(1)}, bf16[16,1152]{1,0:T(8,128)(2,1)S(1)}, u32[]{:S(2)}, u32[]{:S(2)}) collective-permute-start(bf16[16,1152]{1,0:T(8,128)(2,1)S(1)} %shard_map.109.rest_0_), channel_id=1, source_target_pairs={{0,3},{1,0},{2,1},{3,2},{4,7},{5,4},{6,5},{7,6},{8,11},{9,8},{10,9... | collective-permute-start | bytes 110600 | tf_op jit(solution)/shard_map/ppermute | solution.py:522
  104.5 12.1 %collective-permute-start.21 = (bf16[16,4224]{1,0:T(8,128)(2,1)S(1)}, bf16[16,4224]{1,0:T(8,128)(2,1)S(1)}, u32[]{:S(2)}, u32[]{:S(2)}) collective-permute-start(bf16[16,4224]{1,0:T(8,128)(2,1)S(1)} %shard_map.110.after_ref.rest_0_), channel_id=1, source_target_pairs={{0,1},{1,2},{2,3},{3,0},{4,5},{5,6},{6,7},{7,4},{8,9},{9,10},{10,1... | collective-permute-start | bytes 405512 | tf_op jit(solution)/shard_map/ppermute | solution.py:522
  106.6 10.0 %collective-permute-start.22 = (bf16[16,4224]{1,0:T(8,128)(2,1)S(1)}, bf16[16,4224]{1,0:T(8,128)(2,1)S(1)}, u32[]{:S(2)}, u32[]{:S(2)}) collective-permute-start(bf16[16,4224]{1,0:T(8,128)(2,1)S(1)} %shard_map.110.after_ref.rest_0_), channel_id=1, source_target_pairs={{0,2},{1,3},{2,0},{3,1},{4,6},{5,7},{6,4},{7,5},{8,10},{9,11},{10,... | collective-permute-start | bytes 405512 | tf_op jit(solution)/shard_map/ppermute | solution.py:522
  108.4 8.2 %collective-permute-start.23 = (bf16[16,4224]{1,0:T(8,128)(2,1)S(1)}, bf16[16,4224]{1,0:T(8,128)(2,1)S(1)}, u32[]{:S(2)}, u32[]{:S(2)}) collective-permute-start(bf16[16,4224]{1,0:T(8,128)(2,1)S(1)} %shard_map.110.after_ref.rest_0_), channel_id=1, source_target_pairs={{0,3},{1,0},{2,1},{3,2},{4,7},{5,4},{6,5},{7,6},{8,11},{9,8},{10,9... | collective-permute-start | bytes 405512 | tf_op jit(solution)/shard_map/ppermute | solution.py:522
  109.0 16.9 %collective-permute-start.27 = (f32[8,4096]{1,0:T(8,128)S(1)}, f32[8,4096]{1,0:T(8,128)S(1)}, u32[]{:S(2)}, u32[]{:S(2)}) collective-permute-start(f32[8,4096]{1,0:T(8,128)S(1)} %get-tuple-element.36.after_ref.refs_5_), channel_id=1, source_target_pairs={{0,16},{16,0},{1,17},{17,1},{2,18},{18,2},{3,19},{19,3},{4,20},{20... | collective-permute-start | bytes 393224 | tf_op jit(solution)/shard_map/ppermute | solution.py:580
  123.6 5.0 %collective-permute-start.25 = (bf16[8,4096]{1,0:T(8,128)(2,1)S(1)}, bf16[8,4096]{1,0:T(8,128)(2,1)S(1)}, u32[]{:S(2)}, u32[]{:S(2)}) collective-permute-start(bf16[8,4096]{1,0:T(8,128)(2,1)S(1)} %get-tuple-element.35), channel_id=1, source_target_pairs={{0,8},{4,12},{8,0},{12,4},{1,9},{5,13},{9,1},{13,5},{2,10},{6,14},... | collective-permute-start | bytes 196616 | tf_op jit(solution)/shard_map/ppermute | solution.py:593
  124.3 4.4 %collective-permute-start.26 = (bf16[8,4096]{1,0:T(8,128)(2,1)S(1)}, bf16[8,4096]{1,0:T(8,128)(2,1)S(1)}, u32[]{:S(2)}, u32[]{:S(2)}) collective-permute-start(bf16[8,4096]{1,0:T(8,128)(2,1)S(1)} %get-tuple-element.35), channel_id=1, source_target_pairs={{0,12},{4,8},{8,4},{12,0},{1,13},{5,9},{9,5},{13,1},{2,14},{6,10},... | collective-permute-start | bytes 196616 | tf_op jit(solution)/shard_map/ppermute | solution.py:593
  124.3 2.5 %collective-permute-start.24 = (bf16[8,4096]{1,0:T(8,128)(2,1)S(1)}, bf16[8,4096]{1,0:T(8,128)(2,1)S(1)}, u32[]{:S(2)}, u32[]{:S(2)}) collective-permute-start(bf16[8,4096]{1,0:T(8,128)(2,1)S(1)} %get-tuple-element.34.refs_0_), channel_id=1, source_target_pairs={{0,4},{4,0},{8,12},{12,8},{1,5},{5,1},{9,13},{13,9},{2,6},{6,2},{1... | collective-permute-start | bytes 196616 | tf_op jit(solution)/shard_map/ppermute | solution.py:593
